TPU v7x, 512 devices: a whole 4x8x8 slice. The times are simulated.
512 devices in a mesh: pop: 32 (over y, x_hi, core), tile: 16 (over z, x_lo).
Axes of the slice: x: 4 (x_hi: 2, x_lo: 2; x = x_hi * 2 + x_lo), y: 8, z: 8, core: 2. Of those that a mesh axis runs over, the one named last changes fastest.
Arguments:
- weights: int32 [32, 32], replicated, may hold values from -2 to 3
- terminal: float32 [32, 128, 2048], P('pop', 'tile'), may hold values from -4.5 to 4.5
- density_history: bfloat16 [32, 8, 128, 2048], P('pop', None, 'tile'), may hold values from 0.19921875 to 2
- density_init: float32 [32, 128, 2048], P('pop', 'tile'), may hold values from 0.2 to 2
Outputs:
- values: float32 [32, 8, 128, 2048], P('pop', None, 'tile')
- density_final: float32 [32, 128, 2048], P('pop', 'tile')
All inputs are finite; a program needn't handle non-finite values.
Results may differ from a plain program's by a relative error of at most 0.0003.
Values may be sent and summed in bfloat16 or wider, within the bound.
No kernel may reach another device: no remote copies, remote signals or barrier semaphores. Data moves between devices by JAX's collectives and lax.ppermute only.
A program may use at most 64 MiB of HBM per device.

v0:
```python
import jax
import jax.numpy as jnp
from jax import lax
from jax.sharding import Mesh
from jax.sharding import PartitionSpec as P

POP = ("pop_0", "pop_1", "pop_2")


time_step = 0.2
viscosity = 0.2


def laid_out(tiles, dim):
    tiles = jnp.moveaxis(tiles, 0, dim)
    lengths = tiles.shape
    return tiles.reshape(*lengths[:dim], lengths[dim] * lengths[dim + 1], *lengths[dim + 2 :])


def all_blocks(x, axes, turns):
    tiles = x
    for k in turns:
        tiles = lax.all_gather(tiles, axes[k])
    done = turns[::-1]
    back = [done.index(k) for k in range(len(axes))]
    tiles = tiles.transpose(*back, *range(len(axes), tiles.ndim))
    return tiles.reshape(-1, *x.shape)


def gather_axes(x, axes, turns, dim):
    return laid_out(all_blocks(x, axes, turns), dim)


def padded_2(x, sides, width):
    for axis, dim in sides:
        peers, length = (lax.axis_size(axis), x.shape[dim])
        up = [(i, (i + 1) % peers) for i in range(peers)]
        down = [(j, i) for i, j in up]
        last = lax.slice_in_dim(x, length - width, length, axis=dim)
        leading = lax.slice_in_dim(x, 0, width, axis=dim)
        before = lax.ppermute(last, axis, up)
        after = lax.ppermute(leading, axis, down)
        x = jnp.concatenate([before, x, after], axis=dim)
    return x


def sent_to_all(x, axis):
    peers = lax.axis_size(axis)
    return lax.all_to_all(jnp.broadcast_to(x[None], (peers, *x.shape)), axis, 0, 0, tiled=True)


def of_everyone(x, axis):
    everything = sent_to_all(x, axis)
    return jnp.sum(everything, axis=0)


def laplace_padded(padded):
    center = padded[:, 1:-1]
    return (
        padded[:, 2:]
        + padded[:, :-2]
        + jnp.roll(center, -1, 2)
        + jnp.roll(center, 1, 2)
        - 4.0 * center
    )


def hamiltonian_padded(padded):
    center = padded[:, 1:-1]
    ahead_rows = jnp.minimum(padded[:, 2:] - center, 0.0)
    behind_rows = jnp.maximum(center - padded[:, :-2], 0.0)
    ahead_cols = jnp.minimum(jnp.roll(center, -1, 2) - center, 0.0)
    behind_cols = jnp.maximum(center - jnp.roll(center, 1, 2), 0.0)
    return 0.5 * (
        behind_rows * behind_rows
        + ahead_rows * ahead_rows
        + behind_cols * behind_cols
        + ahead_cols * ahead_cols
    )


def transport_padded(padded_mass, padded_value):
    center = padded_mass[:, 1:-1]
    value_mid = padded_value[:, 1:-1]
    drift_rows = -(padded_value[:, 1:] - padded_value[:, :-1])
    flux_rows = (
        jnp.maximum(drift_rows, 0.0) * padded_mass[:, :-1]
        + jnp.minimum(drift_rows, 0.0) * padded_mass[:, 1:]
    )
    drift_cols = -(jnp.roll(value_mid, -1, 2) - value_mid)
    flux_cols = jnp.maximum(drift_cols, 0.0) * center + jnp.minimum(drift_cols, 0.0) * jnp.roll(
        center, -1, 2
    )
    div_rows = flux_rows[:, 1:] - flux_rows[:, :-1]
    div_cols = flux_cols - jnp.roll(flux_cols, 1, 2)
    return center + time_step * (viscosity * laplace_padded(padded_mass) - div_rows - div_cols)


def per_device(weights, terminal, density_history, density_init):
    populations = weights.shape[0]
    horizon = density_history.shape[1]
    own_index = lax.axis_index(POP)
    own_weights = lax.dynamic_slice_in_dim(weights, own_index, 1, 0)[0].astype(jnp.float32)
    total_cells = terminal.shape[1] * lax.axis_size("tile") * terminal.shape[2]
    coupled_all = (
        jnp.tensordot(
            own_weights,
            gather_axes(density_history, POP, (1, 0, 2), 0).astype(jnp.float32),
            axes=1,
            precision=lax.Precision.HIGHEST,
        )
        / populations
    )
    current = terminal
    kept_rims = [None] * horizon
    fields = [None] * horizon
    local_sums = [None] * horizon
    for step in reversed(range(horizon)):
        coupled = coupled_all[step][None]
        padded = padded_2(current, (("tile", 1),), 1)
        if step + 1 < horizon:
            kept_rims[step + 1] = padded
        advanced = current + time_step * (
            viscosity * laplace_padded(padded) - hamiltonian_padded(padded) + coupled
        )
        local_sums[step] = jnp.sum(advanced)
        fields[step] = advanced
        current = advanced
    grid_sums = of_everyone(jnp.stack(local_sums), "tile")
    centred = [fields[step] - grid_sums[step] / total_cells for step in range(horizon)]
    kept_rims[0] = padded_2(fields[0], (("tile", 1),), 1)
    density = density_init
    for step in range(horizon):
        padded_mass = padded_2(density, (("tile", 1),), 1)
        padded_value = kept_rims[step]
        density = transport_padded(padded_mass, padded_value)
    return (jnp.stack(centred, axis=1), density)


def solution(mesh):
    split = Mesh(
        mesh.devices.reshape(8, 2, 2, mesh.shape["tile"]), ("pop_0", "pop_1", "pop_2", "tile")
    )
    in_specs = (P(), P(POP, "tile", None), P(POP, None, "tile", None), P(POP, "tile", None))
    out_specs = (P(POP, None, "tile", None), P(POP, "tile", None))
    return jax.shard_map(
        per_device, mesh=split, in_specs=in_specs, out_specs=out_specs, check_vma=False
    )
```

profile of v0, /device:TPU:6, one launch (start us, length us, event | category | flops | bytes accessed | tf_op | source)
XLA Modules:
  0.0 323.9 jit_solution(95721856448821957)
XLA Ops:
  7.2 11.6 %all-gather = bf16[2,8,8,2048]{3,2,1,0:T(8,128)(2,1)} all-gather(bf16[1,8,8,2048]{3,2,1,0:T(8,128)(2,1)} %param.6), channel_id=2, replica_groups=mesh['pop_0'=8,'pop_1'=2,'pop_2'=2,'tile'=16] {'pop_1'}, dimensions={0}, use_global_device_ids=true | all-gather | bytes 786432 | tf_op jit(solution)/shard_map/all_gather | solution.py:23
  18.9 61.6 %all-gather.6.cloned.1.call-done = bf16[16,8,8,2048]{3,2,1,0:T(8,128)(2,1)} async-done(((bf16[2,8,8,2048]{3,2,1,0:T(8,128)(2,1)}), bf16[16,8,8,2048]{3,2,1,0:T(8,128)(2,1)}) %all-gather.6.cloned.1.call-update) | async-done | bytes 4194320 | tf_op jit(solution)/shard_map/all_gather | solution.py:23
  81.4 3.8 %collective-permute-start.1 = (f32[1,1,2048]{2,1,0:T(1,128)S(1)}, f32[1,1,2048]{2,1,0:T(1,128)S(1)}, u32[]{:S(2)}, u32[]{:S(2)}) collective-permute-start(f32[1,1,2048]{2,1,0:T(1,128)S(1)} %get-tuple-element.113), channel_id=1, source_target_pairs={{0,1},{1,2},{2,3},{3,4},{4,5},{5,6},{6,7},{7,8},{8,9},{9,10},{10,1... | collective-permute-start | bytes 24584 | tf_op jit(solution)/shard_map/ppermute | solution.py:41
  85.3 2.0 collective-permute-start
  88.2 4.7 %collective-permute-start.17 = (f32[1,1,2048]{2,1,0:T(1,128)S(1)}, f32[1,1,2048]{2,1,0:T(1,128)S(1)}, u32[]{:S(2)}, u32[]{:S(2)}) collective-permute-start(f32[1,1,2048]{2,1,0:T(1,128)S(1)} %get-tuple-element.69), channel_id=1, source_target_pairs={{0,1},{1,2},{2,3},{3,4},{4,5},{5,6},{6,7},{7,8},{8,9},{9,10},{10,1... | collective-permute-start | bytes 24584 | tf_op jit(solution)/shard_map/ppermute | solution.py:41
  93.0 2.5 collective-permute-start.16
  98.0 1.0 fusion.222
  99.0 10.6 %all-gather.8.cloned.1.call-done = bf16[16,2,1,8,8,2048]{5,4,3,2,1,0:T(8,128)(2,1)} async-done(((bf16[8,2,1,8,8,2048]{5,4,3,2,1,0:T(8,128)(2,1)}), bf16[16,2,1,8,8,2048]{5,4,3,2,1,0:T(8,128)(2,1)}) %all-gather.8.cloned.1.call-update) | async-done | bytes 8388624 | tf_op jit(solution)/shard_map/all_gather | solution.py:23
  109.6 8.3 %copy.12 = bf16[8,2,2,1,8,8,2048]{6,5,4,2,1,0,3:T(8,128)(2,1)} copy(bf16[8,2,2,1,8,8,2048]{6,5,4,1,0,2,3:T(8,128)(2,1)} %bitcast.57) | data formatting | bytes 16777216 | tf_op jit(solution)/shard_map/transpose | solution.py:26
  117.9 15.9 %fusion = f32[1,8,8,2048]{3,0,2,1:T(1,128)S(1)} fusion(bf16[32,8,8,2048]{3,2,1,0:T(8,128)(2,1)} %bitcast.56, s32[32,32]{1,0:T(8,128)} %param.4, s32[]{:T(128)S(6)} %select_n.3), kind=kOutput, calls=%fused_computation | convolution fusion | flops 50331680 | bytes 8913412 | tf_op jit(solution)/shard_map/dot_general | solution.py:106
  134.8 1.6 fusion.185
  136.5 3.8 %collective-permute-start.3 = (f32[1,1,2048]{2,1,0:T(1,128)S(1)}, f32[1,1,2048]{2,1,0:T(1,128)S(1)}, u32[]{:S(2)}, u32[]{:S(2)}) collective-permute-start(f32[1,1,2048]{2,1,0:T(1,128)S(1)} %get-tuple-element.107), channel_id=1, source_target_pairs={{0,1},{1,2},{2,3},{3,4},{4,5},{5,6},{6,7},{7,8},{8,9},{9,10},{10,1... | collective-permute-start | bytes 24584 | tf_op jit(solution)/shard_map/ppermute | solution.py:41
  140.3 2.0 collective-permute-start.2
  142.4 4.4 %collective-permute-done.2 = f32[1,1,2048]{2,1,0:T(1,128)S(1)} collective-permute-done((f32[1,1,2048]{2,1,0:T(1,128)S(1)}, f32[1,1,2048]{2,1,0:T(1,128)S(1)}, u32[]{:S(2)}, u32[]{:S(2)}) %collective-permute-start.2) | collective-permute-done | bytes 8224 | tf_op jit(solution)/shard_map/ppermute | solution.py:42
  146.8 1.5 fusion.187
  148.4 2.2 collective-permute-start.5
  150.6 3.7 %collective-permute-start.4 = (f32[1,1,2048]{2,1,0:T(1,128)S(1)}, f32[1,1,2048]{2,1,0:T(1,128)S(1)}, u32[]{:S(2)}, u32[]{:S(2)}) collective-permute-start(f32[1,1,2048]{2,1,0:T(1,128)S(1)} %get-tuple-element.100), channel_id=1, source_target_pairs={{1,0},{2,1},{3,2},{4,3},{5,4},{6,5},{7,6},{8,7},{9,8},{10,9},{11,1... | collective-permute-start | bytes 24584 | tf_op jit(solution)/shard_map/ppermute | solution.py:42
  154.4 2.7 collective-permute-done.4
  157.1 1.6 fusion.189
  158.8 3.8 %collective-permute-start.7 = (f32[1,1,2048]{2,1,0:T(1,128)S(1)}, f32[1,1,2048]{2,1,0:T(1,128)S(1)}, u32[]{:S(2)}, u32[]{:S(2)}) collective-permute-start(f32[1,1,2048]{2,1,0:T(1,128)S(1)} %get-tuple-element.95), channel_id=1, source_target_pairs={{0,1},{1,2},{2,3},{3,4},{4,5},{5,6},{6,7},{7,8},{8,9},{9,10},{10,1... | collective-permute-start | bytes 24584 | tf_op jit(solution)/shard_map/ppermute | solution.py:41
  162.7 2.0 collective-permute-start.6
  164.7 4.4 %collective-permute-done.6 = f32[1,1,2048]{2,1,0:T(1,128)S(1)} collective-permute-done((f32[1,1,2048]{2,1,0:T(1,128)S(1)}, f32[1,1,2048]{2,1,0:T(1,128)S(1)}, u32[]{:S(2)}, u32[]{:S(2)}) %collective-permute-start.6) | collective-permute-done | bytes 8224 | tf_op jit(solution)/shard_map/ppermute | solution.py:42
  169.1 1.6 fusion.191
  170.8 2.2 collective-permute-start.9
  173.0 3.7 %collective-permute-start.8 = (f32[1,1,2048]{2,1,0:T(1,128)S(1)}, f32[1,1,2048]{2,1,0:T(1,128)S(1)}, u32[]{:S(2)}, u32[]{:S(2)}) collective-permute-start(f32[1,1,2048]{2,1,0:T(1,128)S(1)} %get-tuple-element.88), channel_id=1, source_target_pairs={{1,0},{2,1},{3,2},{4,3},{5,4},{6,5},{7,6},{8,7},{9,8},{10,9},{11,1... | collective-permute-start | bytes 24584 | tf_op jit(solution)/shard_map/ppermute | solution.py:42
  176.7 3.2 collective-permute-done.8
  179.9 1.6 fusion.193
  181.6 3.9 %collective-permute-start.11 = (f32[1,1,2048]{2,1,0:T(1,128)S(1)}, f32[1,1,2048]{2,1,0:T(1,128)S(1)}, u32[]{:S(2)}, u32[]{:S(2)}) collective-permute-start(f32[1,1,2048]{2,1,0:T(1,128)S(1)} %get-tuple-element.83), channel_id=1, source_target_pairs={{0,1},{1,2},{2,3},{3,4},{4,5},{5,6},{6,7},{7,8},{8,9},{9,10},{10,1... | collective-permute-start | bytes 24584 | tf_op jit(solution)/shard_map/ppermute | solution.py:41
  185.5 1.9 collective-permute-start.10
  187.5 4.4 %collective-permute-done.10 = f32[1,1,2048]{2,1,0:T(1,128)S(1)} collective-permute-done((f32[1,1,2048]{2,1,0:T(1,128)S(1)}, f32[1,1,2048]{2,1,0:T(1,128)S(1)}, u32[]{:S(2)}, u32[]{:S(2)}) %collective-permute-start.10) | collective-permute-done | bytes 8224 | tf_op jit(solution)/shard_map/ppermute | solution.py:42
  192.0 1.6 fusion.195
  193.7 3.9 %collective-permute-start.13 = (f32[1,1,2048]{2,1,0:T(1,128)S(1)}, f32[1,1,2048]{2,1,0:T(1,128)S(1)}, u32[]{:S(2)}, u32[]{:S(2)}) collective-permute-start(f32[1,1,2048]{2,1,0:T(1,128)S(1)} %get-tuple-element.77), channel_id=1, source_target_pairs={{0,1},{1,2},{2,3},{3,4},{4,5},{5,6},{6,7},{7,8},{8,9},{9,10},{10,1... | collective-permute-start | bytes 24584 | tf_op jit(solution)/shard_map/ppermute | solution.py:41
  197.6 1.9 collective-permute-start.12
  199.6 4.4 %collective-permute-done.12 = f32[1,1,2048]{2,1,0:T(1,128)S(1)} collective-permute-done((f32[1,1,2048]{2,1,0:T(1,128)S(1)}, f32[1,1,2048]{2,1,0:T(1,128)S(1)}, u32[]{:S(2)}, u32[]{:S(2)}) %collective-permute-start.12) | collective-permute-done | bytes 8224 | tf_op jit(solution)/shard_map/ppermute | solution.py:42
  204.1 1.6 fusion.197
  205.7 3.9 %collective-permute-start.15 = (f32[1,1,2048]{2,1,0:T(1,128)S(1)}, f32[1,1,2048]{2,1,0:T(1,128)S(1)}, u32[]{:S(2)}, u32[]{:S(2)}) collective-permute-start(f32[1,1,2048]{2,1,0:T(1,128)S(1)} %get-tuple-element.71), channel_id=1, source_target_pairs={{0,1},{1,2},{2,3},{3,4},{4,5},{5,6},{6,7},{7,8},{8,9},{9,10},{10,1... | collective-permute-start | bytes 24584 | tf_op jit(solution)/shard_map/ppermute | solution.py:41
  209.7 1.9 collective-permute-start.14
  211.7 4.4 %collective-permute-done.14 = f32[1,1,2048]{2,1,0:T(1,128)S(1)} collective-permute-done((f32[1,1,2048]{2,1,0:T(1,128)S(1)}, f32[1,1,2048]{2,1,0:T(1,128)S(1)}, u32[]{:S(2)}, u32[]{:S(2)}) %collective-permute-start.14) | collective-permute-done | bytes 8224 | tf_op jit(solution)/shard_map/ppermute | solution.py:42
  216.1 1.6 fusion.199
  217.8 5.1 %stack.62 = f32[8]{0:T(128)S(1)} concatenate(f32[1]{0:T(128)} %bitcast.9, f32[1]{0:T(128)} %bitcast.10, f32[1]{0:T(128)} %bitcast.11, f32[1]{0:T(128)} %bitcast.12, f32[1]{0:T(128)} %bitcast.13, f32[1]{0:T(128)} %bitcast.14, f32[1]{0:T(128)} %bitcast.15, f32[1]{0:T(128)} %bitcast.16), dimensions={0} | concatenate | bytes 64 | tf_op jit(solution)/shard_map/stack | solution.py:129
  223.5 7.3 %all-to-all-start = ((f32[16,1,8]{2,1,0:T(1,128)}), f32[16,1,8]{2,1,0:T(1,128)S(1)}, u32[]{:S(2)}, u32[]{:S(2)}) async-start(f32[16,1,8]{2,1,0:T(1,128)} %broadcast_in_dim.2), calls=%async_computation | async-start | bytes 16384 | tf_op jit(solution)/shard_map/all_to_all | solution.py:49
  230.8 3.4 %collective-permute-start.19 = (f32[1,1,2048]{2,1,0:T(1,128)S(1)}, f32[1,1,2048]{2,1,0:T(1,128)S(1)}, u32[]{:S(2)}, u32[]{:S(2)}) collective-permute-start(f32[1,1,2048]{2,1,0:T(1,128)S(1)} %get-tuple-element.67), channel_id=1, source_target_pairs={{0,1},{1,2},{2,3},{3,4},{4,5},{5,6},{6,7},{7,8},{8,9},{9,10},{10,1... | collective-permute-start | bytes 24584 | tf_op jit(solution)/shard_map/ppermute | solution.py:41
  234.2 2.5 collective-permute-start.18
  244.2 3.6 %collective-permute-start.21 = (f32[1,1,2048]{2,1,0:T(1,128)S(1)}, f32[1,1,2048]{2,1,0:T(1,128)S(1)}, u32[]{:S(2)}, u32[]{:S(2)}) collective-permute-start(f32[1,1,2048]{2,1,0:T(1,128)S(1)} %get-tuple-element.59), channel_id=1, source_target_pairs={{0,1},{1,2},{2,3},{3,4},{4,5},{5,6},{6,7},{7,8},{8,9},{9,10},{10,1... | collective-permute-start | bytes 24584 | tf_op jit(solution)/shard_map/ppermute | solution.py:41
  247.8 2.3 collective-permute-start.20
  250.2 4.0 %collective-permute-done.20 = f32[1,1,2048]{2,1,0:T(1,128)S(1)} collective-permute-done((f32[1,1,2048]{2,1,0:T(1,128)S(1)}, f32[1,1,2048]{2,1,0:T(1,128)S(1)}, u32[]{:S(2)}, u32[]{:S(2)}) %collective-permute-start.20) | collective-permute-done | bytes 8224 | tf_op jit(solution)/shard_map/ppermute | solution.py:42
  254.6 1.9 collective-permute-start.23
  256.5 3.9 %collective-permute-start.22 = (f32[1,1,2048]{2,1,0:T(1,128)S(1)}, f32[1,1,2048]{2,1,0:T(1,128)S(1)}, u32[]{:S(2)}, u32[]{:S(2)}) collective-permute-start(f32[1,1,2048]{2,1,0:T(1,128)S(1)} %get-tuple-element.52), channel_id=1, source_target_pairs={{1,0},{2,1},{3,2},{4,3},{5,4},{6,5},{7,6},{8,7},{9,8},{10,9},{11,1... | collective-permute-start | bytes 24584 | tf_op jit(solution)/shard_map/ppermute | solution.py:42
  260.6 2.4 collective-permute-done.22
  263.3 3.9 %collective-permute-start.25 = (f32[1,1,2048]{2,1,0:T(1,128)S(1)}, f32[1,1,2048]{2,1,0:T(1,128)S(1)}, u32[]{:S(2)}, u32[]{:S(2)}) collective-permute-start(f32[1,1,2048]{2,1,0:T(1,128)S(1)} %get-tuple-element.47), channel_id=1, source_target_pairs={{0,1},{1,2},{2,3},{3,4},{4,5},{5,6},{6,7},{7,8},{8,9},{9,10},{10,1... | collective-permute-start | bytes 24584 | tf_op jit(solution)/shard_map/ppermute | solution.py:41
  267.3 1.9 collective-permute-start.24
  269.4 4.3 %collective-permute-done.24 = f32[1,1,2048]{2,1,0:T(1,128)S(1)} collective-permute-done((f32[1,1,2048]{2,1,0:T(1,128)S(1)}, f32[1,1,2048]{2,1,0:T(1,128)S(1)}, u32[]{:S(2)}, u32[]{:S(2)}) %collective-permute-start.24) | collective-permute-done | bytes 8224 | tf_op jit(solution)/shard_map/ppermute | solution.py:42
  274.1 2.3 collective-permute-start.27
  276.4 3.5 %collective-permute-start.26 = (f32[1,1,2048]{2,1,0:T(1,128)S(1)}, f32[1,1,2048]{2,1,0:T(1,128)S(1)}, u32[]{:S(2)}, u32[]{:S(2)}) collective-permute-start(f32[1,1,2048]{2,1,0:T(1,128)S(1)} %get-tuple-element.40), channel_id=1, source_target_pairs={{1,0},{2,1},{3,2},{4,3},{5,4},{6,5},{7,6},{8,7},{9,8},{10,9},{11,1... | collective-permute-start | bytes 24584 | tf_op jit(solution)/shard_map/ppermute | solution.py:42
  280.1 4.0 %collective-permute-done.26 = f32[1,1,2048]{2,1,0:T(1,128)S(1)} collective-permute-done((f32[1,1,2048]{2,1,0:T(1,128)S(1)}, f32[1,1,2048]{2,1,0:T(1,128)S(1)}, u32[]{:S(2)}, u32[]{:S(2)}) %collective-permute-start.26) | collective-permute-done | bytes 8224 | tf_op jit(solution)/shard_map/ppermute | solution.py:42
  284.4 3.9 %collective-permute-start.29 = (f32[1,1,2048]{2,1,0:T(1,128)S(1)}, f32[1,1,2048]{2,1,0:T(1,128)S(1)}, u32[]{:S(2)}, u32[]{:S(2)}) collective-permute-start(f32[1,1,2048]{2,1,0:T(1,128)S(1)} %get-tuple-element.35), channel_id=1, source_target_pairs={{0,1},{1,2},{2,3},{3,4},{4,5},{5,6},{6,7},{7,8},{8,9},{9,10},{10,1... | collective-permute-start | bytes 24584 | tf_op jit(solution)/shard_map/ppermute | solution.py:41
  288.4 1.9 collective-permute-start.28
  290.4 4.4 %collective-permute-done.28 = f32[1,1,2048]{2,1,0:T(1,128)S(1)} collective-permute-done((f32[1,1,2048]{2,1,0:T(1,128)S(1)}, f32[1,1,2048]{2,1,0:T(1,128)S(1)}, u32[]{:S(2)}, u32[]{:S(2)}) %collective-permute-start.28) | collective-permute-done | bytes 8224 | tf_op jit(solution)/shard_map/ppermute | solution.py:42
  295.2 3.9 %collective-permute-start.31 = (f32[1,1,2048]{2,1,0:T(1,128)S(1)}, f32[1,1,2048]{2,1,0:T(1,128)S(1)}, u32[]{:S(2)}, u32[]{:S(2)}) collective-permute-start(f32[1,1,2048]{2,1,0:T(1,128)S(1)} %get-tuple-element.29), channel_id=1, source_target_pairs={{0,1},{1,2},{2,3},{3,4},{4,5},{5,6},{6,7},{7,8},{8,9},{9,10},{10,1... | collective-permute-start | bytes 24584 | tf_op jit(solution)/shard_map/ppermute | solution.py:41
  299.1 1.9 collective-permute-start.30
  301.2 4.4 %collective-permute-done.30 = f32[1,1,2048]{2,1,0:T(1,128)S(1)} collective-permute-done((f32[1,1,2048]{2,1,0:T(1,128)S(1)}, f32[1,1,2048]{2,1,0:T(1,128)S(1)}, u32[]{:S(2)}, u32[]{:S(2)}) %collective-permute-start.30) | collective-permute-done | bytes 8224 | tf_op jit(solution)/shard_map/ppermute | solution.py:42
  305.9 3.9 %collective-permute-start.33 = (f32[1,1,2048]{2,1,0:T(1,128)S(1)}, f32[1,1,2048]{2,1,0:T(1,128)S(1)}, u32[]{:S(2)}, u32[]{:S(2)}) collective-permute-start(f32[1,1,2048]{2,1,0:T(1,128)S(1)} %get-tuple-element.23), channel_id=1, source_target_pairs={{0,1},{1,2},{2,3},{3,4},{4,5},{5,6},{6,7},{7,8},{8,9},{9,10},{10,1... | collective-permute-start | bytes 24584 | tf_op jit(solution)/shard_map/ppermute | solution.py:41
  309.8 1.9 collective-permute-start.32
  311.9 4.4 %collective-permute-done.32 = f32[1,1,2048]{2,1,0:T(1,128)S(1)} collective-permute-done((f32[1,1,2048]{2,1,0:T(1,128)S(1)}, f32[1,1,2048]{2,1,0:T(1,128)S(1)}, u32[]{:S(2)}, u32[]{:S(2)}) %collective-permute-start.32) | collective-permute-done | bytes 8224 | tf_op jit(solution)/shard_map/ppermute | solution.py:42
  (126 shorter events, 13.8 us)
Async XLA Ops:
  7.2 73.3 %all-gather.6.cloned.1.call-start = ((), (), s32[]{:S(2)}) async-start(), calls=%async_computation.1 | async-start | bytes 4718592 | tf_op jit(solution)/shard_map/all_gather | solution.py:23
  18.8 90.8 %all-gather.8.cloned.1.call-start = ((), (), s32[]{:S(2)}) async-start(), calls=%async_computation.2 | async-start | bytes 12582912 | tf_op jit(solution)/shard_map/all_gather | solution.py:23
  81.4 53.4 %collective-permute-start.1 = (f32[1,1,2048]{2,1,0:T(1,128)S(1)}, f32[1,1,2048]{2,1,0:T(1,128)S(1)}, u32[]{:S(2)}, u32[]{:S(2)}) collective-permute-start(f32[1,1,2048]{2,1,0:T(1,128)S(1)} %get-tuple-element.113), channel_id=1, source_target_pairs={{0,1},{1,2},{2,3},{3,4},{4,5},{5,6},{6,7},{7,8},{8,9},{9,10},{10,1... | collective-permute-start | bytes 24584 | tf_op jit(solution)/shard_map/ppermute | solution.py:41
  85.3 49.6 %collective-permute-start = (f32[1,1,2048]{2,1,0:T(1,128)S(1)}, f32[1,1,2048]{2,1,0:T(1,128)S(1)}, u32[]{:S(2)}, u32[]{:S(2)}) collective-permute-start(f32[1,1,2048]{2,1,0:T(1,128)S(1)} %get-tuple-element.112), channel_id=1, source_target_pairs={{1,0},{2,1},{3,2},{4,3},{5,4},{6,5},{7,6},{8,7},{9,8},{10,9},{11,1... | collective-permute-start | bytes 24584 | tf_op jit(solution)/shard_map/ppermute | solution.py:42
  88.2 155.6 %collective-permute-start.17 = (f32[1,1,2048]{2,1,0:T(1,128)S(1)}, f32[1,1,2048]{2,1,0:T(1,128)S(1)}, u32[]{:S(2)}, u32[]{:S(2)}) collective-permute-start(f32[1,1,2048]{2,1,0:T(1,128)S(1)} %get-tuple-element.69), channel_id=1, source_target_pairs={{0,1},{1,2},{2,3},{3,4},{4,5},{5,6},{6,7},{7,8},{8,9},{9,10},{10,1... | collective-permute-start | bytes 24584 | tf_op jit(solution)/shard_map/ppermute | solution.py:41
  93.0 143.9 %collective-permute-start.16 = (f32[1,1,2048]{2,1,0:T(1,128)S(1)}, f32[1,1,2048]{2,1,0:T(1,128)S(1)}, u32[]{:S(2)}, u32[]{:S(2)}) collective-permute-start(f32[1,1,2048]{2,1,0:T(1,128)S(1)} %get-tuple-element.68), channel_id=1, source_target_pairs={{1,0},{2,1},{3,2},{4,3},{5,4},{6,5},{7,6},{8,7},{9,8},{10,9},{11,1... | collective-permute-start | bytes 24584 | tf_op jit(solution)/shard_map/ppermute | solution.py:42
  117.9 16.9 %copy-start.1 = (f32[1,8,2048]{2,1,0:T(8,128)S(1)}, f32[1,8,2048]{2,1,0:T(8,128)}, u32[]{:S(2)}) copy-start(f32[1,8,2048]{2,1,0:T(8,128)} %param.5) | copy-start | bytes 196612
  117.9 118.7 %copy-start = (f32[1,8,2048]{2,1,0:T(8,128)S(1)}, f32[1,8,2048]{2,1,0:T(8,128)}, u32[]{:S(2)}) copy-start(f32[1,8,2048]{2,1,0:T(8,128)} %param.7) | copy-start | bytes 196612
  136.5 5.9 %collective-permute-start.3 = (f32[1,1,2048]{2,1,0:T(1,128)S(1)}, f32[1,1,2048]{2,1,0:T(1,128)S(1)}, u32[]{:S(2)}, u32[]{:S(2)}) collective-permute-start(f32[1,1,2048]{2,1,0:T(1,128)S(1)} %get-tuple-element.107), channel_id=1, source_target_pairs={{0,1},{1,2},{2,3},{3,4},{4,5},{5,6},{6,7},{7,8},{8,9},{9,10},{10,1... | collective-permute-start | bytes 24584 | tf_op jit(solution)/shard_map/ppermute | solution.py:41
  140.3 6.4 %collective-permute-start.2 = (f32[1,1,2048]{2,1,0:T(1,128)S(1)}, f32[1,1,2048]{2,1,0:T(1,128)S(1)}, u32[]{:S(2)}, u32[]{:S(2)}) collective-permute-start(f32[1,1,2048]{2,1,0:T(1,128)S(1)} %get-tuple-element.106), channel_id=1, source_target_pairs={{1,0},{2,1},{3,2},{4,3},{5,4},{6,5},{7,6},{8,7},{9,8},{10,9},{11,1... | collective-permute-start | bytes 24584 | tf_op jit(solution)/shard_map/ppermute | solution.py:42
  148.4 5.9 %collective-permute-start.5 = (f32[1,1,2048]{2,1,0:T(1,128)S(1)}, f32[1,1,2048]{2,1,0:T(1,128)S(1)}, u32[]{:S(2)}, u32[]{:S(2)}) collective-permute-start(f32[1,1,2048]{2,1,0:T(1,128)S(1)} %get-tuple-element.101), channel_id=1, source_target_pairs={{0,1},{1,2},{2,3},{3,4},{4,5},{5,6},{6,7},{7,8},{8,9},{9,10},{10,1... | collective-permute-start | bytes 24584 | tf_op jit(solution)/shard_map/ppermute | solution.py:41
  150.6 6.4 %collective-permute-start.4 = (f32[1,1,2048]{2,1,0:T(1,128)S(1)}, f32[1,1,2048]{2,1,0:T(1,128)S(1)}, u32[]{:S(2)}, u32[]{:S(2)}) collective-permute-start(f32[1,1,2048]{2,1,0:T(1,128)S(1)} %get-tuple-element.100), channel_id=1, source_target_pairs={{1,0},{2,1},{3,2},{4,3},{5,4},{6,5},{7,6},{8,7},{9,8},{10,9},{11,1... | collective-permute-start | bytes 24584 | tf_op jit(solution)/shard_map/ppermute | solution.py:42
  158.8 5.9 %collective-permute-start.7 = (f32[1,1,2048]{2,1,0:T(1,128)S(1)}, f32[1,1,2048]{2,1,0:T(1,128)S(1)}, u32[]{:S(2)}, u32[]{:S(2)}) collective-permute-start(f32[1,1,2048]{2,1,0:T(1,128)S(1)} %get-tuple-element.95), channel_id=1, source_target_pairs={{0,1},{1,2},{2,3},{3,4},{4,5},{5,6},{6,7},{7,8},{8,9},{9,10},{10,1... | collective-permute-start | bytes 24584 | tf_op jit(solution)/shard_map/ppermute | solution.py:41
  162.7 6.4 %collective-permute-start.6 = (f32[1,1,2048]{2,1,0:T(1,128)S(1)}, f32[1,1,2048]{2,1,0:T(1,128)S(1)}, u32[]{:S(2)}, u32[]{:S(2)}) collective-permute-start(f32[1,1,2048]{2,1,0:T(1,128)S(1)} %get-tuple-element.94), channel_id=1, source_target_pairs={{1,0},{2,1},{3,2},{4,3},{5,4},{6,5},{7,6},{8,7},{9,8},{10,9},{11,1... | collective-permute-start | bytes 24584 | tf_op jit(solution)/shard_map/ppermute | solution.py:42
  170.8 5.9 %collective-permute-start.9 = (f32[1,1,2048]{2,1,0:T(1,128)S(1)}, f32[1,1,2048]{2,1,0:T(1,128)S(1)}, u32[]{:S(2)}, u32[]{:S(2)}) collective-permute-start(f32[1,1,2048]{2,1,0:T(1,128)S(1)} %get-tuple-element.89), channel_id=1, source_target_pairs={{0,1},{1,2},{2,3},{3,4},{4,5},{5,6},{6,7},{7,8},{8,9},{9,10},{10,1... | collective-permute-start | bytes 24584 | tf_op jit(solution)/shard_map/ppermute | solution.py:41
  173.0 7.0 %collective-permute-start.8 = (f32[1,1,2048]{2,1,0:T(1,128)S(1)}, f32[1,1,2048]{2,1,0:T(1,128)S(1)}, u32[]{:S(2)}, u32[]{:S(2)}) collective-permute-start(f32[1,1,2048]{2,1,0:T(1,128)S(1)} %get-tuple-element.88), channel_id=1, source_target_pairs={{1,0},{2,1},{3,2},{4,3},{5,4},{6,5},{7,6},{8,7},{9,8},{10,9},{11,1... | collective-permute-start | bytes 24584 | tf_op jit(solution)/shard_map/ppermute | solution.py:42
  181.6 5.9 %collective-permute-start.11 = (f32[1,1,2048]{2,1,0:T(1,128)S(1)}, f32[1,1,2048]{2,1,0:T(1,128)S(1)}, u32[]{:S(2)}, u32[]{:S(2)}) collective-permute-start(f32[1,1,2048]{2,1,0:T(1,128)S(1)} %get-tuple-element.83), channel_id=1, source_target_pairs={{0,1},{1,2},{2,3},{3,4},{4,5},{5,6},{6,7},{7,8},{8,9},{9,10},{10,1... | collective-permute-start | bytes 24584 | tf_op jit(solution)/shard_map/ppermute | solution.py:41
  185.5 6.4 %collective-permute-start.10 = (f32[1,1,2048]{2,1,0:T(1,128)S(1)}, f32[1,1,2048]{2,1,0:T(1,128)S(1)}, u32[]{:S(2)}, u32[]{:S(2)}) collective-permute-start(f32[1,1,2048]{2,1,0:T(1,128)S(1)} %get-tuple-element.82), channel_id=1, source_target_pairs={{1,0},{2,1},{3,2},{4,3},{5,4},{6,5},{7,6},{8,7},{9,8},{10,9},{11,1... | collective-permute-start | bytes 24584 | tf_op jit(solution)/shard_map/ppermute | solution.py:42
  193.7 5.9 %collective-permute-start.13 = (f32[1,1,2048]{2,1,0:T(1,128)S(1)}, f32[1,1,2048]{2,1,0:T(1,128)S(1)}, u32[]{:S(2)}, u32[]{:S(2)}) collective-permute-start(f32[1,1,2048]{2,1,0:T(1,128)S(1)} %get-tuple-element.77), channel_id=1, source_target_pairs={{0,1},{1,2},{2,3},{3,4},{4,5},{5,6},{6,7},{7,8},{8,9},{9,10},{10,1... | collective-permute-start | bytes 24584 | tf_op jit(solution)/shard_map/ppermute | solution.py:41
  197.6 6.4 %collective-permute-start.12 = (f32[1,1,2048]{2,1,0:T(1,128)S(1)}, f32[1,1,2048]{2,1,0:T(1,128)S(1)}, u32[]{:S(2)}, u32[]{:S(2)}) collective-permute-start(f32[1,1,2048]{2,1,0:T(1,128)S(1)} %get-tuple-element.76), channel_id=1, source_target_pairs={{1,0},{2,1},{3,2},{4,3},{5,4},{6,5},{7,6},{8,7},{9,8},{10,9},{11,1... | collective-permute-start | bytes 24584 | tf_op jit(solution)/shard_map/ppermute | solution.py:42
  205.7 5.9 %collective-permute-start.15 = (f32[1,1,2048]{2,1,0:T(1,128)S(1)}, f32[1,1,2048]{2,1,0:T(1,128)S(1)}, u32[]{:S(2)}, u32[]{:S(2)}) collective-permute-start(f32[1,1,2048]{2,1,0:T(1,128)S(1)} %get-tuple-element.71), channel_id=1, source_target_pairs={{0,1},{1,2},{2,3},{3,4},{4,5},{5,6},{6,7},{7,8},{8,9},{9,10},{10,1... | collective-permute-start | bytes 24584 | tf_op jit(solution)/shard_map/ppermute | solution.py:41
  209.7 6.4 %collective-permute-start.14 = (f32[1,1,2048]{2,1,0:T(1,128)S(1)}, f32[1,1,2048]{2,1,0:T(1,128)S(1)}, u32[]{:S(2)}, u32[]{:S(2)}) collective-permute-start(f32[1,1,2048]{2,1,0:T(1,128)S(1)} %get-tuple-element.70), channel_id=1, source_target_pairs={{1,0},{2,1},{3,2},{4,3},{5,4},{6,5},{7,6},{8,7},{9,8},{10,9},{11,1... | collective-permute-start | bytes 24584 | tf_op jit(solution)/shard_map/ppermute | solution.py:42
  223.5 14.3 %all-to-all-start = ((f32[16,1,8]{2,1,0:T(1,128)}), f32[16,1,8]{2,1,0:T(1,128)S(1)}, u32[]{:S(2)}, u32[]{:S(2)}) async-start(f32[16,1,8]{2,1,0:T(1,128)} %broadcast_in_dim.2), calls=%async_computation | async-start | bytes 16384 | tf_op jit(solution)/shard_map/all_to_all | solution.py:49
  230.8 13.0 %collective-permute-start.19 = (f32[1,1,2048]{2,1,0:T(1,128)S(1)}, f32[1,1,2048]{2,1,0:T(1,128)S(1)}, u32[]{:S(2)}, u32[]{:S(2)}) collective-permute-start(f32[1,1,2048]{2,1,0:T(1,128)S(1)} %get-tuple-element.67), channel_id=1, source_target_pairs={{0,1},{1,2},{2,3},{3,4},{4,5},{5,6},{6,7},{7,8},{8,9},{9,10},{10,1... | collective-permute-start | bytes 24584 | tf_op jit(solution)/shard_map/ppermute | solution.py:41
  234.2 9.7 %collective-permute-start.18 = (f32[1,1,2048]{2,1,0:T(1,128)S(1)}, f32[1,1,2048]{2,1,0:T(1,128)S(1)}, u32[]{:S(2)}, u32[]{:S(2)}) collective-permute-start(f32[1,1,2048]{2,1,0:T(1,128)S(1)} %get-tuple-element.66), channel_id=1, source_target_pairs={{1,0},{2,1},{3,2},{4,3},{5,4},{6,5},{7,6},{8,7},{9,8},{10,9},{11,1... | collective-permute-start | bytes 24584 | tf_op jit(solution)/shard_map/ppermute | solution.py:42
  243.8 73.3 %copy-start.2 = (f32[1,8,8,2048]{3,2,1,0:T(8,128)}, f32[1,8,8,2048]{3,2,1,0:T(8,128)S(1)}, u32[]{:S(2)}) copy-start(f32[1,8,8,2048]{3,2,1,0:T(8,128)S(1)} %bitcast_dynamic-update-slice_fusion) | copy-start | bytes 1572868
  244.2 6.0 %collective-permute-start.21 = (f32[1,1,2048]{2,1,0:T(1,128)S(1)}, f32[1,1,2048]{2,1,0:T(1,128)S(1)}, u32[]{:S(2)}, u32[]{:S(2)}) collective-permute-start(f32[1,1,2048]{2,1,0:T(1,128)S(1)} %get-tuple-element.59), channel_id=1, source_target_pairs={{0,1},{1,2},{2,3},{3,4},{4,5},{5,6},{6,7},{7,8},{8,9},{9,10},{10,1... | collective-permute-start | bytes 24584 | tf_op jit(solution)/shard_map/ppermute | solution.py:41
  247.8 6.4 %collective-permute-start.20 = (f32[1,1,2048]{2,1,0:T(1,128)S(1)}, f32[1,1,2048]{2,1,0:T(1,128)S(1)}, u32[]{:S(2)}, u32[]{:S(2)}) collective-permute-start(f32[1,1,2048]{2,1,0:T(1,128)S(1)} %get-tuple-element.58), channel_id=1, source_target_pairs={{1,0},{2,1},{3,2},{4,3},{5,4},{6,5},{7,6},{8,7},{9,8},{10,9},{11,1... | collective-permute-start | bytes 24584 | tf_op jit(solution)/shard_map/ppermute | solution.py:42
  254.6 6.0 %collective-permute-start.23 = (f32[1,1,2048]{2,1,0:T(1,128)S(1)}, f32[1,1,2048]{2,1,0:T(1,128)S(1)}, u32[]{:S(2)}, u32[]{:S(2)}) collective-permute-start(f32[1,1,2048]{2,1,0:T(1,128)S(1)} %get-tuple-element.53), channel_id=1, source_target_pairs={{0,1},{1,2},{2,3},{3,4},{4,5},{5,6},{6,7},{7,8},{8,9},{9,10},{10,1... | collective-permute-start | bytes 24584 | tf_op jit(solution)/shard_map/ppermute | solution.py:41
  256.5 6.4 %collective-permute-start.22 = (f32[1,1,2048]{2,1,0:T(1,128)S(1)}, f32[1,1,2048]{2,1,0:T(1,128)S(1)}, u32[]{:S(2)}, u32[]{:S(2)}) collective-permute-start(f32[1,1,2048]{2,1,0:T(1,128)S(1)} %get-tuple-element.52), channel_id=1, source_target_pairs={{1,0},{2,1},{3,2},{4,3},{5,4},{6,5},{7,6},{8,7},{9,8},{10,9},{11,1... | collective-permute-start | bytes 24584 | tf_op jit(solution)/shard_map/ppermute | solution.py:42
  263.3 6.0 %collective-permute-start.25 = (f32[1,1,2048]{2,1,0:T(1,128)S(1)}, f32[1,1,2048]{2,1,0:T(1,128)S(1)}, u32[]{:S(2)}, u32[]{:S(2)}) collective-permute-start(f32[1,1,2048]{2,1,0:T(1,128)S(1)} %get-tuple-element.47), channel_id=1, source_target_pairs={{0,1},{1,2},{2,3},{3,4},{4,5},{5,6},{6,7},{7,8},{8,9},{9,10},{10,1... | collective-permute-start | bytes 24584 | tf_op jit(solution)/shard_map/ppermute | solution.py:41
  267.3 6.4 %collective-permute-start.24 = (f32[1,1,2048]{2,1,0:T(1,128)S(1)}, f32[1,1,2048]{2,1,0:T(1,128)S(1)}, u32[]{:S(2)}, u32[]{:S(2)}) collective-permute-start(f32[1,1,2048]{2,1,0:T(1,128)S(1)} %get-tuple-element.46), channel_id=1, source_target_pairs={{1,0},{2,1},{3,2},{4,3},{5,4},{6,5},{7,6},{8,7},{9,8},{10,9},{11,1... | collective-permute-start | bytes 24584 | tf_op jit(solution)/shard_map/ppermute | solution.py:42
  274.1 6.0 %collective-permute-start.27 = (f32[1,1,2048]{2,1,0:T(1,128)S(1)}, f32[1,1,2048]{2,1,0:T(1,128)S(1)}, u32[]{:S(2)}, u32[]{:S(2)}) collective-permute-start(f32[1,1,2048]{2,1,0:T(1,128)S(1)} %get-tuple-element.41), channel_id=1, source_target_pairs={{0,1},{1,2},{2,3},{3,4},{4,5},{5,6},{6,7},{7,8},{8,9},{9,10},{10,1... | collective-permute-start | bytes 24584 | tf_op jit(solution)/shard_map/ppermute | solution.py:41
  276.4 7.7 %collective-permute-start.26 = (f32[1,1,2048]{2,1,0:T(1,128)S(1)}, f32[1,1,2048]{2,1,0:T(1,128)S(1)}, u32[]{:S(2)}, u32[]{:S(2)}) collective-permute-start(f32[1,1,2048]{2,1,0:T(1,128)S(1)} %get-tuple-element.40), channel_id=1, source_target_pairs={{1,0},{2,1},{3,2},{4,3},{5,4},{6,5},{7,6},{8,7},{9,8},{10,9},{11,1... | collective-permute-start | bytes 24584 | tf_op jit(solution)/shard_map/ppermute | solution.py:42
  284.4 6.0 %collective-permute-start.29 = (f32[1,1,2048]{2,1,0:T(1,128)S(1)}, f32[1,1,2048]{2,1,0:T(1,128)S(1)}, u32[]{:S(2)}, u32[]{:S(2)}) collective-permute-start(f32[1,1,2048]{2,1,0:T(1,128)S(1)} %get-tuple-element.35), channel_id=1, source_target_pairs={{0,1},{1,2},{2,3},{3,4},{4,5},{5,6},{6,7},{7,8},{8,9},{9,10},{10,1... | collective-permute-start | bytes 24584 | tf_op jit(solution)/shard_map/ppermute | solution.py:41
  288.4 6.4 %collective-permute-start.28 = (f32[1,1,2048]{2,1,0:T(1,128)S(1)}, f32[1,1,2048]{2,1,0:T(1,128)S(1)}, u32[]{:S(2)}, u32[]{:S(2)}) collective-permute-start(f32[1,1,2048]{2,1,0:T(1,128)S(1)} %get-tuple-element.34), channel_id=1, source_target_pairs={{1,0},{2,1},{3,2},{4,3},{5,4},{6,5},{7,6},{8,7},{9,8},{10,9},{11,1... | collective-permute-start | bytes 24584 | tf_op jit(solution)/shard_map/ppermute | solution.py:42
  295.2 6.0 %collective-permute-start.31 = (f32[1,1,2048]{2,1,0:T(1,128)S(1)}, f32[1,1,2048]{2,1,0:T(1,128)S(1)}, u32[]{:S(2)}, u32[]{:S(2)}) collective-permute-start(f32[1,1,2048]{2,1,0:T(1,128)S(1)} %get-tuple-element.29), channel_id=1, source_target_pairs={{0,1},{1,2},{2,3},{3,4},{4,5},{5,6},{6,7},{7,8},{8,9},{9,10},{10,1... | collective-permute-start | bytes 24584 | tf_op jit(solution)/shard_map/ppermute | solution.py:41
  299.1 6.4 %collective-permute-start.30 = (f32[1,1,2048]{2,1,0:T(1,128)S(1)}, f32[1,1,2048]{2,1,0:T(1,128)S(1)}, u32[]{:S(2)}, u32[]{:S(2)}) collective-permute-start(f32[1,1,2048]{2,1,0:T(1,128)S(1)} %get-tuple-element.28), channel_id=1, source_target_pairs={{1,0},{2,1},{3,2},{4,3},{5,4},{6,5},{7,6},{8,7},{9,8},{10,9},{11,1... | collective-permute-start | bytes 24584 | tf_op jit(solution)/shard_map/ppermute | solution.py:42
  305.9 6.0 %collective-permute-start.33 = (f32[1,1,2048]{2,1,0:T(1,128)S(1)}, f32[1,1,2048]{2,1,0:T(1,128)S(1)}, u32[]{:S(2)}, u32[]{:S(2)}) collective-permute-start(f32[1,1,2048]{2,1,0:T(1,128)S(1)} %get-tuple-element.23), channel_id=1, source_target_pairs={{0,1},{1,2},{2,3},{3,4},{4,5},{5,6},{6,7},{7,8},{8,9},{9,10},{10,1... | collective-permute-start | bytes 24584 | tf_op jit(solution)/shard_map/ppermute | solution.py:41
  309.8 6.4 %collective-permute-start.32 = (f32[1,1,2048]{2,1,0:T(1,128)S(1)}, f32[1,1,2048]{2,1,0:T(1,128)S(1)}, u32[]{:S(2)}, u32[]{:S(2)}) collective-permute-start(f32[1,1,2048]{2,1,0:T(1,128)S(1)} %get-tuple-element.22), channel_id=1, source_target_pairs={{1,0},{2,1},{3,2},{4,3},{5,4},{6,5},{7,6},{8,7},{9,8},{10,9},{11,1... | collective-permute-start | bytes 24584 | tf_op jit(solution)/shard_map/ppermute | solution.py:42
Sparse Core Ops, SparseCore 0:
  19.0 61.4 all-gather.5
  82.5 27.0 all-gather.7
where the time goes:
time: 326 us; the launch traced here: 324 us
  waiting for transfers between devices  129 us (40%)
  starting transfers between devices  108 us (33%)
  local copies, waits for them, and re-layouts  23.5 us (7%)
  between operations  19.7 us (6%)
  other arithmetic  16.5 us (5%)
  matrix products  15.9 us (5%)
  blocking collectives  11.6 us (4%)
    all_gather x2, waiting for transfers between devices, all_blocks(): tiles = lax.all_gather(tiles, axes[k])  72.1 us
    ppermute x17, starting transfers between devices, padded_2(): before = lax.ppermute(last, axis, up)  59.3 us
    ppermute x17, waiting for transfers between devices, padded_2(): after = lax.ppermute(leading, axis, down)  55.7 us
    ppermute x17, starting transfers between devices, padded_2(): after = lax.ppermute(leading, axis, down)  41.4 us
    dot_general x1, matrix products, per_device(): jnp.tensordot(own_weights, gather_axes(density_history, POP, (1, 0, 2), 0...  15.9 us
    reduce_sum x8, other arithmetic, per_device(): local_sums[step] = jnp.sum(advanced)  12.7 us
    all_gather x1, blocking collectives, all_blocks(): tiles = lax.all_gather(tiles, axes[k])  11.6 us
    transpose x1, local copies, waits for them, and re-layouts, all_blocks(): tiles = tiles.transpose(*back, *range(len(axes), tiles.ndim))  8.34 us
  transfers between devices with their start and end apart: 37, of which 17 were waited for; matrix products, arithmetic and copies ran while one was open for 16% of the time, Pallas kernels for 0%

commit v1 on v0

v1 whole, which is shorter than its diff:
```python
import functools

import jax
import jax.numpy as jnp
from jax import lax
from jax.experimental import pallas as pl
from jax.experimental.pallas import tpu as pltpu
from jax.sharding import Mesh
from jax.sharding import PartitionSpec as P

POP = ("pop_0", "pop_1", "pop_2")

time_step = 0.2
viscosity = 0.2

DENSITY_MID = (0.19921875 + 2.0) / 2
DENSITY_HALF = (2.0 - 0.19921875) / 2
LEVELS = 32000.0
TERMINAL_SCALE = 32000.0 / 4.5

HALO = 8
F32 = jnp.float32
I16 = jnp.int16


def to_i16(x):
    return jnp.round(x).astype(jnp.int32).astype(I16)


def coupling_kernel(w_ref, x_ref, out_ref):
    pops = w_ref.shape[0]
    rows = x_ref.shape[0]
    per = rows // pops
    shift = per.bit_length() - 1
    weights = w_ref[...].astype(F32).astype(jnp.bfloat16)
    i = lax.broadcasted_iota(jnp.int32, (rows, pops), 0)
    q = lax.broadcasted_iota(jnp.int32, (rows, pops), 1)
    spread = jnp.where((i >> shift) == q, 1.0, 0.0).astype(jnp.bfloat16)
    tall = jnp.dot(spread, weights, preferred_element_type=F32)
    total = jnp.sum(tall, axis=1, keepdims=True)
    size = jnp.maximum(jnp.sum(jnp.abs(tall), axis=1, keepdims=True), 1.0)
    wide = lax.dot_general(
        tall.astype(jnp.bfloat16), spread, (((1,), (1,)), ((), ())), preferred_element_type=F32
    )
    a = lax.broadcasted_iota(jnp.int32, (rows, rows), 0)
    b = lax.broadcasted_iota(jnp.int32, (rows, rows), 1)
    kron = jnp.where((a & (per - 1)) == (b & (per - 1)), wide, 0.0).astype(jnp.bfloat16)
    product = jnp.dot(kron, x_ref[...], preferred_element_type=F32)
    level = (product - DENSITY_MID * total) * (LEVELS / (DENSITY_HALF * size))
    out_ref[...] = to_i16(level)


def rows_of_step(wide, step, blocks):
    first = step * blocks * HALO
    return jnp.concatenate(
        [wide[first + k * HALO : first + (k + 1) * HALO] for k in range(blocks)], axis=1
    )


def pack_kernel(blocks, steps, c_ref, terminal_ref, down_ref, up_ref):
    wide = c_ref[...].astype(F32)
    c = [rows_of_step(wide, t, blocks) for t in range(steps)]
    row = lax.broadcasted_iota(jnp.int32, c[0].shape, 0)
    down = []
    up = []
    for t in range(1, HALO // 2):
        down.append(jnp.where(row >= t, c[HALO - t], pltpu.roll(c[t], t, 0)))
        up.append(jnp.where(row < HALO - t, c[HALO - t], pltpu.roll(c[t], HALO - t, 0)))
    down.append(c[HALO // 2])
    up.append(c[HALO // 2])
    edge = terminal_ref[...] * TERMINAL_SCALE
    down_ref[...] = to_i16(jnp.concatenate(down + [edge], axis=0))
    up_ref[...] = to_i16(jnp.concatenate(up + [edge], axis=0))


def backward_kernel(
    blocks, steps, w_ref, c_ref, terminal_ref, init_ref, above_ref, below_ref, u_ref, edge_ref, sums_ref
):
    pops = w_ref.shape[0]
    cols = terminal_ref.shape[1]
    own = lax.axis_index(POP)
    own_weights = w_ref[pl.ds(own, 1), :].astype(F32)
    total = jnp.sum(own_weights, axis=1, keepdims=True)
    size = jnp.maximum(jnp.sum(jnp.abs(own_weights), axis=1, keepdims=True), 1.0)
    slope = size * (DENSITY_HALF / (LEVELS * pops))
    offset = total * (DENSITY_MID / pops)
    wide = c_ref[...].astype(F32)
    above = above_ref[...].astype(F32)
    below = below_ref[...].astype(F32)

    def tile(x, k):
        return x[k * HALO : (k + 1) * HALO]

    def levels(t):
        if t == 0:
            top = bottom = jnp.zeros((HALO, cols), F32)
        elif t <= HALO // 2:
            top = tile(above, t - 1)
            bottom = tile(below, t - 1)
            if t < HALO // 2:
                top = pltpu.roll(top, HALO - t, 0)
                bottom = pltpu.roll(bottom, t, 0)
        else:
            top = tile(above, HALO - t - 1)
            bottom = tile(below, HALO - t - 1)
        return jnp.concatenate([top, rows_of_step(wide, t, blocks), bottom], axis=0)

    last = HALO // 2
    u = jnp.concatenate(
        [
            tile(above, last) * (1.0 / TERMINAL_SCALE),
            terminal_ref[...],
            tile(below, last) * (1.0 / TERMINAL_SCALE),
        ],
        axis=0,
    )
    high = u.shape[0]
    partial = [None] * steps
    kept = [None] * steps
    for t in reversed(range(steps)):
        coupled = levels(t) * slope + offset
        behind_r = u - pltpu.roll(u, 1, 0)
        ahead_r = pltpu.roll(u, high - 1, 0) - u
        behind_c = u - pltpu.roll(u, 1, 1)
        ahead_c = pltpu.roll(u, cols - 1, 1) - u
        lap = (ahead_r - behind_r) + (ahead_c - behind_c)
        br = jnp.maximum(behind_r, 0.0)
        ar = jnp.minimum(ahead_r, 0.0)
        bc = jnp.maximum(behind_c, 0.0)
        ac = jnp.minimum(ahead_c, 0.0)
        ham = 0.5 * (br * br + ar * ar + bc * bc + ac * ac)
        u = u + time_step * (viscosity * lap - ham + coupled)
        u_ref[t] = u
        mine = u[HALO : 2 * HALO]
        kept[t] = mine
        lanes = mine[:, :128]
        for k in range(1, cols // 128):
            lanes = lanes + mine[:, k * 128 : (k + 1) * 128]
        partial[t] = jnp.sum(lanes, axis=0, keepdims=True)
    sums = jnp.concatenate(partial, axis=0)
    sums_ref[...] = jnp.broadcast_to(sums[None], sums_ref.shape)
    row = lax.broadcasted_iota(jnp.int32, (HALO, cols), 0)
    edge_ref[0:8] = init_ref[...]
    edge_ref[8:16] = kept[0]
    edge_ref[16:24] = jnp.where((row >= 1) & (row <= 6), kept[1], pltpu.roll(kept[3], 4, 0))
    edge_ref[24:32] = kept[2]


def forward_kernel(
    cells, steps, u_ref, init_ref, above_ref, below_ref, sums_ref, values_ref, final_ref
):
    cols = init_ref.shape[1]
    means = jnp.sum(jnp.sum(sums_ref[...], axis=0), axis=1, keepdims=True) * (1.0 / cells)
    row = lax.broadcasted_iota(jnp.int32, (HALO, cols), 0)
    m = jnp.concatenate([above_ref[0:8], init_ref[...], below_ref[0:8]], axis=0)
    high = m.shape[0]

    def field(t):
        u = u_ref[t]
        if t > 3:
            return u

        def side(ref, near):
            if t == 0:
                return ref[8:16]
            if t == 1:
                return jnp.where((row >= 1) & (row <= 6), ref[16:24], near)
            if t == 2:
                return jnp.where((row >= 2) & (row <= 5), ref[24:32], near)
            return jnp.where((row >= 3) & (row <= 4), pltpu.roll(ref[16:24], 4, 0), near)

        return jnp.concatenate(
            [side(above_ref, u[0:8]), u[8:16], side(below_ref, u[16:24])], axis=0
        )

    for t in range(steps):
        values_ref[t] = u_ref[t, HALO : 2 * HALO, :] - means[t : t + 1, :]
        u = field(t)
        down_m = pltpu.roll(m, high - 1, 0)
        right_m = pltpu.roll(m, cols - 1, 1)
        drift_r = u - pltpu.roll(u, high - 1, 0)
        drift_c = u - pltpu.roll(u, cols - 1, 1)
        flux_r = (
            jnp.maximum(drift_r, 0.0) * m
            + jnp.minimum(drift_r, 0.0) * down_m
            - viscosity * (down_m - m)
        )
        flux_c = (
            jnp.maximum(drift_c, 0.0) * m
            + jnp.minimum(drift_c, 0.0) * right_m
            - viscosity * (right_m - m)
        )
        m = m - time_step * (
            (flux_r - pltpu.roll(flux_r, 1, 0)) + (flux_c - pltpu.roll(flux_c, 1, 1))
        )
    final_ref[...] = m[HALO : 2 * HALO]


def call(kernel, outs, *args):
    spec = pl.BlockSpec(memory_space=pltpu.VMEM)
    return pl.pallas_call(
        kernel,
        out_shape=outs,
        in_specs=[spec] * len(args),
        out_specs=jax.tree.map(lambda _: spec, outs),
        compiler_params=pltpu.CompilerParams(vmem_limit_bytes=40 * 1024 * 1024),
    )(*args)


def shifted(x, by):
    peers = lax.axis_size("tile")
    return lax.ppermute(x, "tile", [(i, (i + by) % peers) for i in range(peers)])


def per_device(weights, terminal, density_history, density_init):
    pops = weights.shape[0]
    steps, rows, cols = density_history.shape[1:]
    tiles = lax.axis_size("tile")
    blocks = pops // steps
    part = cols // blocks
    struct = jax.ShapeDtypeStruct
    terminal = terminal[0]
    init = density_init[0]
    chunks = density_history[0].reshape(steps, rows, blocks, part).transpose(0, 2, 1, 3)
    chunks = lax.all_to_all(chunks.reshape(pops, rows, part), POP, 0, 0, tiled=True)
    levels = call(
        coupling_kernel, struct((pops * rows, part), I16), weights, chunks.reshape(pops * rows, part)
    )
    levels = lax.all_to_all(levels.reshape(pops, rows, part), POP, 0, 0, tiled=True)
    levels = levels.reshape(pops * rows, part)
    down, up = call(
        functools.partial(pack_kernel, blocks, steps),
        (struct((40, cols), I16), struct((40, cols), I16)),
        levels,
        terminal,
    )
    above = shifted(down, 1)
    below = shifted(up, -1)
    fields, edges, sums = call(
        functools.partial(backward_kernel, blocks, steps),
        (
            struct((steps, 3 * HALO, cols), F32),
            struct((32, cols), F32),
            struct((tiles, steps, 128), F32),
        ),
        weights,
        levels,
        terminal,
        init,
        above,
        below,
    )
    above = shifted(edges, 1)
    below = shifted(edges, -1)
    sums = lax.all_to_all(sums, "tile", 0, 0, tiled=True)
    values, final = call(
        functools.partial(forward_kernel, float(tiles * rows * cols), steps),
        (struct((steps, rows, cols), F32), struct((rows, cols), F32)),
        fields,
        init,
        above,
        below,
        sums,
    )
    return values[None], final[None]


def solution(mesh):
    split = Mesh(
        mesh.devices.reshape(8, 2, 2, mesh.shape["tile"]), ("pop_0", "pop_1", "pop_2", "tile")
    )
    in_specs = (P(), P(POP, "tile", None), P(POP, None, "tile", None), P(POP, "tile", None))
    out_specs = (P(POP, None, "tile", None), P(POP, "tile", None))
    return jax.shard_map(
        per_device, mesh=split, in_specs=in_specs, out_specs=out_specs, check_vma=False
    )
```

time: 326 us -> 87 us (0.27)
  the two profiles are of different devices: /device:TPU:6 before, /device:TPU:8 now
where the time goes in v1:
time: 87 us; the launch traced here: 86.6 us
  blocking collectives  55.9 us (64%)
  starting transfers between devices  21.3 us (24%)
  Pallas kernels  5.07 us (6%)
  waiting for transfers between devices  2.82 us (3%)
    all_to_all x1, blocking collectives, per_device(): lax.all_to_all(chunks.reshape(pops, rows, part), POP, 0, 0, tiled=True)  23.3 us
    ppermute x4, starting transfers between devices, shifted(): lax.ppermute(x, 'tile', [(i, (i + by) % peers) for i in range(peers)])  21.3 us
    all_to_all x1, blocking collectives, per_device(): lax.all_to_all(levels.reshape(pops, rows, part), POP, 0, 0, tiled=True)  16.9 us
    all_to_all x1, blocking collectives, per_device(): sums = lax.all_to_all(sums, 'tile', 0, 0, tiled=True)  15.7 us
    pallas_call x4, Pallas kernels, call(): pl.pallas_call(kernel, out_shape=outs, in_specs=[spec] * len(args), out_s...  5.07 us
    ppermute x4, waiting for transfers between devices, shifted(): lax.ppermute(x, 'tile', [(i, (i + by) % peers) for i in range(peers)])  2.82 us
  transfers between devices with their start and end apart: 4, of which 2 were waited for; matrix products, arithmetic and copies ran while one was open for 0% of the time, Pallas kernels for 0%

profile of v1, /device:TPU:8, one launch (start us, length us, event | category | flops | bytes accessed | tf_op | source)
XLA Modules:
  0.0 86.6 jit_solution(4389776916156659285)
XLA Ops:
  0.6 0.0 copy-start
  0.6 0.0 copy-start.1
  0.7 23.3 %all_to_all.15 = bf16[32,8,512]{2,1,0:T(8,128)(2,1)S(1)} all-to-all(bf16[32,8,512]{2,1,0:T(8,128)(2,1)} %bitcast.20), channel_id=1, replica_groups=mesh['pop_0'=8,'pop_1'=2,'pop_2'=2,'tile'=16] {'pop_0','pop_1','pop_2'}, dimensions={0} | all-to-all | bytes 524288 | tf_op jit(solution)/shard_map/all_to_all | solution.py:225
  24.0 0.0 copy-start.2
  24.0 0.7 copy-done.2
  24.7 0.4 shard_map.59
  25.1 16.9 %all_to_all.16 = s16[32,8,512]{2,1,0:T(8,128)(2,1)S(1)} all-to-all(s16[32,8,512]{2,1,0:T(8,128)(2,1)S(1)} %bitcast.14), channel_id=1, replica_groups=mesh['pop_0'=8,'pop_1'=2,'pop_2'=2,'tile'=16] {'pop_0','pop_1','pop_2'}, dimensions={0} | all-to-all | bytes 524288 | tf_op jit(solution)/shard_map/all_to_all | solution.py:229
  42.0 0.0 copy-done
  42.0 0.1 shard_map.60
  42.1 2.5 %collective-permute-start = (s16[40,2048]{1,0:T(8,128)(2,1)S(1)}, s16[40,2048]{1,0:T(8,128)(2,1)S(1)}, u32[]{:S(2)}, u32[]{:S(2)}) collective-permute-start(s16[40,2048]{1,0:T(8,128)(2,1)S(1)} %get-tuple-element.9), channel_id=1, source_target_pairs={{0,1},{1,2},{2,3},{3,4},{4,5},{5,6},{6,7},{7,8},{8,9},{9,10},{10,1... | collective-permute-start | bytes 491528 | tf_op jit(solution)/shard_map/ppermute | solution.py:212
  44.6 10.4 %collective-permute-start.1 = (s16[40,2048]{1,0:T(8,128)(2,1)S(1)}, s16[40,2048]{1,0:T(8,128)(2,1)S(1)}, u32[]{:S(2)}, u32[]{:S(2)}) collective-permute-start(s16[40,2048]{1,0:T(8,128)(2,1)S(1)} %get-tuple-element.10), channel_id=1, source_target_pairs={{0,15},{1,0},{2,1},{3,2},{4,3},{5,4},{6,5},{7,6},{8,7},{9,8},{10,9... | collective-permute-start | bytes 491528 | tf_op jit(solution)/shard_map/ppermute | solution.py:212
  55.0 1.4 %collective-permute-done.above_ref = s16[40,2048]{1,0:T(8,128)(2,1)S(1)} collective-permute-done((s16[40,2048]{1,0:T(8,128)(2,1)S(1)}, s16[40,2048]{1,0:T(8,128)(2,1)S(1)}, u32[]{:S(2)}, u32[]{:S(2)}) %collective-permute-start) | collective-permute-done | bytes 163872 | tf_op jit(solution)/shard_map/ppermute | solution.py:212
  56.4 1.4 %collective-permute-done.1.below_ref = s16[40,2048]{1,0:T(8,128)(2,1)S(1)} collective-permute-done((s16[40,2048]{1,0:T(8,128)(2,1)S(1)}, s16[40,2048]{1,0:T(8,128)(2,1)S(1)}, u32[]{:S(2)}, u32[]{:S(2)}) %collective-permute-start.1) | collective-permute-done | bytes 163872 | tf_op jit(solution)/shard_map/ppermute | solution.py:212
  57.8 0.0 copy-done.1
  57.8 1.8 %shard_map.61 = (f32[8,24,2048]{2,1,0:T(8,128)S(1)}, f32[32,2048]{1,0:T(8,128)S(1)}, f32[16,8,128]{2,1,0:T(8,128)S(1)}) custom-call(s32[32,32]{1,0:T(8,128)S(1)} %copy-done.2, s16[256,512]{1,0:T(8,128)(2,1)S(1)} %bitcast.13, f32[8,2048]{1,0:T(8,128)S(1)} %bitcast.17, f32[8,2048]{1,0:T(8,128)S(1)} %bitcast.18, ...), custom_call_target="tpu_custom_call" | custom-call | tf_op jit(solution)/shard_map/pallas_call | solution.py:201
  59.6 6.5 %collective-permute-start.3 = (f32[32,2048]{1,0:T(8,128)S(1)}, f32[32,2048]{1,0:T(8,128)S(1)}, u32[]{:S(2)}, u32[]{:S(2)}) collective-permute-start(f32[32,2048]{1,0:T(8,128)S(1)} %get-tuple-element.12), channel_id=1, source_target_pairs={{0,15},{1,0},{2,1},{3,2},{4,3},{5,4},{6,5},{7,6},{8,7},{9,8},{10,9... | collective-permute-start | bytes 786440 | tf_op jit(solution)/shard_map/ppermute | solution.py:212
  66.2 1.9 %collective-permute-start.2 = (f32[32,2048]{1,0:T(8,128)S(1)}, f32[32,2048]{1,0:T(8,128)S(1)}, u32[]{:S(2)}, u32[]{:S(2)}) collective-permute-start(f32[32,2048]{1,0:T(8,128)S(1)} %get-tuple-element.12), channel_id=1, source_target_pairs={{0,1},{1,2},{2,3},{3,4},{4,5},{5,6},{6,7},{7,8},{8,9},{9,10},{10,1... | collective-permute-start | bytes 786440 | tf_op jit(solution)/shard_map/ppermute | solution.py:212
  68.1 15.7 %all_to_all.17.sums_ref = f32[16,8,128]{2,1,0:T(8,128)S(1)} all-to-all(f32[16,8,128]{2,1,0:T(8,128)S(1)} %get-tuple-element.13), channel_id=1, replica_groups=mesh['pop_0'=8,'pop_1'=2,'pop_2'=2,'tile'=16] {'tile'}, dimensions={0} | all-to-all | bytes 131072 | tf_op jit(solution)/shard_map/all_to_all | solution.py:255
  83.8 0.0 collective-permute-done.3.below_ref
  83.8 0.0 collective-permute-done.2.above_ref
  83.8 2.7 %shard_map.62 = (f32[8,8,2048]{2,1,0:T(8,128)}, f32[8,2048]{1,0:T(8,128)}) custom-call(f32[8,24,2048]{2,1,0:T(8,128)S(1)} %get-tuple-element.11.u_ref, f32[8,2048]{1,0:T(8,128)S(1)} %bitcast.19, f32[32,2048]{1,0:T(8,128)S(1)} %collective-permute-done.2.above_ref, f32[32,2048]{1,0:T(8,128)S(1)} %collective-permute-done.3.below_ref, ...), custom_call_target="tpu_custom_call" | custom-call | tf_op jit(solution)/shard_map/pallas_call | solution.py:201
Async XLA Ops:
  0.6 41.4 %copy-start = (f32[1,8,2048]{2,1,0:T(8,128)S(1)}, f32[1,8,2048]{2,1,0:T(8,128)}, u32[]{:S(2)}) copy-start(f32[1,8,2048]{2,1,0:T(8,128)} %param.5) | copy-start | bytes 196612
  0.6 57.2 %copy-start.1 = (f32[1,8,2048]{2,1,0:T(8,128)S(1)}, f32[1,8,2048]{2,1,0:T(8,128)}, u32[]{:S(2)}) copy-start(f32[1,8,2048]{2,1,0:T(8,128)} %param.7) | copy-start | bytes 196612
  24.0 0.7 copy-start.2
  42.1 14.3 %collective-permute-start = (s16[40,2048]{1,0:T(8,128)(2,1)S(1)}, s16[40,2048]{1,0:T(8,128)(2,1)S(1)}, u32[]{:S(2)}, u32[]{:S(2)}) collective-permute-start(s16[40,2048]{1,0:T(8,128)(2,1)S(1)} %get-tuple-element.9), channel_id=1, source_target_pairs={{0,1},{1,2},{2,3},{3,4},{4,5},{5,6},{6,7},{7,8},{8,9},{9,10},{10,1... | collective-permute-start | bytes 491528 | tf_op jit(solution)/shard_map/ppermute | solution.py:212
  44.6 13.2 %collective-permute-start.1 = (s16[40,2048]{1,0:T(8,128)(2,1)S(1)}, s16[40,2048]{1,0:T(8,128)(2,1)S(1)}, u32[]{:S(2)}, u32[]{:S(2)}) collective-permute-start(s16[40,2048]{1,0:T(8,128)(2,1)S(1)} %get-tuple-element.10), channel_id=1, source_target_pairs={{0,15},{1,0},{2,1},{3,2},{4,3},{5,4},{6,5},{7,6},{8,7},{9,8},{10,9... | collective-permute-start | bytes 491528 | tf_op jit(solution)/shard_map/ppermute | solution.py:212
  59.6 24.2 %collective-permute-start.3 = (f32[32,2048]{1,0:T(8,128)S(1)}, f32[32,2048]{1,0:T(8,128)S(1)}, u32[]{:S(2)}, u32[]{:S(2)}) collective-permute-start(f32[32,2048]{1,0:T(8,128)S(1)} %get-tuple-element.12), channel_id=1, source_target_pairs={{0,15},{1,0},{2,1},{3,2},{4,3},{5,4},{6,5},{7,6},{8,7},{9,8},{10,9... | collective-permute-start | bytes 786440 | tf_op jit(solution)/shard_map/ppermute | solution.py:212
  66.2 17.7 %collective-permute-start.2 = (f32[32,2048]{1,0:T(8,128)S(1)}, f32[32,2048]{1,0:T(8,128)S(1)}, u32[]{:S(2)}, u32[]{:S(2)}) collective-permute-start(f32[32,2048]{1,0:T(8,128)S(1)} %get-tuple-element.12), channel_id=1, source_target_pairs={{0,1},{1,2},{2,3},{3,4},{4,5},{5,6},{6,7},{7,8},{8,9},{9,10},{10,1... | collective-permute-start | bytes 786440 | tf_op jit(solution)/shard_map/ppermute | solution.py:212

commit v2 on v1

--- a/solution.py
+++ b/solution.py
@@ -57,7 +57,11 @@
     )
 
 
-def pack_kernel(blocks, steps, c_ref, terminal_ref, down_ref, up_ref):
+def is_even():
+    return (lax.axis_index("tile") & 1) == 0
+
+
+def pack_kernel(blocks, steps, c_ref, terminal_ref, first_ref, second_ref):
     wide = c_ref[...].astype(F32)
     c = [rows_of_step(wide, t, blocks) for t in range(steps)]
     row = lax.broadcasted_iota(jnp.int32, c[0].shape, 0)
@@ -66,15 +70,16 @@
     for t in range(1, HALO // 2):
         down.append(jnp.where(row >= t, c[HALO - t], pltpu.roll(c[t], t, 0)))
         up.append(jnp.where(row < HALO - t, c[HALO - t], pltpu.roll(c[t], HALO - t, 0)))
-    down.append(c[HALO // 2])
-    up.append(c[HALO // 2])
+    even = is_even()
     edge = terminal_ref[...] * TERMINAL_SCALE
-    down_ref[...] = to_i16(jnp.concatenate(down + [edge], axis=0))
-    up_ref[...] = to_i16(jnp.concatenate(up + [edge], axis=0))
+    first = [jnp.where(even, d, u) for d, u in zip(down, up)] + [c[HALO // 2], edge]
+    second = [jnp.where(even, u, d) for d, u in zip(down, up)] + [c[HALO // 2], edge]
+    first_ref[...] = to_i16(jnp.concatenate(first, axis=0))
+    second_ref[...] = to_i16(jnp.concatenate(second, axis=0))
 
 
 def backward_kernel(
-    blocks, steps, w_ref, c_ref, terminal_ref, init_ref, above_ref, below_ref, u_ref, edge_ref, sums_ref
+    blocks, steps, w_ref, c_ref, terminal_ref, init_ref, first_ref, second_ref, u_ref, edge_ref, sums_ref
 ):
     pops = w_ref.shape[0]
     cols = terminal_ref.shape[1]
@@ -85,8 +90,11 @@
     slope = size * (DENSITY_HALF / (LEVELS * pops))
     offset = total * (DENSITY_MID / pops)
     wide = c_ref[...].astype(F32)
-    above = above_ref[...].astype(F32)
-    below = below_ref[...].astype(F32)
+    even = is_even()
+    first = first_ref[...].astype(F32)
+    second = second_ref[...].astype(F32)
+    above = jnp.where(even, second, first)
+    below = jnp.where(even, first, second)
 
     def tile(x, k):
         return x[k * HALO : (k + 1) * HALO]
@@ -137,8 +145,11 @@
         for k in range(1, cols // 128):
             lanes = lanes + mine[:, k * 128 : (k + 1) * 128]
         partial[t] = jnp.sum(lanes, axis=0, keepdims=True)
-    sums = jnp.concatenate(partial, axis=0)
-    sums_ref[...] = jnp.broadcast_to(sums[None], sums_ref.shape)
+    sums = jnp.sum(jnp.concatenate(partial, axis=0), axis=1, keepdims=True)
+    lane = lax.broadcasted_iota(jnp.int32, (steps, 128), 1)
+    step = lax.broadcasted_iota(jnp.int32, (steps, 128), 0)
+    line = jnp.sum(jnp.where(lane == step, sums, 0.0), axis=0, keepdims=True)
+    sums_ref[...] = jnp.broadcast_to(line[None], sums_ref.shape)
     row = lax.broadcasted_iota(jnp.int32, (HALO, cols), 0)
     edge_ref[0:8] = init_ref[...]
     edge_ref[8:16] = kept[0]
@@ -147,12 +158,17 @@
 
 
 def forward_kernel(
-    cells, steps, u_ref, init_ref, above_ref, below_ref, sums_ref, values_ref, final_ref
+    cells, steps, u_ref, init_ref, second_ref, first_ref, sums_ref, values_ref, final_ref
 ):
     cols = init_ref.shape[1]
-    means = jnp.sum(jnp.sum(sums_ref[...], axis=0), axis=1, keepdims=True) * (1.0 / cells)
+    means = jnp.sum(sums_ref[...], axis=0) * (1.0 / cells)
     row = lax.broadcasted_iota(jnp.int32, (HALO, cols), 0)
-    m = jnp.concatenate([above_ref[0:8], init_ref[...], below_ref[0:8]], axis=0)
+    even = is_even()
+    first = first_ref[...]
+    second = second_ref[...]
+    above = jnp.where(even, second, first)
+    below = jnp.where(even, first, second)
+    m = jnp.concatenate([above[0:8], init_ref[...], below[0:8]], axis=0)
     high = m.shape[0]
 
     def field(t):
@@ -160,21 +176,21 @@
         if t > 3:
             return u
 
-        def side(ref, near):
+        def side(far, near):
             if t == 0:
-                return ref[8:16]
+                return far[8:16]
             if t == 1:
-                return jnp.where((row >= 1) & (row <= 6), ref[16:24], near)
+                return jnp.where((row >= 1) & (row <= 6), far[16:24], near)
             if t == 2:
-                return jnp.where((row >= 2) & (row <= 5), ref[24:32], near)
-            return jnp.where((row >= 3) & (row <= 4), pltpu.roll(ref[16:24], 4, 0), near)
+                return jnp.where((row >= 2) & (row <= 5), far[24:32], near)
+            return jnp.where((row >= 3) & (row <= 4), pltpu.roll(far[16:24], 4, 0), near)
 
         return jnp.concatenate(
-            [side(above_ref, u[0:8]), u[8:16], side(below_ref, u[16:24])], axis=0
+            [side(above, u[0:8]), u[8:16], side(below, u[16:24])], axis=0
         )
 
     for t in range(steps):
-        values_ref[t] = u_ref[t, HALO : 2 * HALO, :] - means[t : t + 1, :]
+        values_ref[t] = u_ref[t, HALO : 2 * HALO, :] - means[:, t : t + 1]
         u = field(t)
         down_m = pltpu.roll(m, high - 1, 0)
         right_m = pltpu.roll(m, cols - 1, 1)
@@ -207,9 +223,14 @@
     )(*args)
 
 
-def shifted(x, by):
+def first_swap(x):
     peers = lax.axis_size("tile")
-    return lax.ppermute(x, "tile", [(i, (i + by) % peers) for i in range(peers)])
+    return lax.ppermute(x, "tile", [(i, i ^ 1) for i in range(peers)])
+
+
+def second_swap(x):
+    peers = lax.axis_size("tile")
+    return lax.ppermute(x, "tile", [(i, (((i + 1) ^ 1) - 1) % peers) for i in range(peers)])
 
 
 def per_device(weights, terminal, density_history, density_init):
@@ -228,38 +249,38 @@
     )
     levels = lax.all_to_all(levels.reshape(pops, rows, part), POP, 0, 0, tiled=True)
     levels = levels.reshape(pops * rows, part)
-    down, up = call(
+    first, second = call(
         functools.partial(pack_kernel, blocks, steps),
         (struct((40, cols), I16), struct((40, cols), I16)),
         levels,
         terminal,
     )
-    above = shifted(down, 1)
-    below = shifted(up, -1)
+    second = second_swap(second)
+    first = first_swap(first)
     fields, edges, sums = call(
         functools.partial(backward_kernel, blocks, steps),
         (
             struct((steps, 3 * HALO, cols), F32),
             struct((32, cols), F32),
-            struct((tiles, steps, 128), F32),
+            struct((tiles, 1, 128), F32),
         ),
         weights,
         levels,
         terminal,
         init,
-        above,
-        below,
-    )
-    above = shifted(edges, 1)
-    below = shifted(edges, -1)
+        first,
+        second,
+    )
+    first = first_swap(edges)
+    second = second_swap(edges)
     sums = lax.all_to_all(sums, "tile", 0, 0, tiled=True)
     values, final = call(
         functools.partial(forward_kernel, float(tiles * rows * cols), steps),
         (struct((steps, rows, cols), F32), struct((rows, cols), F32)),
         fields,
         init,
-        above,
-        below,
+        second,
+        first,
         sums,
     )
     return values[None], final[None]

time: 87 us -> 85.5 us (0.983)
  blocking collectives: 55.9 us -> 52.8 us
  starting transfers between devices: 21.3 us -> 22.3 us
    all_to_all x1, blocking collectives: 15.7 us -> 12.6 us  [per_device(): sums = lax.all_to_all(sums, 'tile', 0, 0, tiled=True)]
    ppermute x4, starting transfers between devices: 21.3 us -> 22.3 us  [the longest x2 17.8 us: second_swap(): lax.ppermute(x, 'tile', [(i, ((i + 1 ^ 1) - 1) % peers) for i in range(pe...]
  transfers between devices with their start and end apart: 4 -> 4, of which waited for: 2 -> 1; matrix products, arithmetic and copies ran while one was open for 0% -> 0% of each run, Pallas kernels for 0% -> 0%
where the time goes in v2:
time: 85.5 us; the launch traced here: 85 us
  blocking collectives  52.8 us (62%)
  starting transfers between devices  22.3 us (26%)
  Pallas kernels  5.27 us (6%)
  waiting for transfers between devices  3.28 us (4%)
    all_to_all x1, blocking collectives, per_device(): lax.all_to_all(chunks.reshape(pops, rows, part), POP, 0, 0, tiled=True)  23.3 us
    ppermute x2, starting transfers between devices, second_swap(): lax.ppermute(x, 'tile', [(i, ((i + 1 ^ 1) - 1) % peers) for i in range(pe...  17.8 us
    all_to_all x1, blocking collectives, per_device(): lax.all_to_all(levels.reshape(pops, rows, part), POP, 0, 0, tiled=True)  16.9 us
    all_to_all x1, blocking collectives, per_device(): sums = lax.all_to_all(sums, 'tile', 0, 0, tiled=True)  12.6 us
    pallas_call x4, Pallas kernels, call(): pl.pallas_call(kernel, out_shape=outs, in_specs=[spec] * len(args), out_s...  5.27 us
    ppermute x2, starting transfers between devices, first_swap(): return lax.ppermute(x, 'tile', [(i, i ^ 1) for i in range(peers)])  4.42 us
    ppermute x2, waiting for transfers between devices, second_swap(): lax.ppermute(x, 'tile', [(i, ((i + 1 ^ 1) - 1) % peers) for i in range(pe...  3.27 us
  transfers between devices with their start and end apart: 4, of which 1 were waited for; matrix products, arithmetic and copies ran while one was open for 0% of the time, Pallas kernels for 0%

profile of v2, /device:TPU:8, one launch (start us, length us, event | category | flops | bytes accessed | tf_op | source)
XLA Modules:
  0.0 85.0 jit_solution(8137618183699871847)
XLA Ops:
  0.6 0.0 copy-start
  0.6 0.0 copy-start.1
  0.7 23.3 %all_to_all.15 = bf16[32,8,512]{2,1,0:T(8,128)(2,1)S(1)} all-to-all(bf16[32,8,512]{2,1,0:T(8,128)(2,1)} %bitcast.20), channel_id=1, replica_groups=mesh['pop_0'=8,'pop_1'=2,'pop_2'=2,'tile'=16] {'pop_0','pop_1','pop_2'}, dimensions={0} | all-to-all | bytes 524288 | tf_op jit(solution)/shard_map/all_to_all | solution.py:246
  24.0 0.0 copy-start.2
  24.0 0.7 copy-done.2
  24.7 0.4 shard_map.59
  25.1 16.9 %all_to_all.16 = s16[32,8,512]{2,1,0:T(8,128)(2,1)S(1)} all-to-all(s16[32,8,512]{2,1,0:T(8,128)(2,1)S(1)} %bitcast.14), channel_id=1, replica_groups=mesh['pop_0'=8,'pop_1'=2,'pop_2'=2,'tile'=16] {'pop_0','pop_1','pop_2'}, dimensions={0} | all-to-all | bytes 524288 | tf_op jit(solution)/shard_map/all_to_all | solution.py:250
  42.0 0.0 copy-done
  42.0 0.1 shard_map.60
  42.1 2.5 %collective-permute-start = (s16[40,2048]{1,0:T(8,128)(2,1)S(1)}, s16[40,2048]{1,0:T(8,128)(2,1)S(1)}, u32[]{:S(2)}, u32[]{:S(2)}) collective-permute-start(s16[40,2048]{1,0:T(8,128)(2,1)S(1)} %get-tuple-element.9), channel_id=1, source_target_pairs={{0,1},{1,0},{2,3},{3,2},{4,5},{5,4},{6,7},{7,6},{8,9},{9,8},{10,11... | collective-permute-start | bytes 491528 | tf_op jit(solution)/shard_map/ppermute | solution.py:228
  44.6 11.8 %collective-permute-start.1 = (s16[40,2048]{1,0:T(8,128)(2,1)S(1)}, s16[40,2048]{1,0:T(8,128)(2,1)S(1)}, u32[]{:S(2)}, u32[]{:S(2)}) collective-permute-start(s16[40,2048]{1,0:T(8,128)(2,1)S(1)} %get-tuple-element.10), channel_id=1, source_target_pairs={{0,15},{1,2},{2,1},{3,4},{4,3},{5,6},{6,5},{7,8},{8,7},{9,10},{10,... | collective-permute-start | bytes 491528 | tf_op jit(solution)/shard_map/ppermute | solution.py:233
  56.4 0.0 collective-permute-done.first_ref
  56.5 3.3 %collective-permute-done.1.second_ref = s16[40,2048]{1,0:T(8,128)(2,1)S(1)} collective-permute-done((s16[40,2048]{1,0:T(8,128)(2,1)S(1)}, s16[40,2048]{1,0:T(8,128)(2,1)S(1)}, u32[]{:S(2)}, u32[]{:S(2)}) %collective-permute-start.1) | collective-permute-done | bytes 163872 | tf_op jit(solution)/shard_map/ppermute | solution.py:233
  59.7 0.0 copy-done.1
  59.7 1.9 %shard_map.61 = (f32[8,24,2048]{2,1,0:T(8,128)S(1)}, f32[32,2048]{1,0:T(8,128)S(1)}, f32[16,1,128]{2,1,0:T(1,128)S(1)}) custom-call(s32[32,32]{1,0:T(8,128)S(1)} %copy-done.2, s16[256,512]{1,0:T(8,128)(2,1)S(1)} %bitcast.13, f32[8,2048]{1,0:T(8,128)S(1)} %bitcast.17, f32[8,2048]{1,0:T(8,128)S(1)} %bitcast.18, ...), custom_call_target="tpu_custom_call" | custom-call | tf_op jit(solution)/shard_map/pallas_call | solution.py:217
  61.6 1.9 %collective-permute-start.3 = (f32[32,2048]{1,0:T(8,128)S(1)}, f32[32,2048]{1,0:T(8,128)S(1)}, u32[]{:S(2)}, u32[]{:S(2)}) collective-permute-start(f32[32,2048]{1,0:T(8,128)S(1)} %get-tuple-element.12), channel_id=1, source_target_pairs={{0,1},{1,0},{2,3},{3,2},{4,5},{5,4},{6,7},{7,6},{8,9},{9,8},{10,11... | collective-permute-start | bytes 786440 | tf_op jit(solution)/shard_map/ppermute | solution.py:228
  63.6 6.0 %collective-permute-start.2 = (f32[32,2048]{1,0:T(8,128)S(1)}, f32[32,2048]{1,0:T(8,128)S(1)}, u32[]{:S(2)}, u32[]{:S(2)}) collective-permute-start(f32[32,2048]{1,0:T(8,128)S(1)} %get-tuple-element.12), channel_id=1, source_target_pairs={{0,15},{1,2},{2,1},{3,4},{4,3},{5,6},{6,5},{7,8},{8,7},{9,10},{10,... | collective-permute-start | bytes 786440 | tf_op jit(solution)/shard_map/ppermute | solution.py:233
  69.6 12.6 %all_to_all.17.sums_ref = f32[16,1,128]{2,1,0:T(1,128)S(1)} all-to-all(f32[16,1,128]{2,1,0:T(1,128)S(1)} %get-tuple-element.13), channel_id=1, replica_groups=mesh['pop_0'=8,'pop_1'=2,'pop_2'=2,'tile'=16] {'tile'}, dimensions={0} | all-to-all | bytes 16384 | tf_op jit(solution)/shard_map/all_to_all | solution.py:276
  82.2 0.0 collective-permute-done.3.first_ref
  82.2 0.0 collective-permute-done.2.second_ref
  82.2 2.8 %shard_map.62 = (f32[8,8,2048]{2,1,0:T(8,128)}, f32[8,2048]{1,0:T(8,128)}) custom-call(f32[8,24,2048]{2,1,0:T(8,128)S(1)} %get-tuple-element.11.u_ref, f32[8,2048]{1,0:T(8,128)S(1)} %bitcast.19, f32[32,2048]{1,0:T(8,128)S(1)} %collective-permute-done.2.second_ref, f32[32,2048]{1,0:T(8,128)S(1)} %collective-permute-done.3.first_ref, ...), custom_call_target="tpu_custom_call" | custom-call | tf_op jit(solution)/shard_map/pallas_call | solution.py:217
Async XLA Ops:
  0.6 41.4 %copy-start = (f32[1,8,2048]{2,1,0:T(8,128)S(1)}, f32[1,8,2048]{2,1,0:T(8,128)}, u32[]{:S(2)}) copy-start(f32[1,8,2048]{2,1,0:T(8,128)} %param.5) | copy-start | bytes 196612
  0.6 59.1 %copy-start.1 = (f32[1,8,2048]{2,1,0:T(8,128)S(1)}, f32[1,8,2048]{2,1,0:T(8,128)}, u32[]{:S(2)}) copy-start(f32[1,8,2048]{2,1,0:T(8,128)} %param.7) | copy-start | bytes 196612
  24.0 0.7 copy-start.2
  42.1 14.3 %collective-permute-start = (s16[40,2048]{1,0:T(8,128)(2,1)S(1)}, s16[40,2048]{1,0:T(8,128)(2,1)S(1)}, u32[]{:S(2)}, u32[]{:S(2)}) collective-permute-start(s16[40,2048]{1,0:T(8,128)(2,1)S(1)} %get-tuple-element.9), channel_id=1, source_target_pairs={{0,1},{1,0},{2,3},{3,2},{4,5},{5,4},{6,7},{7,6},{8,9},{9,8},{10,11... | collective-permute-start | bytes 491528 | tf_op jit(solution)/shard_map/ppermute | solution.py:228
  44.6 15.1 %collective-permute-start.1 = (s16[40,2048]{1,0:T(8,128)(2,1)S(1)}, s16[40,2048]{1,0:T(8,128)(2,1)S(1)}, u32[]{:S(2)}, u32[]{:S(2)}) collective-permute-start(s16[40,2048]{1,0:T(8,128)(2,1)S(1)} %get-tuple-element.10), channel_id=1, source_target_pairs={{0,15},{1,2},{2,1},{3,4},{4,3},{5,6},{6,5},{7,8},{8,7},{9,10},{10,... | collective-permute-start | bytes 491528 | tf_op jit(solution)/shard_map/ppermute | solution.py:233
  61.6 20.6 %collective-permute-start.3 = (f32[32,2048]{1,0:T(8,128)S(1)}, f32[32,2048]{1,0:T(8,128)S(1)}, u32[]{:S(2)}, u32[]{:S(2)}) collective-permute-start(f32[32,2048]{1,0:T(8,128)S(1)} %get-tuple-element.12), channel_id=1, source_target_pairs={{0,1},{1,0},{2,3},{3,2},{4,5},{5,4},{6,7},{7,6},{8,9},{9,8},{10,11... | collective-permute-start | bytes 786440 | tf_op jit(solution)/shard_map/ppermute | solution.py:228
  63.6 18.6 %collective-permute-start.2 = (f32[32,2048]{1,0:T(8,128)S(1)}, f32[32,2048]{1,0:T(8,128)S(1)}, u32[]{:S(2)}, u32[]{:S(2)}) collective-permute-start(f32[32,2048]{1,0:T(8,128)S(1)} %get-tuple-element.12), channel_id=1, source_target_pairs={{0,15},{1,2},{2,1},{3,4},{4,3},{5,6},{6,5},{7,8},{8,7},{9,10},{10,... | collective-permute-start | bytes 786440 | tf_op jit(solution)/shard_map/ppermute | solution.py:233

commit v3 on v2

--- a/solution.py
+++ b/solution.py
@@ -27,9 +27,9 @@
     return jnp.round(x).astype(jnp.int32).astype(I16)
 
 
-def coupling_kernel(w_ref, x_ref, out_ref):
+def spread_kernel(w_ref, kron_ref, scale_ref):
     pops = w_ref.shape[0]
-    rows = x_ref.shape[0]
+    rows = kron_ref.shape[0]
     per = rows // pops
     shift = per.bit_length() - 1
     weights = w_ref[...].astype(F32).astype(jnp.bfloat16)
@@ -44,10 +44,16 @@
     )
     a = lax.broadcasted_iota(jnp.int32, (rows, rows), 0)
     b = lax.broadcasted_iota(jnp.int32, (rows, rows), 1)
-    kron = jnp.where((a & (per - 1)) == (b & (per - 1)), wide, 0.0).astype(jnp.bfloat16)
-    product = jnp.dot(kron, x_ref[...], preferred_element_type=F32)
-    level = (product - DENSITY_MID * total) * (LEVELS / (DENSITY_HALF * size))
-    out_ref[...] = to_i16(level)
+    kron_ref[...] = jnp.where((a & (per - 1)) == (b & (per - 1)), wide, 0.0).astype(jnp.bfloat16)
+    lane = lax.broadcasted_iota(jnp.int32, scale_ref.shape, 1)
+    scale_ref[...] = jnp.where(
+        lane == 0, DENSITY_MID * total, LEVELS / (DENSITY_HALF * size)
+    )
+
+
+def coupling_kernel(kron_ref, scale_ref, x_ref, out_ref):
+    product = jnp.dot(kron_ref[...], x_ref[...], preferred_element_type=F32)
+    out_ref[...] = to_i16((product - scale_ref[:, 0:1]) * scale_ref[:, 1:2])
 
 
 def rows_of_step(wide, step, blocks):
@@ -158,10 +164,9 @@
 
 
 def forward_kernel(
-    cells, steps, u_ref, init_ref, second_ref, first_ref, sums_ref, values_ref, final_ref
+    steps, u_ref, init_ref, second_ref, first_ref, final_ref
 ):
     cols = init_ref.shape[1]
-    means = jnp.sum(sums_ref[...], axis=0) * (1.0 / cells)
     row = lax.broadcasted_iota(jnp.int32, (HALO, cols), 0)
     even = is_even()
     first = first_ref[...]
@@ -190,7 +195,6 @@
         )
 
     for t in range(steps):
-        values_ref[t] = u_ref[t, HALO : 2 * HALO, :] - means[:, t : t + 1]
         u = field(t)
         down_m = pltpu.roll(m, high - 1, 0)
         right_m = pltpu.roll(m, cols - 1, 1)
@@ -212,6 +216,12 @@
     final_ref[...] = m[HALO : 2 * HALO]
 
 
+def centre_kernel(cells, steps, u_ref, sums_ref, values_ref):
+    means = jnp.sum(sums_ref[...], axis=0) * (1.0 / cells)
+    for t in range(steps):
+        values_ref[t] = u_ref[t, HALO : 2 * HALO, :] - means[:, t : t + 1]
+
+
 def call(kernel, outs, *args):
     spec = pl.BlockSpec(memory_space=pltpu.VMEM)
     return pl.pallas_call(
@@ -244,8 +254,17 @@
     init = density_init[0]
     chunks = density_history[0].reshape(steps, rows, blocks, part).transpose(0, 2, 1, 3)
     chunks = lax.all_to_all(chunks.reshape(pops, rows, part), POP, 0, 0, tiled=True)
+    kron, scale = call(
+        spread_kernel,
+        (struct((pops * rows, pops * rows), jnp.bfloat16), struct((pops * rows, 128), F32)),
+        weights,
+    )
     levels = call(
-        coupling_kernel, struct((pops * rows, part), I16), weights, chunks.reshape(pops * rows, part)
+        coupling_kernel,
+        struct((pops * rows, part), I16),
+        kron,
+        scale,
+        chunks.reshape(pops * rows, part),
     )
     levels = lax.all_to_all(levels.reshape(pops, rows, part), POP, 0, 0, tiled=True)
     levels = levels.reshape(pops * rows, part)
@@ -274,13 +293,19 @@
     first = first_swap(edges)
     second = second_swap(edges)
     sums = lax.all_to_all(sums, "tile", 0, 0, tiled=True)
-    values, final = call(
-        functools.partial(forward_kernel, float(tiles * rows * cols), steps),
-        (struct((steps, rows, cols), F32), struct((rows, cols), F32)),
+    final = call(
+        functools.partial(forward_kernel, steps),
+        struct((rows, cols), F32),
         fields,
         init,
         second,
         first,
+    )
+    sums, final = lax.optimization_barrier((sums, final))
+    values = call(
+        functools.partial(centre_kernel, float(tiles * rows * cols), steps),
+        struct((steps, rows, cols), F32),
+        fields,
         sums,
     )
     return values[None], final[None]

time: 85.5 us -> 83.4 us (0.975)
  blocking collectives: 52.8 us -> 16.9 us
  waiting for transfers between devices: 3.28 us -> 21.1 us
  starting transfers between devices: 22.3 us -> 36.9 us
  Pallas kernels: 5.27 us -> 6.61 us
    all_to_all x2 -> x0, blocking collectives: 35.9 us -> none  [the longest x1 23.3 us: per_device(): lax.all_to_all(chunks.reshape(pops, rows, part), POP, 0, 0, tiled=True)]
    all_to_all x0 -> x2, waiting for transfers between devices: none -> 16.2 us  [the longest x1 12 us: per_device(): lax.all_to_all(chunks.reshape(pops, rows, part), POP, 0, 0, tiled=True)]
    all_to_all x0 -> x2, starting transfers between devices: none -> 14.6 us  [the longest x1 10.3 us: per_device(): lax.all_to_all(chunks.reshape(pops, rows, part), POP, 0, 0, tiled=True)]
    ppermute x2, waiting for transfers between devices: 0.01 us -> 1.63 us  [first_swap(): return lax.ppermute(x, 'tile', [(i, i ^ 1) for i in range(peers)])]
    pallas_call x4 -> x6, Pallas kernels: 5.27 us -> 6.61 us  [call(): pl.pallas_call(kernel, out_shape=outs, in_specs=[spec] * len(args), out_s...]
  transfers between devices with their start and end apart: 4 -> 6, of which waited for: 1 -> 4; matrix products, arithmetic and copies ran while one was open for 0% -> 0% of each run, Pallas kernels for 0% -> 3%
where the time goes in v3:
time: 83.4 us; the launch traced here: 82.9 us
  starting transfers between devices  36.9 us (44%)
  waiting for transfers between devices  21.1 us (25%)
  blocking collectives  16.9 us (20%)
  Pallas kernels  6.61 us (8%)
    ppermute x2, starting transfers between devices, second_swap(): lax.ppermute(x, 'tile', [(i, ((i + 1 ^ 1) - 1) % peers) for i in range(pe...  17.8 us
    all_to_all x1, blocking collectives, per_device(): lax.all_to_all(levels.reshape(pops, rows, part), POP, 0, 0, tiled=True)  16.9 us
    all_to_all x1, waiting for transfers between devices, per_device(): lax.all_to_all(chunks.reshape(pops, rows, part), POP, 0, 0, tiled=True)  12 us
    all_to_all x1, starting transfers between devices, per_device(): lax.all_to_all(chunks.reshape(pops, rows, part), POP, 0, 0, tiled=True)  10.3 us
    pallas_call x6, Pallas kernels, call(): pl.pallas_call(kernel, out_shape=outs, in_specs=[spec] * len(args), out_s...  6.61 us
    ppermute x2, starting transfers between devices, first_swap(): return lax.ppermute(x, 'tile', [(i, i ^ 1) for i in range(peers)])  4.41 us
    all_to_all x1, starting transfers between devices, per_device(): sums = lax.all_to_all(sums, 'tile', 0, 0, tiled=True)  4.31 us
    all_to_all x1, waiting for transfers between devices, per_device(): sums = lax.all_to_all(sums, 'tile', 0, 0, tiled=True)  4.2 us
  transfers between devices with their start and end apart: 6, of which 4 were waited for; matrix products, arithmetic and copies ran while one was open for 0% of the time, Pallas kernels for 3%

profile of v3, /device:TPU:8, one launch (start us, length us, event | category | flops | bytes accessed | tf_op | source)
XLA Modules:
  0.0 82.9 jit_solution(2578206119481933840)
XLA Ops:
  0.6 0.0 copy-start
  0.6 0.0 copy-start.1
  0.6 10.3 %all-to-all-start = ((bf16[32,8,512]{2,1,0:T(8,128)(2,1)}), bf16[32,8,512]{2,1,0:T(8,128)(2,1)S(1)}, u32[]{:S(2)}, u32[]{:S(2)}) async-start(bf16[32,8,512]{2,1,0:T(8,128)(2,1)} %bitcast.21), calls=%async_computation | async-start | bytes 524288 | tf_op jit(solution)/shard_map/all_to_all | solution.py:256
  11.0 0.0 copy-start.2
  11.0 0.7 copy-done.2
  11.7 0.3 shard_map.59
  12.0 12.0 %all-to-all-done = bf16[32,8,512]{2,1,0:T(8,128)(2,1)S(1)} async-done(((bf16[32,8,512]{2,1,0:T(8,128)(2,1)}), bf16[32,8,512]{2,1,0:T(8,128)(2,1)S(1)}, u32[]{:S(2)}, u32[]{:S(2)}) %all-to-all-start) | async-done | bytes 262176 | tf_op jit(solution)/shard_map/all_to_all | solution.py:256
  24.0 0.2 shard_map.60
  24.2 16.9 %all_to_all.15 = s16[32,8,512]{2,1,0:T(8,128)(2,1)S(1)} all-to-all(s16[32,8,512]{2,1,0:T(8,128)(2,1)S(1)} %bitcast.15), channel_id=1, replica_groups=mesh['pop_0'=8,'pop_1'=2,'pop_2'=2,'tile'=16] {'pop_0','pop_1','pop_2'}, dimensions={0} | all-to-all | bytes 524288 | tf_op jit(solution)/shard_map/all_to_all | solution.py:269
  41.1 0.0 copy-done
  41.1 0.1 shard_map.61
  41.2 2.5 %collective-permute-start = (s16[40,2048]{1,0:T(8,128)(2,1)S(1)}, s16[40,2048]{1,0:T(8,128)(2,1)S(1)}, u32[]{:S(2)}, u32[]{:S(2)}) collective-permute-start(s16[40,2048]{1,0:T(8,128)(2,1)S(1)} %get-tuple-element.13), channel_id=1, source_target_pairs={{0,1},{1,0},{2,3},{3,2},{4,5},{5,4},{6,7},{7,6},{8,9},{9,8},{10,11... | collective-permute-start | bytes 491528 | tf_op jit(solution)/shard_map/ppermute | solution.py:238
  43.7 11.8 %collective-permute-start.1 = (s16[40,2048]{1,0:T(8,128)(2,1)S(1)}, s16[40,2048]{1,0:T(8,128)(2,1)S(1)}, u32[]{:S(2)}, u32[]{:S(2)}) collective-permute-start(s16[40,2048]{1,0:T(8,128)(2,1)S(1)} %get-tuple-element.14), channel_id=1, source_target_pairs={{0,15},{1,2},{2,1},{3,4},{4,3},{5,6},{6,5},{7,8},{8,7},{9,10},{10,... | collective-permute-start | bytes 491528 | tf_op jit(solution)/shard_map/ppermute | solution.py:243
  55.5 0.0 collective-permute-done.first_ref
  55.5 3.3 %collective-permute-done.1.second_ref = s16[40,2048]{1,0:T(8,128)(2,1)S(1)} collective-permute-done((s16[40,2048]{1,0:T(8,128)(2,1)S(1)}, s16[40,2048]{1,0:T(8,128)(2,1)S(1)}, u32[]{:S(2)}, u32[]{:S(2)}) %collective-permute-start.1) | collective-permute-done | bytes 163872 | tf_op jit(solution)/shard_map/ppermute | solution.py:243
  58.8 0.0 copy-done.1
  58.8 2.4 %shard_map.62 = (f32[8,24,2048]{2,1,0:T(8,128)S(1)}, f32[32,2048]{1,0:T(8,128)S(1)}, f32[16,1,128]{2,1,0:T(1,128)}) custom-call(s32[32,32]{1,0:T(8,128)S(1)} %copy-done.2, s16[256,512]{1,0:T(8,128)(2,1)S(1)} %bitcast.13, f32[8,2048]{1,0:T(8,128)S(1)} %bitcast.17, f32[8,2048]{1,0:T(8,128)S(1)} %bitcast.18, ...), custom_call_target="tpu_custom_call" | custom-call | tf_op jit(solution)/shard_map/pallas_call | solution.py:227
  61.2 1.9 %collective-permute-start.3 = (f32[32,2048]{1,0:T(8,128)S(1)}, f32[32,2048]{1,0:T(8,128)S(1)}, u32[]{:S(2)}, u32[]{:S(2)}) collective-permute-start(f32[32,2048]{1,0:T(8,128)S(1)} %get-tuple-element.17), channel_id=1, source_target_pairs={{0,1},{1,0},{2,3},{3,2},{4,5},{5,4},{6,7},{7,6},{8,9},{9,8},{10,11... | collective-permute-start | bytes 786440 | tf_op jit(solution)/shard_map/ppermute | solution.py:238
  63.2 6.0 %collective-permute-start.2 = (f32[32,2048]{1,0:T(8,128)S(1)}, f32[32,2048]{1,0:T(8,128)S(1)}, u32[]{:S(2)}, u32[]{:S(2)}) collective-permute-start(f32[32,2048]{1,0:T(8,128)S(1)} %get-tuple-element.17), channel_id=1, source_target_pairs={{0,15},{1,2},{2,1},{3,4},{4,3},{5,6},{6,5},{7,8},{8,7},{9,10},{10,... | collective-permute-start | bytes 786440 | tf_op jit(solution)/shard_map/ppermute | solution.py:243
  69.2 4.3 %all-to-all-start.2 = ((f32[16,1,128]{2,1,0:T(1,128)}), f32[16,1,128]{2,1,0:T(1,128)S(1)}, u32[]{:S(2)}, u32[]{:S(2)}) async-start(f32[16,1,128]{2,1,0:T(1,128)} %get-tuple-element.16), calls=%async_computation.2 | async-start | bytes 16384 | tf_op jit(solution)/shard_map/all_to_all | solution.py:295
  73.5 1.6 %collective-permute-done.3.first_ref = f32[32,2048]{1,0:T(8,128)S(1)} collective-permute-done((f32[32,2048]{1,0:T(8,128)S(1)}, f32[32,2048]{1,0:T(8,128)S(1)}, u32[]{:S(2)}, u32[]{:S(2)}) %collective-permute-start.3) | collective-permute-done | bytes 262176 | tf_op jit(solution)/shard_map/ppermute | solution.py:238
  75.1 0.0 collective-permute-done.2.second_ref
  75.1 2.6 %shard_map.63 = f32[8,2048]{1,0:T(8,128)} custom-call(f32[8,24,2048]{2,1,0:T(8,128)S(1)} %get-tuple-element.15.u_ref, f32[8,2048]{1,0:T(8,128)S(1)} %bitcast.19, f32[32,2048]{1,0:T(8,128)S(1)} %collective-permute-done.2.second_ref, f32[32,2048]{1,0:T(8,128)S(1)} %collective-permute-done.3.first_ref), custom_call_target="tpu_custom_call" | custom-call | tf_op jit(solution)/shard_map/pallas_call | solution.py:227
  77.7 4.2 %all-to-all-done.2.sums_ref = f32[16,1,128]{2,1,0:T(1,128)S(1)} async-done(((f32[16,1,128]{2,1,0:T(1,128)}), f32[16,1,128]{2,1,0:T(1,128)S(1)}, u32[]{:S(2)}, u32[]{:S(2)}) %all-to-all-start.2) | async-done | bytes 8224 | tf_op jit(solution)/shard_map/all_to_all | solution.py:295
  81.9 0.9 %shard_map.64 = f32[8,8,2048]{2,1,0:T(8,128)} custom-call(f32[8,24,2048]{2,1,0:T(8,128)S(1)} %get-tuple-element.15.u_ref, f32[16,1,128]{2,1,0:T(1,128)S(1)} %all-to-all-done.2.sums_ref), custom_call_target="tpu_custom_call" | custom-call | tf_op jit(solution)/shard_map/pallas_call | solution.py:227
Async XLA Ops:
  0.6 40.5 %copy-start = (f32[1,8,2048]{2,1,0:T(8,128)S(1)}, f32[1,8,2048]{2,1,0:T(8,128)}, u32[]{:S(2)}) copy-start(f32[1,8,2048]{2,1,0:T(8,128)} %param.5) | copy-start | bytes 196612
  0.6 58.2 %copy-start.1 = (f32[1,8,2048]{2,1,0:T(8,128)S(1)}, f32[1,8,2048]{2,1,0:T(8,128)}, u32[]{:S(2)}) copy-start(f32[1,8,2048]{2,1,0:T(8,128)} %param.7) | copy-start | bytes 196612
  0.6 23.3 %all-to-all-start = ((bf16[32,8,512]{2,1,0:T(8,128)(2,1)}), bf16[32,8,512]{2,1,0:T(8,128)(2,1)S(1)}, u32[]{:S(2)}, u32[]{:S(2)}) async-start(bf16[32,8,512]{2,1,0:T(8,128)(2,1)} %bitcast.21), calls=%async_computation | async-start | bytes 524288 | tf_op jit(solution)/shard_map/all_to_all | solution.py:256
  11.0 0.7 copy-start.2
  41.2 14.3 %collective-permute-start = (s16[40,2048]{1,0:T(8,128)(2,1)S(1)}, s16[40,2048]{1,0:T(8,128)(2,1)S(1)}, u32[]{:S(2)}, u32[]{:S(2)}) collective-permute-start(s16[40,2048]{1,0:T(8,128)(2,1)S(1)} %get-tuple-element.13), channel_id=1, source_target_pairs={{0,1},{1,0},{2,3},{3,2},{4,5},{5,4},{6,7},{7,6},{8,9},{9,8},{10,11... | collective-permute-start | bytes 491528 | tf_op jit(solution)/shard_map/ppermute | solution.py:238
  43.7 15.1 %collective-permute-start.1 = (s16[40,2048]{1,0:T(8,128)(2,1)S(1)}, s16[40,2048]{1,0:T(8,128)(2,1)S(1)}, u32[]{:S(2)}, u32[]{:S(2)}) collective-permute-start(s16[40,2048]{1,0:T(8,128)(2,1)S(1)} %get-tuple-element.14), channel_id=1, source_target_pairs={{0,15},{1,2},{2,1},{3,4},{4,3},{5,6},{6,5},{7,8},{8,7},{9,10},{10,... | collective-permute-start | bytes 491528 | tf_op jit(solution)/shard_map/ppermute | solution.py:243
  61.2 13.9 %collective-permute-start.3 = (f32[32,2048]{1,0:T(8,128)S(1)}, f32[32,2048]{1,0:T(8,128)S(1)}, u32[]{:S(2)}, u32[]{:S(2)}) collective-permute-start(f32[32,2048]{1,0:T(8,128)S(1)} %get-tuple-element.17), channel_id=1, source_target_pairs={{0,1},{1,0},{2,3},{3,2},{4,5},{5,4},{6,7},{7,6},{8,9},{9,8},{10,11... | collective-permute-start | bytes 786440 | tf_op jit(solution)/shard_map/ppermute | solution.py:238
  63.2 12.0 %collective-permute-start.2 = (f32[32,2048]{1,0:T(8,128)S(1)}, f32[32,2048]{1,0:T(8,128)S(1)}, u32[]{:S(2)}, u32[]{:S(2)}) collective-permute-start(f32[32,2048]{1,0:T(8,128)S(1)} %get-tuple-element.17), channel_id=1, source_target_pairs={{0,15},{1,2},{2,1},{3,4},{4,3},{5,6},{6,5},{7,8},{8,7},{9,10},{10,... | collective-permute-start | bytes 786440 | tf_op jit(solution)/shard_map/ppermute | solution.py:243
  69.2 12.7 %all-to-all-start.2 = ((f32[16,1,128]{2,1,0:T(1,128)}), f32[16,1,128]{2,1,0:T(1,128)S(1)}, u32[]{:S(2)}, u32[]{:S(2)}) async-start(f32[16,1,128]{2,1,0:T(1,128)} %get-tuple-element.16), calls=%async_computation.2 | async-start | bytes 16384 | tf_op jit(solution)/shard_map/all_to_all | solution.py:295

commit v4 on v3

--- a/solution.py
+++ b/solution.py
@@ -17,6 +17,8 @@
 DENSITY_HALF = (2.0 - 0.19921875) / 2
 LEVELS = 32000.0
 TERMINAL_SCALE = 32000.0 / 4.5
+INIT_MID = 1.1
+INIT_SCALE = 32000.0 / 0.9
 
 HALO = 8
 F32 = jnp.float32
@@ -157,10 +159,31 @@
     line = jnp.sum(jnp.where(lane == step, sums, 0.0), axis=0, keepdims=True)
     sums_ref[...] = jnp.broadcast_to(line[None], sums_ref.shape)
     row = lax.broadcasted_iota(jnp.int32, (HALO, cols), 0)
-    edge_ref[0:8] = init_ref[...]
-    edge_ref[8:16] = kept[0]
-    edge_ref[16:24] = jnp.where((row >= 1) & (row <= 6), kept[1], pltpu.roll(kept[3], 4, 0))
-    edge_ref[24:32] = kept[2]
+    largest = jnp.maximum(
+        jnp.maximum(jnp.abs(kept[0]), jnp.abs(kept[1])),
+        jnp.maximum(jnp.abs(kept[2]), jnp.abs(kept[3])),
+    )
+    largest = jnp.max(jnp.max(largest, axis=1, keepdims=True), axis=0, keepdims=True)
+    exponent = jnp.ceil(jnp.log2(jnp.maximum(largest, 1e-30)))
+    scale = LEVELS / jnp.exp2(exponent)
+    inner = jnp.where((row >= 1) & (row <= 6), kept[1], pltpu.roll(kept[3], 4, 0))
+    edge_ref[...] = to_i16(
+        jnp.concatenate(
+            [
+                (init_ref[...] - INIT_MID) * INIT_SCALE,
+                kept[0] * scale,
+                inner * scale,
+                jnp.where(row == 0, exponent, kept[2] * scale),
+            ],
+            axis=0,
+        )
+    )
+
+
+def decoded(edge):
+    edge = edge.astype(F32)
+    size = jnp.exp2(edge[24:25, 0:1]) * (1.0 / LEVELS)
+    return jnp.concatenate([edge[0:8] * (1.0 / INIT_SCALE) + INIT_MID, edge[8:32] * size], axis=0)
 
 
 def forward_kernel(
@@ -169,8 +192,8 @@
     cols = init_ref.shape[1]
     row = lax.broadcasted_iota(jnp.int32, (HALO, cols), 0)
     even = is_even()
-    first = first_ref[...]
-    second = second_ref[...]
+    first = decoded(first_ref[...])
+    second = decoded(second_ref[...])
     above = jnp.where(even, second, first)
     below = jnp.where(even, first, second)
     m = jnp.concatenate([above[0:8], init_ref[...], below[0:8]], axis=0)
@@ -217,7 +240,7 @@
 
 
 def centre_kernel(cells, steps, u_ref, sums_ref, values_ref):
-    means = jnp.sum(sums_ref[...], axis=0) * (1.0 / cells)
+    means = jnp.sum(sums_ref[:, 0:1, :], axis=0) * (1.0 / cells)
     for t in range(steps):
         values_ref[t] = u_ref[t, HALO : 2 * HALO, :] - means[:, t : t + 1]
 
@@ -280,8 +303,8 @@
         functools.partial(backward_kernel, blocks, steps),
         (
             struct((steps, 3 * HALO, cols), F32),
-            struct((32, cols), F32),
-            struct((tiles, 1, 128), F32),
+            struct((32, cols), I16),
+            struct((tiles, 16, 128), F32),
         ),
         weights,
         levels,

time: 83.4 us -> 83.7 us (level)
  starting transfers between devices: 36.9 us -> 38.5 us
  waiting for transfers between devices: 21.1 us -> 19.6 us
    ppermute x2, waiting for transfers between devices: 3.27 us -> 7.64 us  [second_swap(): lax.ppermute(x, 'tile', [(i, ((i + 1 ^ 1) - 1) % peers) for i in range(pe...]
    all_to_all x1, waiting for transfers between devices: 4.2 us -> 0.01 us  [per_device(): sums = lax.all_to_all(sums, 'tile', 0, 0, tiled=True)]
    ppermute x2, starting transfers between devices: 4.41 us -> 6.33 us  [first_swap(): return lax.ppermute(x, 'tile', [(i, i ^ 1) for i in range(peers)])]
    ppermute x2, waiting for transfers between devices: 1.63 us -> 0.01 us  [first_swap(): return lax.ppermute(x, 'tile', [(i, i ^ 1) for i in range(peers)])]
    ppermute x2, starting transfers between devices: 17.8 us -> 16.4 us  [second_swap(): lax.ppermute(x, 'tile', [(i, ((i + 1 ^ 1) - 1) % peers) for i in range(pe...]
    all_to_all x1, starting transfers between devices: 4.31 us -> 5.5 us  [per_device(): sums = lax.all_to_all(sums, 'tile', 0, 0, tiled=True)]
  transfers between devices with their start and end apart: 6 -> 6, of which waited for: 4 -> 3; matrix products, arithmetic and copies ran while one was open for 0% -> 0% of each run, Pallas kernels for 3% -> 4%
where the time goes in v4:
time: 83.7 us; the launch traced here: 83.2 us
  starting transfers between devices  38.5 us (46%)
  waiting for transfers between devices  19.6 us (23%)
  blocking collectives  16.9 us (20%)
  Pallas kernels  6.74 us (8%)
    all_to_all x1, blocking collectives, per_device(): lax.all_to_all(levels.reshape(pops, rows, part), POP, 0, 0, tiled=True)  16.9 us
    ppermute x2, starting transfers between devices, second_swap(): lax.ppermute(x, 'tile', [(i, ((i + 1 ^ 1) - 1) % peers) for i in range(pe...  16.4 us
    all_to_all x1, waiting for transfers between devices, per_device(): lax.all_to_all(chunks.reshape(pops, rows, part), POP, 0, 0, tiled=True)  12 us
    all_to_all x1, starting transfers between devices, per_device(): lax.all_to_all(chunks.reshape(pops, rows, part), POP, 0, 0, tiled=True)  10.3 us
    ppermute x2, waiting for transfers between devices, second_swap(): lax.ppermute(x, 'tile', [(i, ((i + 1 ^ 1) - 1) % peers) for i in range(pe...  7.64 us
    pallas_call x6, Pallas kernels, call(): pl.pallas_call(kernel, out_shape=outs, in_specs=[spec] * len(args), out_s...  6.74 us
    ppermute x2, starting transfers between devices, first_swap(): return lax.ppermute(x, 'tile', [(i, i ^ 1) for i in range(peers)])  6.33 us
    all_to_all x1, starting transfers between devices, per_device(): sums = lax.all_to_all(sums, 'tile', 0, 0, tiled=True)  5.5 us
  transfers between devices with their start and end apart: 6, of which 3 were waited for; matrix products, arithmetic and copies ran while one was open for 0% of the time, Pallas kernels for 4%

profile of v4, /device:TPU:8, one launch (start us, length us, event | category | flops | bytes accessed | tf_op | source)
XLA Modules:
  0.0 83.2 jit_solution(8549830520775703356)
XLA Ops:
  0.6 0.0 copy-start
  0.6 0.0 copy-start.1
  0.6 10.3 %all-to-all-start = ((bf16[32,8,512]{2,1,0:T(8,128)(2,1)}), bf16[32,8,512]{2,1,0:T(8,128)(2,1)S(1)}, u32[]{:S(2)}, u32[]{:S(2)}) async-start(bf16[32,8,512]{2,1,0:T(8,128)(2,1)} %bitcast.21), calls=%async_computation | async-start | bytes 524288 | tf_op jit(solution)/shard_map/all_to_all | solution.py:279
  11.0 0.0 copy-start.2
  11.0 0.7 copy-done.2
  11.7 0.3 shard_map.59
  12.0 12.0 %all-to-all-done = bf16[32,8,512]{2,1,0:T(8,128)(2,1)S(1)} async-done(((bf16[32,8,512]{2,1,0:T(8,128)(2,1)}), bf16[32,8,512]{2,1,0:T(8,128)(2,1)S(1)}, u32[]{:S(2)}, u32[]{:S(2)}) %all-to-all-start) | async-done | bytes 262176 | tf_op jit(solution)/shard_map/all_to_all | solution.py:279
  24.0 0.2 shard_map.60
  24.2 16.9 %all_to_all.15 = s16[32,8,512]{2,1,0:T(8,128)(2,1)S(1)} all-to-all(s16[32,8,512]{2,1,0:T(8,128)(2,1)S(1)} %bitcast.15), channel_id=1, replica_groups=mesh['pop_0'=8,'pop_1'=2,'pop_2'=2,'tile'=16] {'pop_0','pop_1','pop_2'}, dimensions={0} | all-to-all | bytes 524288 | tf_op jit(solution)/shard_map/all_to_all | solution.py:292
  41.1 0.0 copy-done
  41.1 0.1 shard_map.61
  41.2 2.5 %collective-permute-start = (s16[40,2048]{1,0:T(8,128)(2,1)S(1)}, s16[40,2048]{1,0:T(8,128)(2,1)S(1)}, u32[]{:S(2)}, u32[]{:S(2)}) collective-permute-start(s16[40,2048]{1,0:T(8,128)(2,1)S(1)} %get-tuple-element.13), channel_id=1, source_target_pairs={{0,1},{1,0},{2,3},{3,2},{4,5},{5,4},{6,7},{7,6},{8,9},{9,8},{10,11... | collective-permute-start | bytes 491528 | tf_op jit(solution)/shard_map/ppermute | solution.py:261
  43.7 11.8 %collective-permute-start.1 = (s16[40,2048]{1,0:T(8,128)(2,1)S(1)}, s16[40,2048]{1,0:T(8,128)(2,1)S(1)}, u32[]{:S(2)}, u32[]{:S(2)}) collective-permute-start(s16[40,2048]{1,0:T(8,128)(2,1)S(1)} %get-tuple-element.14), channel_id=1, source_target_pairs={{0,15},{1,2},{2,1},{3,4},{4,3},{5,6},{6,5},{7,8},{8,7},{9,10},{10,... | collective-permute-start | bytes 491528 | tf_op jit(solution)/shard_map/ppermute | solution.py:266
  55.5 0.0 collective-permute-done.first_ref
  55.5 3.3 %collective-permute-done.1.second_ref = s16[40,2048]{1,0:T(8,128)(2,1)S(1)} collective-permute-done((s16[40,2048]{1,0:T(8,128)(2,1)S(1)}, s16[40,2048]{1,0:T(8,128)(2,1)S(1)}, u32[]{:S(2)}, u32[]{:S(2)}) %collective-permute-start.1) | collective-permute-done | bytes 163872 | tf_op jit(solution)/shard_map/ppermute | solution.py:266
  58.8 0.0 copy-done.1
  58.8 2.5 %shard_map.62 = (f32[8,24,2048]{2,1,0:T(8,128)S(1)}, s16[32,2048]{1,0:T(8,128)(2,1)S(1)}, f32[16,16,128]{2,1,0:T(8,128)}) custom-call(s32[32,32]{1,0:T(8,128)S(1)} %copy-done.2, s16[256,512]{1,0:T(8,128)(2,1)S(1)} %bitcast.13, f32[8,2048]{1,0:T(8,128)S(1)} %bitcast.17, f32[8,2048]{1,0:T(8,128)S(1)} %bitcast.18, ...), custom_call_target="tpu_custom_call" | custom-call | tf_op jit(solution)/shard_map/pallas_call | solution.py:250
  61.3 5.5 %all-to-all-start.2 = ((f32[16,16,128]{2,1,0:T(8,128)}), f32[16,16,128]{2,1,0:T(8,128)S(1)}, u32[]{:S(2)}, u32[]{:S(2)}) async-start(f32[16,16,128]{2,1,0:T(8,128)} %get-tuple-element.16), calls=%async_computation.2 | async-start | bytes 262144 | tf_op jit(solution)/shard_map/all_to_all | solution.py:318
  66.9 3.8 %collective-permute-start.3 = (s16[32,2048]{1,0:T(8,128)(2,1)S(1)}, s16[32,2048]{1,0:T(8,128)(2,1)S(1)}, u32[]{:S(2)}, u32[]{:S(2)}) collective-permute-start(s16[32,2048]{1,0:T(8,128)(2,1)S(1)} %get-tuple-element.17), channel_id=1, source_target_pairs={{0,1},{1,0},{2,3},{3,2},{4,5},{5,4},{6,7},{7,6},{8,9},{9,8},{10,11... | collective-permute-start | bytes 393224 | tf_op jit(solution)/shard_map/ppermute | solution.py:261
  70.7 4.6 %collective-permute-start.2 = (s16[32,2048]{1,0:T(8,128)(2,1)S(1)}, s16[32,2048]{1,0:T(8,128)(2,1)S(1)}, u32[]{:S(2)}, u32[]{:S(2)}) collective-permute-start(s16[32,2048]{1,0:T(8,128)(2,1)S(1)} %get-tuple-element.17), channel_id=1, source_target_pairs={{0,15},{1,2},{2,1},{3,4},{4,3},{5,6},{6,5},{7,8},{8,7},{9,10},{10,... | collective-permute-start | bytes 393224 | tf_op jit(solution)/shard_map/ppermute | solution.py:266
  75.3 0.0 collective-permute-done.3.first_ref
  75.3 4.4 %collective-permute-done.2.second_ref = s16[32,2048]{1,0:T(8,128)(2,1)S(1)} collective-permute-done((s16[32,2048]{1,0:T(8,128)(2,1)S(1)}, s16[32,2048]{1,0:T(8,128)(2,1)S(1)}, u32[]{:S(2)}, u32[]{:S(2)}) %collective-permute-start.2) | collective-permute-done | bytes 131104 | tf_op jit(solution)/shard_map/ppermute | solution.py:266
  79.7 2.6 %shard_map.63 = f32[8,2048]{1,0:T(8,128)} custom-call(f32[8,24,2048]{2,1,0:T(8,128)S(1)} %get-tuple-element.15.u_ref, f32[8,2048]{1,0:T(8,128)S(1)} %bitcast.19, s16[32,2048]{1,0:T(8,128)(2,1)S(1)} %collective-permute-done.2.second_ref, s16[32,2048]{1,0:T(8,128)(2,1)S(1)} %collective-permute-done.3.first_ref), custom_call_target="tpu_custom_call" | custom-call | tf_op jit(solution)/shard_map/pallas_call | solution.py:250
  82.3 0.0 all-to-all-done.2.sums_ref
  82.3 0.9 %shard_map.64 = f32[8,8,2048]{2,1,0:T(8,128)} custom-call(f32[8,24,2048]{2,1,0:T(8,128)S(1)} %get-tuple-element.15.u_ref, f32[16,16,128]{2,1,0:T(8,128)S(1)} %all-to-all-done.2.sums_ref), custom_call_target="tpu_custom_call" | custom-call | tf_op jit(solution)/shard_map/pallas_call | solution.py:250
Async XLA Ops:
  0.6 40.5 %copy-start = (f32[1,8,2048]{2,1,0:T(8,128)S(1)}, f32[1,8,2048]{2,1,0:T(8,128)}, u32[]{:S(2)}) copy-start(f32[1,8,2048]{2,1,0:T(8,128)} %param.5) | copy-start | bytes 196612
  0.6 58.2 %copy-start.1 = (f32[1,8,2048]{2,1,0:T(8,128)S(1)}, f32[1,8,2048]{2,1,0:T(8,128)}, u32[]{:S(2)}) copy-start(f32[1,8,2048]{2,1,0:T(8,128)} %param.7) | copy-start | bytes 196612
  0.6 23.3 %all-to-all-start = ((bf16[32,8,512]{2,1,0:T(8,128)(2,1)}), bf16[32,8,512]{2,1,0:T(8,128)(2,1)S(1)}, u32[]{:S(2)}, u32[]{:S(2)}) async-start(bf16[32,8,512]{2,1,0:T(8,128)(2,1)} %bitcast.21), calls=%async_computation | async-start | bytes 524288 | tf_op jit(solution)/shard_map/all_to_all | solution.py:279
  11.0 0.7 copy-start.2
  41.2 14.3 %collective-permute-start = (s16[40,2048]{1,0:T(8,128)(2,1)S(1)}, s16[40,2048]{1,0:T(8,128)(2,1)S(1)}, u32[]{:S(2)}, u32[]{:S(2)}) collective-permute-start(s16[40,2048]{1,0:T(8,128)(2,1)S(1)} %get-tuple-element.13), channel_id=1, source_target_pairs={{0,1},{1,0},{2,3},{3,2},{4,5},{5,4},{6,7},{7,6},{8,9},{9,8},{10,11... | collective-permute-start | bytes 491528 | tf_op jit(solution)/shard_map/ppermute | solution.py:261
  43.7 15.1 %collective-permute-start.1 = (s16[40,2048]{1,0:T(8,128)(2,1)S(1)}, s16[40,2048]{1,0:T(8,128)(2,1)S(1)}, u32[]{:S(2)}, u32[]{:S(2)}) collective-permute-start(s16[40,2048]{1,0:T(8,128)(2,1)S(1)} %get-tuple-element.14), channel_id=1, source_target_pairs={{0,15},{1,2},{2,1},{3,4},{4,3},{5,6},{6,5},{7,8},{8,7},{9,10},{10,... | collective-permute-start | bytes 491528 | tf_op jit(solution)/shard_map/ppermute | solution.py:266
  61.3 20.9 %all-to-all-start.2 = ((f32[16,16,128]{2,1,0:T(8,128)}), f32[16,16,128]{2,1,0:T(8,128)S(1)}, u32[]{:S(2)}, u32[]{:S(2)}) async-start(f32[16,16,128]{2,1,0:T(8,128)} %get-tuple-element.16), calls=%async_computation.2 | async-start | bytes 262144 | tf_op jit(solution)/shard_map/all_to_all | solution.py:318
  66.9 8.4 %collective-permute-start.3 = (s16[32,2048]{1,0:T(8,128)(2,1)S(1)}, s16[32,2048]{1,0:T(8,128)(2,1)S(1)}, u32[]{:S(2)}, u32[]{:S(2)}) collective-permute-start(s16[32,2048]{1,0:T(8,128)(2,1)S(1)} %get-tuple-element.17), channel_id=1, source_target_pairs={{0,1},{1,0},{2,3},{3,2},{4,5},{5,4},{6,7},{7,6},{8,9},{9,8},{10,11... | collective-permute-start | bytes 393224 | tf_op jit(solution)/shard_map/ppermute | solution.py:261
  70.7 9.0 %collective-permute-start.2 = (s16[32,2048]{1,0:T(8,128)(2,1)S(1)}, s16[32,2048]{1,0:T(8,128)(2,1)S(1)}, u32[]{:S(2)}, u32[]{:S(2)}) collective-permute-start(s16[32,2048]{1,0:T(8,128)(2,1)S(1)} %get-tuple-element.17), channel_id=1, source_target_pairs={{0,15},{1,2},{2,1},{3,4},{4,3},{5,6},{6,5},{7,8},{8,7},{9,10},{10,... | collective-permute-start | bytes 393224 | tf_op jit(solution)/shard_map/ppermute | solution.py:266

commit v5 on v4

--- a/solution.py
+++ b/solution.py
@@ -87,7 +87,7 @@
 
 
 def backward_kernel(
-    blocks, steps, w_ref, c_ref, terminal_ref, init_ref, first_ref, second_ref, u_ref, edge_ref, sums_ref
+    blocks, steps, w_ref, c_ref, terminal_ref, init_ref, first_ref, second_ref, u_ref, first_edge_ref, second_edge_ref, sums_ref
 ):
     pops = w_ref.shape[0]
     cols = terminal_ref.shape[1]
@@ -157,7 +157,9 @@
     lane = lax.broadcasted_iota(jnp.int32, (steps, 128), 1)
     step = lax.broadcasted_iota(jnp.int32, (steps, 128), 0)
     line = jnp.sum(jnp.where(lane == step, sums, 0.0), axis=0, keepdims=True)
-    sums_ref[...] = jnp.broadcast_to(line[None], sums_ref.shape)
+    sums_ref[...] = jnp.broadcast_to(
+        jnp.concatenate([line] * (sums_ref.shape[2] // 128), axis=1)[None], sums_ref.shape
+    )
     row = lax.broadcasted_iota(jnp.int32, (HALO, cols), 0)
     largest = jnp.maximum(
         jnp.maximum(jnp.abs(kept[0]), jnp.abs(kept[1])),
@@ -167,7 +169,11 @@
     exponent = jnp.ceil(jnp.log2(jnp.maximum(largest, 1e-30)))
     scale = LEVELS / jnp.exp2(exponent)
     inner = jnp.where((row >= 1) & (row <= 6), kept[1], pltpu.roll(kept[3], 4, 0))
-    edge_ref[...] = to_i16(
+    first_edge_ref[0:8] = init_ref[...]
+    first_edge_ref[8:16] = kept[0]
+    first_edge_ref[16:24] = inner
+    first_edge_ref[24:32] = kept[2]
+    second_edge_ref[...] = to_i16(
         jnp.concatenate(
             [
                 (init_ref[...] - INIT_MID) * INIT_SCALE,
@@ -192,7 +198,7 @@
     cols = init_ref.shape[1]
     row = lax.broadcasted_iota(jnp.int32, (HALO, cols), 0)
     even = is_even()
-    first = decoded(first_ref[...])
+    first = first_ref[...]
     second = decoded(second_ref[...])
     above = jnp.where(even, second, first)
     below = jnp.where(even, first, second)
@@ -240,7 +246,7 @@
 
 
 def centre_kernel(cells, steps, u_ref, sums_ref, values_ref):
-    means = jnp.sum(sums_ref[:, 0:1, :], axis=0) * (1.0 / cells)
+    means = jnp.sum(sums_ref[:, :, 0:128], axis=0) * (1.0 / cells)
     for t in range(steps):
         values_ref[t] = u_ref[t, HALO : 2 * HALO, :] - means[:, t : t + 1]
 
@@ -299,12 +305,13 @@
     )
     second = second_swap(second)
     first = first_swap(first)
-    fields, edges, sums = call(
+    fields, first, second, sums = call(
         functools.partial(backward_kernel, blocks, steps),
         (
             struct((steps, 3 * HALO, cols), F32),
+            struct((32, cols), F32),
             struct((32, cols), I16),
-            struct((tiles, 16, 128), F32),
+            struct((tiles, 1, 1152), F32),
         ),
         weights,
         levels,
@@ -313,8 +320,8 @@
         first,
         second,
     )
-    first = first_swap(edges)
-    second = second_swap(edges)
+    first = first_swap(first)
+    second = second_swap(second)
     sums = lax.all_to_all(sums, "tile", 0, 0, tiled=True)
     final = call(
         functools.partial(forward_kernel, steps),

time: 83.7 us -> 82.5 us (0.986)
  waiting for transfers between devices: 19.6 us -> 18.5 us
    ppermute x2, starting transfers between devices: 6.33 us -> 4.41 us  [first_swap(): return lax.ppermute(x, 'tile', [(i, i ^ 1) for i in range(peers)])]
    ppermute x2, starting transfers between devices: 16.4 us -> 17.8 us  [second_swap(): lax.ppermute(x, 'tile', [(i, ((i + 1 ^ 1) - 1) % peers) for i in range(pe...]
    ppermute x2, waiting for transfers between devices: 7.64 us -> 6.49 us  [second_swap(): lax.ppermute(x, 'tile', [(i, ((i + 1 ^ 1) - 1) % peers) for i in range(pe...]
where the time goes in v5:
time: 82.5 us; the launch traced here: 82 us
  starting transfers between devices  38.5 us (47%)
  waiting for transfers between devices  18.5 us (22%)
  blocking collectives  16.9 us (20%)
  Pallas kernels  6.68 us (8%)
    ppermute x2, starting transfers between devices, second_swap(): lax.ppermute(x, 'tile', [(i, ((i + 1 ^ 1) - 1) % peers) for i in range(pe...  17.8 us
    all_to_all x1, blocking collectives, per_device(): lax.all_to_all(levels.reshape(pops, rows, part), POP, 0, 0, tiled=True)  16.9 us
    all_to_all x1, waiting for transfers between devices, per_device(): lax.all_to_all(chunks.reshape(pops, rows, part), POP, 0, 0, tiled=True)  12 us
    all_to_all x1, starting transfers between devices, per_device(): lax.all_to_all(chunks.reshape(pops, rows, part), POP, 0, 0, tiled=True)  10.3 us
    pallas_call x6, Pallas kernels, call(): pl.pallas_call(kernel, out_shape=outs, in_specs=[spec] * len(args), out_s...  6.68 us
    ppermute x2, waiting for transfers between devices, second_swap(): lax.ppermute(x, 'tile', [(i, ((i + 1 ^ 1) - 1) % peers) for i in range(pe...  6.49 us
    all_to_all x1, starting transfers between devices, per_device(): sums = lax.all_to_all(sums, 'tile', 0, 0, tiled=True)  6.07 us
    ppermute x2, starting transfers between devices, first_swap(): return lax.ppermute(x, 'tile', [(i, i ^ 1) for i in range(peers)])  4.41 us
  transfers between devices with their start and end apart: 6, of which 3 were waited for; matrix products, arithmetic and copies ran while one was open for 0% of the time, Pallas kernels for 4%

profile of v5, /device:TPU:8, one launch (start us, length us, event | category | flops | bytes accessed | tf_op | source)
XLA Modules:
  0.0 82.0 jit_solution(17994088655748808972)
XLA Ops:
  0.6 0.0 copy-start.3
  0.6 0.0 copy-start
  0.6 0.0 copy-start.1
  0.7 10.3 %all-to-all-start = ((bf16[32,8,512]{2,1,0:T(8,128)(2,1)}), bf16[32,8,512]{2,1,0:T(8,128)(2,1)S(1)}, u32[]{:S(2)}, u32[]{:S(2)}) async-start(bf16[32,8,512]{2,1,0:T(8,128)(2,1)} %bitcast.21), calls=%async_computation | async-start | bytes 524288 | tf_op jit(solution)/shard_map/all_to_all | solution.py:285
  11.0 0.0 copy-start.2
  11.0 0.7 copy-done.2
  11.7 0.3 shard_map.59
  12.0 12.0 %all-to-all-done = bf16[32,8,512]{2,1,0:T(8,128)(2,1)S(1)} async-done(((bf16[32,8,512]{2,1,0:T(8,128)(2,1)}), bf16[32,8,512]{2,1,0:T(8,128)(2,1)S(1)}, u32[]{:S(2)}, u32[]{:S(2)}) %all-to-all-start) | async-done | bytes 262176 | tf_op jit(solution)/shard_map/all_to_all | solution.py:285
  24.0 0.2 shard_map.60
  24.2 16.9 %all_to_all.15 = s16[32,8,512]{2,1,0:T(8,128)(2,1)S(1)} all-to-all(s16[32,8,512]{2,1,0:T(8,128)(2,1)S(1)} %bitcast.15), channel_id=1, replica_groups=mesh['pop_0'=8,'pop_1'=2,'pop_2'=2,'tile'=16] {'pop_0','pop_1','pop_2'}, dimensions={0} | all-to-all | bytes 524288 | tf_op jit(solution)/shard_map/all_to_all | solution.py:298
  41.1 0.0 copy-done
  41.1 0.1 shard_map.61
  41.2 2.5 %collective-permute-start = (s16[40,2048]{1,0:T(8,128)(2,1)S(1)}, s16[40,2048]{1,0:T(8,128)(2,1)S(1)}, u32[]{:S(2)}, u32[]{:S(2)}) collective-permute-start(s16[40,2048]{1,0:T(8,128)(2,1)S(1)} %get-tuple-element.14), channel_id=1, source_target_pairs={{0,1},{1,0},{2,3},{3,2},{4,5},{5,4},{6,7},{7,6},{8,9},{9,8},{10,11... | collective-permute-start | bytes 491528 | tf_op jit(solution)/shard_map/ppermute | solution.py:267
  43.7 11.8 %collective-permute-start.1 = (s16[40,2048]{1,0:T(8,128)(2,1)S(1)}, s16[40,2048]{1,0:T(8,128)(2,1)S(1)}, u32[]{:S(2)}, u32[]{:S(2)}) collective-permute-start(s16[40,2048]{1,0:T(8,128)(2,1)S(1)} %get-tuple-element.15), channel_id=1, source_target_pairs={{0,15},{1,2},{2,1},{3,4},{4,3},{5,6},{6,5},{7,8},{8,7},{9,10},{10,... | collective-permute-start | bytes 491528 | tf_op jit(solution)/shard_map/ppermute | solution.py:272
  55.5 0.0 collective-permute-done.first_ref
  55.5 3.3 %collective-permute-done.1.second_ref = s16[40,2048]{1,0:T(8,128)(2,1)S(1)} collective-permute-done((s16[40,2048]{1,0:T(8,128)(2,1)S(1)}, s16[40,2048]{1,0:T(8,128)(2,1)S(1)}, u32[]{:S(2)}, u32[]{:S(2)}) %collective-permute-start.1) | collective-permute-done | bytes 163872 | tf_op jit(solution)/shard_map/ppermute | solution.py:272
  58.8 0.0 copy-done.3
  58.8 0.0 copy-done.1
  58.8 2.5 %shard_map.62 = (f32[8,24,2048]{2,1,0:T(8,128)S(1)}, f32[32,2048]{1,0:T(8,128)S(1)}, s16[32,2048]{1,0:T(8,128)(2,1)S(1)}, f32[16,1,1152]{2,1,0:T(1,128)}) custom-call(s32[32,32]{1,0:T(8,128)S(1)} %copy-done.3, s16[256,512]{1,0:T(8,128)(2,1)S(1)} %bitcast.13, f32[8,2048]{1,0:T(8,128)S(1)} %bitcast.17, f32[8,2048]{1,0:T(8,128)S(1)} %bitcast.18, ...), custom_call_target="tpu_custom_call" | custom-call | tf_op jit(solution)/shard_map/pallas_call | solution.py:256
  61.3 1.9 %collective-permute-start.3 = (f32[32,2048]{1,0:T(8,128)S(1)}, f32[32,2048]{1,0:T(8,128)S(1)}, u32[]{:S(2)}, u32[]{:S(2)}) collective-permute-start(f32[32,2048]{1,0:T(8,128)S(1)} %get-tuple-element.19), channel_id=1, source_target_pairs={{0,1},{1,0},{2,3},{3,2},{4,5},{5,4},{6,7},{7,6},{8,9},{9,8},{10,11... | collective-permute-start | bytes 786440 | tf_op jit(solution)/shard_map/ppermute | solution.py:267
  63.2 6.1 %all-to-all-start.2 = ((f32[16,1,1152]{2,1,0:T(1,128)}), f32[16,1,1152]{2,1,0:T(1,128)S(1)}, u32[]{:S(2)}, u32[]{:S(2)}) async-start(f32[16,1,1152]{2,1,0:T(1,128)} %get-tuple-element.17), calls=%async_computation.2 | async-start | bytes 147456 | tf_op jit(solution)/shard_map/all_to_all | solution.py:325
  69.3 5.9 %collective-permute-start.2 = (s16[32,2048]{1,0:T(8,128)(2,1)S(1)}, s16[32,2048]{1,0:T(8,128)(2,1)S(1)}, u32[]{:S(2)}, u32[]{:S(2)}) collective-permute-start(s16[32,2048]{1,0:T(8,128)(2,1)S(1)} %get-tuple-element.18), channel_id=1, source_target_pairs={{0,15},{1,2},{2,1},{3,4},{4,3},{5,6},{6,5},{7,8},{8,7},{9,10},{10,... | collective-permute-start | bytes 393224 | tf_op jit(solution)/shard_map/ppermute | solution.py:272
  75.2 3.2 %collective-permute-done.2.second_ref = s16[32,2048]{1,0:T(8,128)(2,1)S(1)} collective-permute-done((s16[32,2048]{1,0:T(8,128)(2,1)S(1)}, s16[32,2048]{1,0:T(8,128)(2,1)S(1)}, u32[]{:S(2)}, u32[]{:S(2)}) %collective-permute-start.2) | collective-permute-done | bytes 131104 | tf_op jit(solution)/shard_map/ppermute | solution.py:272
  78.5 0.0 collective-permute-done.3.first_ref
  78.5 2.6 %shard_map.63 = f32[8,2048]{1,0:T(8,128)} custom-call(f32[8,24,2048]{2,1,0:T(8,128)S(1)} %get-tuple-element.16.u_ref, f32[8,2048]{1,0:T(8,128)S(1)} %bitcast.19, s16[32,2048]{1,0:T(8,128)(2,1)S(1)} %collective-permute-done.2.second_ref, f32[32,2048]{1,0:T(8,128)S(1)} %collective-permute-done.3.first_ref), custom_call_target="tpu_custom_call" | custom-call | tf_op jit(solution)/shard_map/pallas_call | solution.py:256
  81.1 0.0 all-to-all-done.2.sums_ref
  81.1 0.9 %shard_map.64 = f32[8,8,2048]{2,1,0:T(8,128)} custom-call(f32[8,24,2048]{2,1,0:T(8,128)S(1)} %get-tuple-element.16.u_ref, f32[16,1,1152]{2,1,0:T(1,128)S(1)} %all-to-all-done.2.sums_ref), custom_call_target="tpu_custom_call" | custom-call | tf_op jit(solution)/shard_map/pallas_call | solution.py:256
Async XLA Ops:
  0.6 58.2 %copy-start.3 = (s32[32,32]{1,0:T(8,128)S(1)}, s32[32,32]{1,0:T(8,128)}, u32[]{:S(2)}) copy-start(s32[32,32]{1,0:T(8,128)} %w_ref.3) | copy-start | bytes 12292
  0.6 40.5 %copy-start = (f32[1,8,2048]{2,1,0:T(8,128)S(1)}, f32[1,8,2048]{2,1,0:T(8,128)}, u32[]{:S(2)}) copy-start(f32[1,8,2048]{2,1,0:T(8,128)} %param.5) | copy-start | bytes 196612
  0.6 58.2 %copy-start.1 = (f32[1,8,2048]{2,1,0:T(8,128)S(1)}, f32[1,8,2048]{2,1,0:T(8,128)}, u32[]{:S(2)}) copy-start(f32[1,8,2048]{2,1,0:T(8,128)} %param.7) | copy-start | bytes 196612
  0.7 23.3 %all-to-all-start = ((bf16[32,8,512]{2,1,0:T(8,128)(2,1)}), bf16[32,8,512]{2,1,0:T(8,128)(2,1)S(1)}, u32[]{:S(2)}, u32[]{:S(2)}) async-start(bf16[32,8,512]{2,1,0:T(8,128)(2,1)} %bitcast.21), calls=%async_computation | async-start | bytes 524288 | tf_op jit(solution)/shard_map/all_to_all | solution.py:285
  11.0 0.7 copy-start.2
  41.2 14.3 %collective-permute-start = (s16[40,2048]{1,0:T(8,128)(2,1)S(1)}, s16[40,2048]{1,0:T(8,128)(2,1)S(1)}, u32[]{:S(2)}, u32[]{:S(2)}) collective-permute-start(s16[40,2048]{1,0:T(8,128)(2,1)S(1)} %get-tuple-element.14), channel_id=1, source_target_pairs={{0,1},{1,0},{2,3},{3,2},{4,5},{5,4},{6,7},{7,6},{8,9},{9,8},{10,11... | collective-permute-start | bytes 491528 | tf_op jit(solution)/shard_map/ppermute | solution.py:267
  43.7 15.1 %collective-permute-start.1 = (s16[40,2048]{1,0:T(8,128)(2,1)S(1)}, s16[40,2048]{1,0:T(8,128)(2,1)S(1)}, u32[]{:S(2)}, u32[]{:S(2)}) collective-permute-start(s16[40,2048]{1,0:T(8,128)(2,1)S(1)} %get-tuple-element.15), channel_id=1, source_target_pairs={{0,15},{1,2},{2,1},{3,4},{4,3},{5,6},{6,5},{7,8},{8,7},{9,10},{10,... | collective-permute-start | bytes 491528 | tf_op jit(solution)/shard_map/ppermute | solution.py:272
  61.3 17.2 %collective-permute-start.3 = (f32[32,2048]{1,0:T(8,128)S(1)}, f32[32,2048]{1,0:T(8,128)S(1)}, u32[]{:S(2)}, u32[]{:S(2)}) collective-permute-start(f32[32,2048]{1,0:T(8,128)S(1)} %get-tuple-element.19), channel_id=1, source_target_pairs={{0,1},{1,0},{2,3},{3,2},{4,5},{5,4},{6,7},{7,6},{8,9},{9,8},{10,11... | collective-permute-start | bytes 786440 | tf_op jit(solution)/shard_map/ppermute | solution.py:267
  63.2 17.9 %all-to-all-start.2 = ((f32[16,1,1152]{2,1,0:T(1,128)}), f32[16,1,1152]{2,1,0:T(1,128)S(1)}, u32[]{:S(2)}, u32[]{:S(2)}) async-start(f32[16,1,1152]{2,1,0:T(1,128)} %get-tuple-element.17), calls=%async_computation.2 | async-start | bytes 147456 | tf_op jit(solution)/shard_map/all_to_all | solution.py:325
  69.3 9.2 %collective-permute-start.2 = (s16[32,2048]{1,0:T(8,128)(2,1)S(1)}, s16[32,2048]{1,0:T(8,128)(2,1)S(1)}, u32[]{:S(2)}, u32[]{:S(2)}) collective-permute-start(s16[32,2048]{1,0:T(8,128)(2,1)S(1)} %get-tuple-element.18), channel_id=1, source_target_pairs={{0,15},{1,2},{2,1},{3,4},{4,3},{5,6},{6,5},{7,8},{8,7},{9,10},{10,... | collective-permute-start | bytes 393224 | tf_op jit(solution)/shard_map/ppermute | solution.py:272

commit v6 on v5

--- a/solution.py
+++ b/solution.py
@@ -21,6 +21,8 @@
 INIT_SCALE = 32000.0 / 0.9
 
 HALO = 8
+KAPPA = time_step / 2
+
 F32 = jnp.float32
 I16 = jnp.int16
 
@@ -86,6 +88,16 @@
     second_ref[...] = to_i16(jnp.concatenate(second, axis=0))
 
 
+def shares(ahead):
+    falling = jnp.minimum(ahead, 0.0)
+    low = (time_step * viscosity) * ahead - falling * falling
+    return low, ahead * ahead + low
+
+
+def flux(drift, m, beyond):
+    return (jnp.maximum(drift, 0.0) + KAPPA * viscosity) * (m - beyond) + drift * beyond
+
+
 def backward_kernel(
     blocks, steps, w_ref, c_ref, terminal_ref, init_ref, first_ref, second_ref, u_ref, first_edge_ref, second_edge_ref, sums_ref
 ):
@@ -95,8 +107,8 @@
     own_weights = w_ref[pl.ds(own, 1), :].astype(F32)
     total = jnp.sum(own_weights, axis=1, keepdims=True)
     size = jnp.maximum(jnp.sum(jnp.abs(own_weights), axis=1, keepdims=True), 1.0)
-    slope = size * (DENSITY_HALF / (LEVELS * pops))
-    offset = total * (DENSITY_MID / pops)
+    slope = size * (KAPPA * time_step * DENSITY_HALF / (LEVELS * pops))
+    offset = total * (KAPPA * time_step * DENSITY_MID / pops)
     wide = c_ref[...].astype(F32)
     even = is_even()
     first = first_ref[...].astype(F32)
@@ -124,9 +136,9 @@
     last = HALO // 2
     u = jnp.concatenate(
         [
-            tile(above, last) * (1.0 / TERMINAL_SCALE),
-            terminal_ref[...],
-            tile(below, last) * (1.0 / TERMINAL_SCALE),
+            tile(above, last) * (KAPPA / TERMINAL_SCALE),
+            terminal_ref[...] * KAPPA,
+            tile(below, last) * (KAPPA / TERMINAL_SCALE),
         ],
         axis=0,
     )
@@ -134,18 +146,12 @@
     partial = [None] * steps
     kept = [None] * steps
     for t in reversed(range(steps)):
-        coupled = levels(t) * slope + offset
-        behind_r = u - pltpu.roll(u, 1, 0)
         ahead_r = pltpu.roll(u, high - 1, 0) - u
-        behind_c = u - pltpu.roll(u, 1, 1)
         ahead_c = pltpu.roll(u, cols - 1, 1) - u
-        lap = (ahead_r - behind_r) + (ahead_c - behind_c)
-        br = jnp.maximum(behind_r, 0.0)
-        ar = jnp.minimum(ahead_r, 0.0)
-        bc = jnp.maximum(behind_c, 0.0)
-        ac = jnp.minimum(ahead_c, 0.0)
-        ham = 0.5 * (br * br + ar * ar + bc * bc + ac * ac)
-        u = u + time_step * (viscosity * lap - ham + coupled)
+        low_r, up_r = shares(ahead_r)
+        low_c, up_c = shares(ahead_c)
+        source = levels(t) * slope + offset
+        u = (u + source) + (low_r - pltpu.roll(up_r, 1, 0)) + (low_c - pltpu.roll(up_c, 1, 1))
         u_ref[t] = u
         mine = u[HALO : 2 * HALO]
         kept[t] = mine
@@ -227,19 +233,9 @@
         u = field(t)
         down_m = pltpu.roll(m, high - 1, 0)
         right_m = pltpu.roll(m, cols - 1, 1)
-        drift_r = u - pltpu.roll(u, high - 1, 0)
-        drift_c = u - pltpu.roll(u, cols - 1, 1)
-        flux_r = (
-            jnp.maximum(drift_r, 0.0) * m
-            + jnp.minimum(drift_r, 0.0) * down_m
-            - viscosity * (down_m - m)
-        )
-        flux_c = (
-            jnp.maximum(drift_c, 0.0) * m
-            + jnp.minimum(drift_c, 0.0) * right_m
-            - viscosity * (right_m - m)
-        )
-        m = m - time_step * (
+        flux_r = flux(u - pltpu.roll(u, high - 1, 0), m, down_m)
+        flux_c = flux(u - pltpu.roll(u, cols - 1, 1), m, right_m)
+        m = m - (time_step / KAPPA) * (
             (flux_r - pltpu.roll(flux_r, 1, 0)) + (flux_c - pltpu.roll(flux_c, 1, 1))
         )
     final_ref[...] = m[HALO : 2 * HALO]
@@ -248,7 +244,7 @@
 def centre_kernel(cells, steps, u_ref, sums_ref, values_ref):
     means = jnp.sum(sums_ref[:, :, 0:128], axis=0) * (1.0 / cells)
     for t in range(steps):
-        values_ref[t] = u_ref[t, HALO : 2 * HALO, :] - means[:, t : t + 1]
+        values_ref[t] = (u_ref[t, HALO : 2 * HALO, :] - means[:, t : t + 1]) * (1.0 / KAPPA)
 
 
 def call(kernel, outs, *args):

time: 82.5 us -> 82.4 us (level)
  no operation moved by 1% of the time
where the time goes in v6:
time: 82.4 us; the launch traced here: 81.9 us
  starting transfers between devices  38.5 us (47%)
  waiting for transfers between devices  18.5 us (22%)
  blocking collectives  16.9 us (21%)
  Pallas kernels  6.54 us (8%)
    ppermute x2, starting transfers between devices, second_swap(): lax.ppermute(x, 'tile', [(i, ((i + 1 ^ 1) - 1) % peers) for i in range(pe...  17.8 us
    all_to_all x1, blocking collectives, per_device(): lax.all_to_all(levels.reshape(pops, rows, part), POP, 0, 0, tiled=True)  16.9 us
    all_to_all x1, waiting for transfers between devices, per_device(): lax.all_to_all(chunks.reshape(pops, rows, part), POP, 0, 0, tiled=True)  12 us
    all_to_all x1, starting transfers between devices, per_device(): lax.all_to_all(chunks.reshape(pops, rows, part), POP, 0, 0, tiled=True)  10.3 us
    pallas_call x6, Pallas kernels, call(): pl.pallas_call(kernel, out_shape=outs, in_specs=[spec] * len(args), out_s...  6.54 us
    ppermute x2, waiting for transfers between devices, second_swap(): lax.ppermute(x, 'tile', [(i, ((i + 1 ^ 1) - 1) % peers) for i in range(pe...  6.49 us
    all_to_all x1, starting transfers between devices, per_device(): sums = lax.all_to_all(sums, 'tile', 0, 0, tiled=True)  6.07 us
    ppermute x2, starting transfers between devices, first_swap(): return lax.ppermute(x, 'tile', [(i, i ^ 1) for i in range(peers)])  4.41 us
  transfers between devices with their start and end apart: 6, of which 3 were waited for; matrix products, arithmetic and copies ran while one was open for 0% of the time, Pallas kernels for 4%

profile of v6, /device:TPU:8, one launch (start us, length us, event | category | flops | bytes accessed | tf_op | source)
XLA Modules:
  0.0 81.9 jit_solution(1918127157315095068)
XLA Ops:
  0.6 0.0 copy-start.3
  0.6 0.0 copy-start
  0.6 0.0 copy-start.1
  0.7 10.3 %all-to-all-start = ((bf16[32,8,512]{2,1,0:T(8,128)(2,1)}), bf16[32,8,512]{2,1,0:T(8,128)(2,1)S(1)}, u32[]{:S(2)}, u32[]{:S(2)}) async-start(bf16[32,8,512]{2,1,0:T(8,128)(2,1)} %bitcast.21), calls=%async_computation | async-start | bytes 524288 | tf_op jit(solution)/shard_map/all_to_all | solution.py:281
  11.0 0.0 copy-start.2
  11.0 0.7 copy-done.2
  11.7 0.3 shard_map.59
  12.0 12.0 %all-to-all-done = bf16[32,8,512]{2,1,0:T(8,128)(2,1)S(1)} async-done(((bf16[32,8,512]{2,1,0:T(8,128)(2,1)}), bf16[32,8,512]{2,1,0:T(8,128)(2,1)S(1)}, u32[]{:S(2)}, u32[]{:S(2)}) %all-to-all-start) | async-done | bytes 262176 | tf_op jit(solution)/shard_map/all_to_all | solution.py:281
  24.0 0.2 shard_map.60
  24.2 16.9 %all_to_all.15 = s16[32,8,512]{2,1,0:T(8,128)(2,1)S(1)} all-to-all(s16[32,8,512]{2,1,0:T(8,128)(2,1)S(1)} %bitcast.15), channel_id=1, replica_groups=mesh['pop_0'=8,'pop_1'=2,'pop_2'=2,'tile'=16] {'pop_0','pop_1','pop_2'}, dimensions={0} | all-to-all | bytes 524288 | tf_op jit(solution)/shard_map/all_to_all | solution.py:294
  41.1 0.0 copy-done
  41.1 0.1 shard_map.61
  41.2 2.5 %collective-permute-start = (s16[40,2048]{1,0:T(8,128)(2,1)S(1)}, s16[40,2048]{1,0:T(8,128)(2,1)S(1)}, u32[]{:S(2)}, u32[]{:S(2)}) collective-permute-start(s16[40,2048]{1,0:T(8,128)(2,1)S(1)} %get-tuple-element.14), channel_id=1, source_target_pairs={{0,1},{1,0},{2,3},{3,2},{4,5},{5,4},{6,7},{7,6},{8,9},{9,8},{10,11... | collective-permute-start | bytes 491528 | tf_op jit(solution)/shard_map/ppermute | solution.py:263
  43.7 11.8 %collective-permute-start.1 = (s16[40,2048]{1,0:T(8,128)(2,1)S(1)}, s16[40,2048]{1,0:T(8,128)(2,1)S(1)}, u32[]{:S(2)}, u32[]{:S(2)}) collective-permute-start(s16[40,2048]{1,0:T(8,128)(2,1)S(1)} %get-tuple-element.15), channel_id=1, source_target_pairs={{0,15},{1,2},{2,1},{3,4},{4,3},{5,6},{6,5},{7,8},{8,7},{9,10},{10,... | collective-permute-start | bytes 491528 | tf_op jit(solution)/shard_map/ppermute | solution.py:268
  55.5 0.0 collective-permute-done.first_ref
  55.5 3.3 %collective-permute-done.1.second_ref = s16[40,2048]{1,0:T(8,128)(2,1)S(1)} collective-permute-done((s16[40,2048]{1,0:T(8,128)(2,1)S(1)}, s16[40,2048]{1,0:T(8,128)(2,1)S(1)}, u32[]{:S(2)}, u32[]{:S(2)}) %collective-permute-start.1) | collective-permute-done | bytes 163872 | tf_op jit(solution)/shard_map/ppermute | solution.py:268
  58.8 0.0 copy-done.3
  58.8 0.0 copy-done.1
  58.8 2.4 %shard_map.62 = (f32[8,24,2048]{2,1,0:T(8,128)S(1)}, f32[32,2048]{1,0:T(8,128)S(1)}, s16[32,2048]{1,0:T(8,128)(2,1)S(1)}, f32[16,1,1152]{2,1,0:T(1,128)}) custom-call(s32[32,32]{1,0:T(8,128)S(1)} %copy-done.3, s16[256,512]{1,0:T(8,128)(2,1)S(1)} %bitcast.13, f32[8,2048]{1,0:T(8,128)S(1)} %bitcast.17, f32[8,2048]{1,0:T(8,128)S(1)} %bitcast.18, ...), custom_call_target="tpu_custom_call" | custom-call | tf_op jit(solution)/shard_map/pallas_call | solution.py:252
  61.2 1.9 %collective-permute-start.3 = (f32[32,2048]{1,0:T(8,128)S(1)}, f32[32,2048]{1,0:T(8,128)S(1)}, u32[]{:S(2)}, u32[]{:S(2)}) collective-permute-start(f32[32,2048]{1,0:T(8,128)S(1)} %get-tuple-element.19), channel_id=1, source_target_pairs={{0,1},{1,0},{2,3},{3,2},{4,5},{5,4},{6,7},{7,6},{8,9},{9,8},{10,11... | collective-permute-start | bytes 786440 | tf_op jit(solution)/shard_map/ppermute | solution.py:263
  63.1 6.1 %all-to-all-start.2 = ((f32[16,1,1152]{2,1,0:T(1,128)}), f32[16,1,1152]{2,1,0:T(1,128)S(1)}, u32[]{:S(2)}, u32[]{:S(2)}) async-start(f32[16,1,1152]{2,1,0:T(1,128)} %get-tuple-element.17), calls=%async_computation.2 | async-start | bytes 147456 | tf_op jit(solution)/shard_map/all_to_all | solution.py:321
  69.2 5.9 %collective-permute-start.2 = (s16[32,2048]{1,0:T(8,128)(2,1)S(1)}, s16[32,2048]{1,0:T(8,128)(2,1)S(1)}, u32[]{:S(2)}, u32[]{:S(2)}) collective-permute-start(s16[32,2048]{1,0:T(8,128)(2,1)S(1)} %get-tuple-element.18), channel_id=1, source_target_pairs={{0,15},{1,2},{2,1},{3,4},{4,3},{5,6},{6,5},{7,8},{8,7},{9,10},{10,... | collective-permute-start | bytes 393224 | tf_op jit(solution)/shard_map/ppermute | solution.py:268
  75.1 3.2 %collective-permute-done.2.second_ref = s16[32,2048]{1,0:T(8,128)(2,1)S(1)} collective-permute-done((s16[32,2048]{1,0:T(8,128)(2,1)S(1)}, s16[32,2048]{1,0:T(8,128)(2,1)S(1)}, u32[]{:S(2)}, u32[]{:S(2)}) %collective-permute-start.2) | collective-permute-done | bytes 131104 | tf_op jit(solution)/shard_map/ppermute | solution.py:268
  78.4 0.0 collective-permute-done.3.first_ref
  78.4 2.6 %shard_map.63 = f32[8,2048]{1,0:T(8,128)} custom-call(f32[8,24,2048]{2,1,0:T(8,128)S(1)} %get-tuple-element.16.u_ref, f32[8,2048]{1,0:T(8,128)S(1)} %bitcast.19, s16[32,2048]{1,0:T(8,128)(2,1)S(1)} %collective-permute-done.2.second_ref, f32[32,2048]{1,0:T(8,128)S(1)} %collective-permute-done.3.first_ref), custom_call_target="tpu_custom_call" | custom-call | tf_op jit(solution)/shard_map/pallas_call | solution.py:252
  80.9 0.0 all-to-all-done.2.sums_ref
  81.0 0.9 %shard_map.64 = f32[8,8,2048]{2,1,0:T(8,128)} custom-call(f32[8,24,2048]{2,1,0:T(8,128)S(1)} %get-tuple-element.16.u_ref, f32[16,1,1152]{2,1,0:T(1,128)S(1)} %all-to-all-done.2.sums_ref), custom_call_target="tpu_custom_call" | custom-call | tf_op jit(solution)/shard_map/pallas_call | solution.py:252
Async XLA Ops:
  0.6 58.2 %copy-start.3 = (s32[32,32]{1,0:T(8,128)S(1)}, s32[32,32]{1,0:T(8,128)}, u32[]{:S(2)}) copy-start(s32[32,32]{1,0:T(8,128)} %w_ref.3) | copy-start | bytes 12292
  0.6 40.5 %copy-start = (f32[1,8,2048]{2,1,0:T(8,128)S(1)}, f32[1,8,2048]{2,1,0:T(8,128)}, u32[]{:S(2)}) copy-start(f32[1,8,2048]{2,1,0:T(8,128)} %param.5) | copy-start | bytes 196612
  0.6 58.2 %copy-start.1 = (f32[1,8,2048]{2,1,0:T(8,128)S(1)}, f32[1,8,2048]{2,1,0:T(8,128)}, u32[]{:S(2)}) copy-start(f32[1,8,2048]{2,1,0:T(8,128)} %param.7) | copy-start | bytes 196612
  0.7 23.3 %all-to-all-start = ((bf16[32,8,512]{2,1,0:T(8,128)(2,1)}), bf16[32,8,512]{2,1,0:T(8,128)(2,1)S(1)}, u32[]{:S(2)}, u32[]{:S(2)}) async-start(bf16[32,8,512]{2,1,0:T(8,128)(2,1)} %bitcast.21), calls=%async_computation | async-start | bytes 524288 | tf_op jit(solution)/shard_map/all_to_all | solution.py:281
  11.0 0.7 copy-start.2
  41.2 14.3 %collective-permute-start = (s16[40,2048]{1,0:T(8,128)(2,1)S(1)}, s16[40,2048]{1,0:T(8,128)(2,1)S(1)}, u32[]{:S(2)}, u32[]{:S(2)}) collective-permute-start(s16[40,2048]{1,0:T(8,128)(2,1)S(1)} %get-tuple-element.14), channel_id=1, source_target_pairs={{0,1},{1,0},{2,3},{3,2},{4,5},{5,4},{6,7},{7,6},{8,9},{9,8},{10,11... | collective-permute-start | bytes 491528 | tf_op jit(solution)/shard_map/ppermute | solution.py:263
  43.7 15.1 %collective-permute-start.1 = (s16[40,2048]{1,0:T(8,128)(2,1)S(1)}, s16[40,2048]{1,0:T(8,128)(2,1)S(1)}, u32[]{:S(2)}, u32[]{:S(2)}) collective-permute-start(s16[40,2048]{1,0:T(8,128)(2,1)S(1)} %get-tuple-element.15), channel_id=1, source_target_pairs={{0,15},{1,2},{2,1},{3,4},{4,3},{5,6},{6,5},{7,8},{8,7},{9,10},{10,... | collective-permute-start | bytes 491528 | tf_op jit(solution)/shard_map/ppermute | solution.py:268
  61.2 17.2 %collective-permute-start.3 = (f32[32,2048]{1,0:T(8,128)S(1)}, f32[32,2048]{1,0:T(8,128)S(1)}, u32[]{:S(2)}, u32[]{:S(2)}) collective-permute-start(f32[32,2048]{1,0:T(8,128)S(1)} %get-tuple-element.19), channel_id=1, source_target_pairs={{0,1},{1,0},{2,3},{3,2},{4,5},{5,4},{6,7},{7,6},{8,9},{9,8},{10,11... | collective-permute-start | bytes 786440 | tf_op jit(solution)/shard_map/ppermute | solution.py:263
  63.1 17.8 %all-to-all-start.2 = ((f32[16,1,1152]{2,1,0:T(1,128)}), f32[16,1,1152]{2,1,0:T(1,128)S(1)}, u32[]{:S(2)}, u32[]{:S(2)}) async-start(f32[16,1,1152]{2,1,0:T(1,128)} %get-tuple-element.17), calls=%async_computation.2 | async-start | bytes 147456 | tf_op jit(solution)/shard_map/all_to_all | solution.py:321
  69.2 9.2 %collective-permute-start.2 = (s16[32,2048]{1,0:T(8,128)(2,1)S(1)}, s16[32,2048]{1,0:T(8,128)(2,1)S(1)}, u32[]{:S(2)}, u32[]{:S(2)}) collective-permute-start(s16[32,2048]{1,0:T(8,128)(2,1)S(1)} %get-tuple-element.18), channel_id=1, source_target_pairs={{0,15},{1,2},{2,1},{3,4},{4,3},{5,6},{6,5},{7,8},{8,7},{9,10},{10,... | collective-permute-start | bytes 393224 | tf_op jit(solution)/shard_map/ppermute | solution.py:268

commit v7 on v6

--- a/solution.py
+++ b/solution.py
@@ -199,7 +199,7 @@
 
 
 def forward_kernel(
-    steps, u_ref, init_ref, second_ref, first_ref, final_ref
+    cells, steps, u_ref, init_ref, second_ref, first_ref, sums_ref, values_ref, final_ref
 ):
     cols = init_ref.shape[1]
     row = lax.broadcasted_iota(jnp.int32, (HALO, cols), 0)
@@ -229,7 +229,9 @@
             [side(above, u[0:8]), u[8:16], side(below, u[16:24])], axis=0
         )
 
+    means = jnp.sum(sums_ref[:, :, 0:128], axis=0) * (1.0 / cells)
     for t in range(steps):
+        values_ref[t] = (u_ref[t, HALO : 2 * HALO, :] - means[:, t : t + 1]) * (1.0 / KAPPA)
         u = field(t)
         down_m = pltpu.roll(m, high - 1, 0)
         right_m = pltpu.roll(m, cols - 1, 1)
@@ -239,12 +241,6 @@
             (flux_r - pltpu.roll(flux_r, 1, 0)) + (flux_c - pltpu.roll(flux_c, 1, 1))
         )
     final_ref[...] = m[HALO : 2 * HALO]
-
-
-def centre_kernel(cells, steps, u_ref, sums_ref, values_ref):
-    means = jnp.sum(sums_ref[:, :, 0:128], axis=0) * (1.0 / cells)
-    for t in range(steps):
-        values_ref[t] = (u_ref[t, HALO : 2 * HALO, :] - means[:, t : t + 1]) * (1.0 / KAPPA)
 
 
 def call(kernel, outs, *args):
@@ -319,19 +315,13 @@
     first = first_swap(first)
     second = second_swap(second)
     sums = lax.all_to_all(sums, "tile", 0, 0, tiled=True)
-    final = call(
-        functools.partial(forward_kernel, steps),
-        struct((rows, cols), F32),
+    values, final = call(
+        functools.partial(forward_kernel, float(tiles * rows * cols), steps),
+        (struct((steps, rows, cols), F32), struct((rows, cols), F32)),
         fields,
         init,
         second,
         first,
-    )
-    sums, final = lax.optimization_barrier((sums, final))
-    values = call(
-        functools.partial(centre_kernel, float(tiles * rows * cols), steps),
-        struct((steps, rows, cols), F32),
-        fields,
         sums,
     )
     return values[None], final[None]

time: 82.4 us -> 81.6 us (level)
    pallas_call x6 -> x5, Pallas kernels: 6.54 us -> 5.79 us  [call(): pl.pallas_call(kernel, out_shape=outs, in_specs=[spec] * len(args), out_s...]
  transfers between devices with their start and end apart: 6 -> 6, of which waited for: 3 -> 3; matrix products, arithmetic and copies ran while one was open for 0% -> 0% of each run, Pallas kernels for 4% -> 0%
where the time goes in v7:
time: 81.6 us; the launch traced here: 81.1 us
  starting transfers between devices  38.5 us (47%)
  waiting for transfers between devices  18.5 us (23%)
  blocking collectives  16.9 us (21%)
  Pallas kernels  5.79 us (7%)
    ppermute x2, starting transfers between devices, second_swap(): lax.ppermute(x, 'tile', [(i, ((i + 1 ^ 1) - 1) % peers) for i in range(pe...  17.8 us
    all_to_all x1, blocking collectives, per_device(): lax.all_to_all(levels.reshape(pops, rows, part), POP, 0, 0, tiled=True)  16.9 us
    all_to_all x1, waiting for transfers between devices, per_device(): lax.all_to_all(chunks.reshape(pops, rows, part), POP, 0, 0, tiled=True)  12 us
    all_to_all x1, starting transfers between devices, per_device(): lax.all_to_all(chunks.reshape(pops, rows, part), POP, 0, 0, tiled=True)  10.3 us
    ppermute x2, waiting for transfers between devices, second_swap(): lax.ppermute(x, 'tile', [(i, ((i + 1 ^ 1) - 1) % peers) for i in range(pe...  6.49 us
    all_to_all x1, starting transfers between devices, per_device(): sums = lax.all_to_all(sums, 'tile', 0, 0, tiled=True)  6.07 us
    pallas_call x5, Pallas kernels, call(): pl.pallas_call(kernel, out_shape=outs, in_specs=[spec] * len(args), out_s...  5.79 us
    ppermute x2, starting transfers between devices, first_swap(): return lax.ppermute(x, 'tile', [(i, i ^ 1) for i in range(peers)])  4.41 us
  transfers between devices with their start and end apart: 6, of which 3 were waited for; matrix products, arithmetic and copies ran while one was open for 0% of the time, Pallas kernels for 0%

profile of v7, /device:TPU:8, one launch (start us, length us, event | category | flops | bytes accessed | tf_op | source)
XLA Modules:
  0.0 81.1 jit_solution(16688159339562651137)
XLA Ops:
  0.6 0.0 copy-start.3
  0.6 0.0 copy-start
  0.6 0.0 copy-start.1
  0.7 10.3 %all-to-all-start = ((bf16[32,8,512]{2,1,0:T(8,128)(2,1)}), bf16[32,8,512]{2,1,0:T(8,128)(2,1)S(1)}, u32[]{:S(2)}, u32[]{:S(2)}) async-start(bf16[32,8,512]{2,1,0:T(8,128)(2,1)} %bitcast.20), calls=%async_computation | async-start | bytes 524288 | tf_op jit(solution)/shard_map/all_to_all | solution.py:277
  11.0 0.0 copy-start.2
  11.0 0.7 copy-done.2
  11.7 0.3 shard_map.59
  12.0 12.0 %all-to-all-done = bf16[32,8,512]{2,1,0:T(8,128)(2,1)S(1)} async-done(((bf16[32,8,512]{2,1,0:T(8,128)(2,1)}), bf16[32,8,512]{2,1,0:T(8,128)(2,1)S(1)}, u32[]{:S(2)}, u32[]{:S(2)}) %all-to-all-start) | async-done | bytes 262176 | tf_op jit(solution)/shard_map/all_to_all | solution.py:277
  24.0 0.2 shard_map.60
  24.2 16.9 %all_to_all.15 = s16[32,8,512]{2,1,0:T(8,128)(2,1)S(1)} all-to-all(s16[32,8,512]{2,1,0:T(8,128)(2,1)S(1)} %bitcast.15), channel_id=1, replica_groups=mesh['pop_0'=8,'pop_1'=2,'pop_2'=2,'tile'=16] {'pop_0','pop_1','pop_2'}, dimensions={0} | all-to-all | bytes 524288 | tf_op jit(solution)/shard_map/all_to_all | solution.py:290
  41.1 0.0 copy-done
  41.1 0.1 shard_map.61
  41.2 2.5 %collective-permute-start = (s16[40,2048]{1,0:T(8,128)(2,1)S(1)}, s16[40,2048]{1,0:T(8,128)(2,1)S(1)}, u32[]{:S(2)}, u32[]{:S(2)}) collective-permute-start(s16[40,2048]{1,0:T(8,128)(2,1)S(1)} %get-tuple-element.14), channel_id=1, source_target_pairs={{0,1},{1,0},{2,3},{3,2},{4,5},{5,4},{6,7},{7,6},{8,9},{9,8},{10,11... | collective-permute-start | bytes 491528 | tf_op jit(solution)/shard_map/ppermute | solution.py:259
  43.7 11.8 %collective-permute-start.1 = (s16[40,2048]{1,0:T(8,128)(2,1)S(1)}, s16[40,2048]{1,0:T(8,128)(2,1)S(1)}, u32[]{:S(2)}, u32[]{:S(2)}) collective-permute-start(s16[40,2048]{1,0:T(8,128)(2,1)S(1)} %get-tuple-element.15), channel_id=1, source_target_pairs={{0,15},{1,2},{2,1},{3,4},{4,3},{5,6},{6,5},{7,8},{8,7},{9,10},{10,... | collective-permute-start | bytes 491528 | tf_op jit(solution)/shard_map/ppermute | solution.py:264
  55.5 0.0 collective-permute-done.first_ref
  55.5 3.3 %collective-permute-done.1.second_ref = s16[40,2048]{1,0:T(8,128)(2,1)S(1)} collective-permute-done((s16[40,2048]{1,0:T(8,128)(2,1)S(1)}, s16[40,2048]{1,0:T(8,128)(2,1)S(1)}, u32[]{:S(2)}, u32[]{:S(2)}) %collective-permute-start.1) | collective-permute-done | bytes 163872 | tf_op jit(solution)/shard_map/ppermute | solution.py:264
  58.8 0.0 copy-done.3
  58.8 0.0 copy-done.1
  58.8 2.4 %shard_map.62 = (f32[8,24,2048]{2,1,0:T(8,128)S(1)}, f32[32,2048]{1,0:T(8,128)S(1)}, s16[32,2048]{1,0:T(8,128)(2,1)S(1)}, f32[16,1,1152]{2,1,0:T(1,128)}) custom-call(s32[32,32]{1,0:T(8,128)S(1)} %copy-done.3, s16[256,512]{1,0:T(8,128)(2,1)S(1)} %bitcast.13, f32[8,2048]{1,0:T(8,128)S(1)} %bitcast.17, f32[8,2048]{1,0:T(8,128)S(1)} %bitcast.18, ...), custom_call_target="tpu_custom_call" | custom-call | tf_op jit(solution)/shard_map/pallas_call | solution.py:248
  61.2 1.9 %collective-permute-start.3 = (f32[32,2048]{1,0:T(8,128)S(1)}, f32[32,2048]{1,0:T(8,128)S(1)}, u32[]{:S(2)}, u32[]{:S(2)}) collective-permute-start(f32[32,2048]{1,0:T(8,128)S(1)} %get-tuple-element.18), channel_id=1, source_target_pairs={{0,1},{1,0},{2,3},{3,2},{4,5},{5,4},{6,7},{7,6},{8,9},{9,8},{10,11... | collective-permute-start | bytes 786440 | tf_op jit(solution)/shard_map/ppermute | solution.py:259
  63.1 6.1 %all-to-all-start.2 = ((f32[16,1,1152]{2,1,0:T(1,128)}), f32[16,1,1152]{2,1,0:T(1,128)S(1)}, u32[]{:S(2)}, u32[]{:S(2)}) async-start(f32[16,1,1152]{2,1,0:T(1,128)} %get-tuple-element.19), calls=%async_computation.2 | async-start | bytes 147456 | tf_op jit(solution)/shard_map/all_to_all | solution.py:317
  69.2 5.9 %collective-permute-start.2 = (s16[32,2048]{1,0:T(8,128)(2,1)S(1)}, s16[32,2048]{1,0:T(8,128)(2,1)S(1)}, u32[]{:S(2)}, u32[]{:S(2)}) collective-permute-start(s16[32,2048]{1,0:T(8,128)(2,1)S(1)} %get-tuple-element.17), channel_id=1, source_target_pairs={{0,15},{1,2},{2,1},{3,4},{4,3},{5,6},{6,5},{7,8},{8,7},{9,10},{10,... | collective-permute-start | bytes 393224 | tf_op jit(solution)/shard_map/ppermute | solution.py:264
  75.1 3.2 %collective-permute-done.2.second_ref = s16[32,2048]{1,0:T(8,128)(2,1)S(1)} collective-permute-done((s16[32,2048]{1,0:T(8,128)(2,1)S(1)}, s16[32,2048]{1,0:T(8,128)(2,1)S(1)}, u32[]{:S(2)}, u32[]{:S(2)}) %collective-permute-start.2) | collective-permute-done | bytes 131104 | tf_op jit(solution)/shard_map/ppermute | solution.py:264
  78.4 0.0 all-to-all-done.2.sums_ref
  78.4 0.0 collective-permute-done.3.first_ref
  78.4 2.8 %shard_map.63 = (f32[8,8,2048]{2,1,0:T(8,128)}, f32[8,2048]{1,0:T(8,128)}) custom-call(f32[8,24,2048]{2,1,0:T(8,128)S(1)} %get-tuple-element.16.u_ref, f32[8,2048]{1,0:T(8,128)S(1)} %bitcast.19, s16[32,2048]{1,0:T(8,128)(2,1)S(1)} %collective-permute-done.2.second_ref, f32[32,2048]{1,0:T(8,128)S(1)} %collective-permute-done.3.first_ref, ...), custom_call_target="tpu_custom_call" | custom-call | tf_op jit(solution)/shard_map/pallas_call | solution.py:248
Async XLA Ops:
  0.6 58.2 %copy-start.3 = (s32[32,32]{1,0:T(8,128)S(1)}, s32[32,32]{1,0:T(8,128)}, u32[]{:S(2)}) copy-start(s32[32,32]{1,0:T(8,128)} %w_ref.3) | copy-start | bytes 12292
  0.6 40.5 %copy-start = (f32[1,8,2048]{2,1,0:T(8,128)S(1)}, f32[1,8,2048]{2,1,0:T(8,128)}, u32[]{:S(2)}) copy-start(f32[1,8,2048]{2,1,0:T(8,128)} %param.5) | copy-start | bytes 196612
  0.6 58.2 %copy-start.1 = (f32[1,8,2048]{2,1,0:T(8,128)S(1)}, f32[1,8,2048]{2,1,0:T(8,128)}, u32[]{:S(2)}) copy-start(f32[1,8,2048]{2,1,0:T(8,128)} %param.7) | copy-start | bytes 196612
  0.7 23.3 %all-to-all-start = ((bf16[32,8,512]{2,1,0:T(8,128)(2,1)}), bf16[32,8,512]{2,1,0:T(8,128)(2,1)S(1)}, u32[]{:S(2)}, u32[]{:S(2)}) async-start(bf16[32,8,512]{2,1,0:T(8,128)(2,1)} %bitcast.20), calls=%async_computation | async-start | bytes 524288 | tf_op jit(solution)/shard_map/all_to_all | solution.py:277
  11.0 0.7 copy-start.2
  41.2 14.3 %collective-permute-start = (s16[40,2048]{1,0:T(8,128)(2,1)S(1)}, s16[40,2048]{1,0:T(8,128)(2,1)S(1)}, u32[]{:S(2)}, u32[]{:S(2)}) collective-permute-start(s16[40,2048]{1,0:T(8,128)(2,1)S(1)} %get-tuple-element.14), channel_id=1, source_target_pairs={{0,1},{1,0},{2,3},{3,2},{4,5},{5,4},{6,7},{7,6},{8,9},{9,8},{10,11... | collective-permute-start | bytes 491528 | tf_op jit(solution)/shard_map/ppermute | solution.py:259
  43.7 15.1 %collective-permute-start.1 = (s16[40,2048]{1,0:T(8,128)(2,1)S(1)}, s16[40,2048]{1,0:T(8,128)(2,1)S(1)}, u32[]{:S(2)}, u32[]{:S(2)}) collective-permute-start(s16[40,2048]{1,0:T(8,128)(2,1)S(1)} %get-tuple-element.15), channel_id=1, source_target_pairs={{0,15},{1,2},{2,1},{3,4},{4,3},{5,6},{6,5},{7,8},{8,7},{9,10},{10,... | collective-permute-start | bytes 491528 | tf_op jit(solution)/shard_map/ppermute | solution.py:264
  61.2 17.2 %collective-permute-start.3 = (f32[32,2048]{1,0:T(8,128)S(1)}, f32[32,2048]{1,0:T(8,128)S(1)}, u32[]{:S(2)}, u32[]{:S(2)}) collective-permute-start(f32[32,2048]{1,0:T(8,128)S(1)} %get-tuple-element.18), channel_id=1, source_target_pairs={{0,1},{1,0},{2,3},{3,2},{4,5},{5,4},{6,7},{7,6},{8,9},{9,8},{10,11... | collective-permute-start | bytes 786440 | tf_op jit(solution)/shard_map/ppermute | solution.py:259
  63.1 15.2 %all-to-all-start.2 = ((f32[16,1,1152]{2,1,0:T(1,128)}), f32[16,1,1152]{2,1,0:T(1,128)S(1)}, u32[]{:S(2)}, u32[]{:S(2)}) async-start(f32[16,1,1152]{2,1,0:T(1,128)} %get-tuple-element.19), calls=%async_computation.2 | async-start | bytes 147456 | tf_op jit(solution)/shard_map/all_to_all | solution.py:317
  69.2 9.2 %collective-permute-start.2 = (s16[32,2048]{1,0:T(8,128)(2,1)S(1)}, s16[32,2048]{1,0:T(8,128)(2,1)S(1)}, u32[]{:S(2)}, u32[]{:S(2)}) collective-permute-start(s16[32,2048]{1,0:T(8,128)(2,1)S(1)} %get-tuple-element.17), channel_id=1, source_target_pairs={{0,15},{1,2},{2,1},{3,4},{4,3},{5,6},{6,5},{7,8},{8,7},{9,10},{10,... | collective-permute-start | bytes 393224 | tf_op jit(solution)/shard_map/ppermute | solution.py:264

commit v8 on v7

--- a/solution.py
+++ b/solution.py
@@ -82,10 +82,20 @@
         up.append(jnp.where(row < HALO - t, c[HALO - t], pltpu.roll(c[t], HALO - t, 0)))
     even = is_even()
     edge = terminal_ref[...] * TERMINAL_SCALE
-    first = [jnp.where(even, d, u) for d, u in zip(down, up)] + [c[HALO // 2], edge]
-    second = [jnp.where(even, u, d) for d, u in zip(down, up)] + [c[HALO // 2], edge]
-    first_ref[...] = to_i16(jnp.concatenate(first, axis=0))
-    second_ref[...] = to_i16(jnp.concatenate(second, axis=0))
+    half = edge.shape[1] // 2
+    left, right = c[HALO // 2][:, :half], pltpu.roll(c[HALO // 2][:, half:], HALO // 2, 0)
+    upper = row[:, :half] < HALO // 2
+    down_mid = jnp.where(upper, right, left)
+    up_mid = jnp.where(upper, left, right)
+
+    def stacked(tiles, mid):
+        parts = [x[:, at : at + half] for x in tiles + [edge] for at in (0, half)]
+        return to_i16(jnp.concatenate(parts + [mid], axis=0))
+
+    first = [jnp.where(even, d, u) for d, u in zip(down, up)]
+    second = [jnp.where(even, u, d) for d, u in zip(down, up)]
+    first_ref[...] = stacked(first, jnp.where(even, down_mid, up_mid))
+    second_ref[...] = stacked(second, jnp.where(even, up_mid, down_mid))
 
 
 def shares(ahead):
@@ -117,23 +127,28 @@
     below = jnp.where(even, first, second)
 
     def tile(x, k):
-        return x[k * HALO : (k + 1) * HALO]
+        at = 2 * k * HALO
+        return jnp.concatenate([x[at : at + HALO], x[at + HALO : at + 2 * HALO]], axis=1)
+
+    def middle(x):
+        shared = x[HALO * HALO :]
+        return jnp.concatenate([shared, pltpu.roll(shared, HALO // 2, 0)], axis=1)
 
     def levels(t):
         if t == 0:
             top = bottom = jnp.zeros((HALO, cols), F32)
-        elif t <= HALO // 2:
-            top = tile(above, t - 1)
-            bottom = tile(below, t - 1)
-            if t < HALO // 2:
-                top = pltpu.roll(top, HALO - t, 0)
-                bottom = pltpu.roll(bottom, t, 0)
+        elif t < HALO // 2:
+            top = pltpu.roll(tile(above, t - 1), HALO - t, 0)
+            bottom = pltpu.roll(tile(below, t - 1), t, 0)
+        elif t == HALO // 2:
+            top = middle(above)
+            bottom = middle(below)
         else:
             top = tile(above, HALO - t - 1)
             bottom = tile(below, HALO - t - 1)
         return jnp.concatenate([top, rows_of_step(wide, t, blocks), bottom], axis=0)
 
-    last = HALO // 2
+    last = HALO // 2 - 1
     u = jnp.concatenate(
         [
             tile(above, last) * (KAPPA / TERMINAL_SCALE),
@@ -291,7 +306,7 @@
     levels = levels.reshape(pops * rows, part)
     first, second = call(
         functools.partial(pack_kernel, blocks, steps),
-        (struct((40, cols), I16), struct((40, cols), I16)),
+        (struct((72, cols // 2), I16), struct((72, cols // 2), I16)),
         levels,
         terminal,
     )

time: 81.6 us -> 81.5 us (level)
  no operation moved by 1% of the time
where the time goes in v8:
time: 81.5 us; the launch traced here: 81 us
  starting transfers between devices  38.5 us (47%)
  waiting for transfers between devices  18.3 us (22%)
  blocking collectives  16.9 us (21%)
  Pallas kernels  5.79 us (7%)
    ppermute x2, starting transfers between devices, second_swap(): lax.ppermute(x, 'tile', [(i, ((i + 1 ^ 1) - 1) % peers) for i in range(pe...  17.8 us
    all_to_all x1, blocking collectives, per_device(): lax.all_to_all(levels.reshape(pops, rows, part), POP, 0, 0, tiled=True)  16.9 us
    all_to_all x1, waiting for transfers between devices, per_device(): lax.all_to_all(chunks.reshape(pops, rows, part), POP, 0, 0, tiled=True)  12 us
    all_to_all x1, starting transfers between devices, per_device(): lax.all_to_all(chunks.reshape(pops, rows, part), POP, 0, 0, tiled=True)  10.3 us
    ppermute x2, waiting for transfers between devices, second_swap(): lax.ppermute(x, 'tile', [(i, ((i + 1 ^ 1) - 1) % peers) for i in range(pe...  6.32 us
    all_to_all x1, starting transfers between devices, per_device(): sums = lax.all_to_all(sums, 'tile', 0, 0, tiled=True)  6.07 us
    pallas_call x5, Pallas kernels, call(): pl.pallas_call(kernel, out_shape=outs, in_specs=[spec] * len(args), out_s...  5.79 us
    ppermute x2, starting transfers between devices, first_swap(): return lax.ppermute(x, 'tile', [(i, i ^ 1) for i in range(peers)])  4.41 us
  transfers between devices with their start and end apart: 6, of which 3 were waited for; matrix products, arithmetic and copies ran while one was open for 0% of the time, Pallas kernels for 0%

profile of v8, /device:TPU:8, one launch (start us, length us, event | category | flops | bytes accessed | tf_op | source)
XLA Modules:
  0.0 81.0 jit_solution(1709008323124377661)
XLA Ops:
  0.6 0.0 copy-start.3
  0.6 0.0 copy-start
  0.6 0.0 copy-start.1
  0.7 10.3 %all-to-all-start = ((bf16[32,8,512]{2,1,0:T(8,128)(2,1)}), bf16[32,8,512]{2,1,0:T(8,128)(2,1)S(1)}, u32[]{:S(2)}, u32[]{:S(2)}) async-start(bf16[32,8,512]{2,1,0:T(8,128)(2,1)} %bitcast.20), calls=%async_computation | async-start | bytes 524288 | tf_op jit(solution)/shard_map/all_to_all | solution.py:292
  11.0 0.0 copy-start.2
  11.0 0.7 copy-done.2
  11.7 0.3 shard_map.59
  12.0 12.0 %all-to-all-done = bf16[32,8,512]{2,1,0:T(8,128)(2,1)S(1)} async-done(((bf16[32,8,512]{2,1,0:T(8,128)(2,1)}), bf16[32,8,512]{2,1,0:T(8,128)(2,1)S(1)}, u32[]{:S(2)}, u32[]{:S(2)}) %all-to-all-start) | async-done | bytes 262176 | tf_op jit(solution)/shard_map/all_to_all | solution.py:292
  24.0 0.2 shard_map.60
  24.2 16.9 %all_to_all.15 = s16[32,8,512]{2,1,0:T(8,128)(2,1)S(1)} all-to-all(s16[32,8,512]{2,1,0:T(8,128)(2,1)S(1)} %bitcast.15), channel_id=1, replica_groups=mesh['pop_0'=8,'pop_1'=2,'pop_2'=2,'tile'=16] {'pop_0','pop_1','pop_2'}, dimensions={0} | all-to-all | bytes 524288 | tf_op jit(solution)/shard_map/all_to_all | solution.py:305
  41.1 0.0 copy-done
  41.1 0.1 shard_map.61
  41.2 2.5 %collective-permute-start = (s16[72,1024]{1,0:T(8,128)(2,1)S(1)}, s16[72,1024]{1,0:T(8,128)(2,1)S(1)}, u32[]{:S(2)}, u32[]{:S(2)}) collective-permute-start(s16[72,1024]{1,0:T(8,128)(2,1)S(1)} %get-tuple-element.14), channel_id=1, source_target_pairs={{0,1},{1,0},{2,3},{3,2},{4,5},{5,4},{6,7},{7,6},{8,9},{9,8},{10,11... | collective-permute-start | bytes 442376 | tf_op jit(solution)/shard_map/ppermute | solution.py:274
  43.7 11.8 %collective-permute-start.1 = (s16[72,1024]{1,0:T(8,128)(2,1)S(1)}, s16[72,1024]{1,0:T(8,128)(2,1)S(1)}, u32[]{:S(2)}, u32[]{:S(2)}) collective-permute-start(s16[72,1024]{1,0:T(8,128)(2,1)S(1)} %get-tuple-element.15), channel_id=1, source_target_pairs={{0,15},{1,2},{2,1},{3,4},{4,3},{5,6},{6,5},{7,8},{8,7},{9,10},{10,... | collective-permute-start | bytes 442376 | tf_op jit(solution)/shard_map/ppermute | solution.py:279
  55.5 0.0 collective-permute-done.first_ref
  55.6 3.1 %collective-permute-done.1.second_ref = s16[72,1024]{1,0:T(8,128)(2,1)S(1)} collective-permute-done((s16[72,1024]{1,0:T(8,128)(2,1)S(1)}, s16[72,1024]{1,0:T(8,128)(2,1)S(1)}, u32[]{:S(2)}, u32[]{:S(2)}) %collective-permute-start.1) | collective-permute-done | bytes 147488 | tf_op jit(solution)/shard_map/ppermute | solution.py:279
  58.6 0.0 copy-done.3
  58.7 0.0 copy-done.1
  58.7 2.4 %shard_map.62 = (f32[8,24,2048]{2,1,0:T(8,128)S(1)}, f32[32,2048]{1,0:T(8,128)S(1)}, s16[32,2048]{1,0:T(8,128)(2,1)S(1)}, f32[16,1,1152]{2,1,0:T(1,128)}) custom-call(s32[32,32]{1,0:T(8,128)S(1)} %copy-done.3, s16[256,512]{1,0:T(8,128)(2,1)S(1)} %bitcast.13, f32[8,2048]{1,0:T(8,128)S(1)} %bitcast.17, f32[8,2048]{1,0:T(8,128)S(1)} %bitcast.18, ...), custom_call_target="tpu_custom_call" | custom-call | tf_op jit(solution)/shard_map/pallas_call | solution.py:263
  61.0 1.9 %collective-permute-start.3 = (f32[32,2048]{1,0:T(8,128)S(1)}, f32[32,2048]{1,0:T(8,128)S(1)}, u32[]{:S(2)}, u32[]{:S(2)}) collective-permute-start(f32[32,2048]{1,0:T(8,128)S(1)} %get-tuple-element.18), channel_id=1, source_target_pairs={{0,1},{1,0},{2,3},{3,2},{4,5},{5,4},{6,7},{7,6},{8,9},{9,8},{10,11... | collective-permute-start | bytes 786440 | tf_op jit(solution)/shard_map/ppermute | solution.py:274
  62.9 6.1 %all-to-all-start.2 = ((f32[16,1,1152]{2,1,0:T(1,128)}), f32[16,1,1152]{2,1,0:T(1,128)S(1)}, u32[]{:S(2)}, u32[]{:S(2)}) async-start(f32[16,1,1152]{2,1,0:T(1,128)} %get-tuple-element.19), calls=%async_computation.2 | async-start | bytes 147456 | tf_op jit(solution)/shard_map/all_to_all | solution.py:332
  69.0 5.9 %collective-permute-start.2 = (s16[32,2048]{1,0:T(8,128)(2,1)S(1)}, s16[32,2048]{1,0:T(8,128)(2,1)S(1)}, u32[]{:S(2)}, u32[]{:S(2)}) collective-permute-start(s16[32,2048]{1,0:T(8,128)(2,1)S(1)} %get-tuple-element.17), channel_id=1, source_target_pairs={{0,15},{1,2},{2,1},{3,4},{4,3},{5,6},{6,5},{7,8},{8,7},{9,10},{10,... | collective-permute-start | bytes 393224 | tf_op jit(solution)/shard_map/ppermute | solution.py:279
  75.0 3.2 %collective-permute-done.2.second_ref = s16[32,2048]{1,0:T(8,128)(2,1)S(1)} collective-permute-done((s16[32,2048]{1,0:T(8,128)(2,1)S(1)}, s16[32,2048]{1,0:T(8,128)(2,1)S(1)}, u32[]{:S(2)}, u32[]{:S(2)}) %collective-permute-start.2) | collective-permute-done | bytes 131104 | tf_op jit(solution)/shard_map/ppermute | solution.py:279
  78.2 0.0 all-to-all-done.2.sums_ref
  78.2 0.0 collective-permute-done.3.first_ref
  78.2 2.8 %shard_map.63 = (f32[8,8,2048]{2,1,0:T(8,128)}, f32[8,2048]{1,0:T(8,128)}) custom-call(f32[8,24,2048]{2,1,0:T(8,128)S(1)} %get-tuple-element.16.u_ref, f32[8,2048]{1,0:T(8,128)S(1)} %bitcast.19, s16[32,2048]{1,0:T(8,128)(2,1)S(1)} %collective-permute-done.2.second_ref, f32[32,2048]{1,0:T(8,128)S(1)} %collective-permute-done.3.first_ref, ...), custom_call_target="tpu_custom_call" | custom-call | tf_op jit(solution)/shard_map/pallas_call | solution.py:263
Async XLA Ops:
  0.6 58.0 %copy-start.3 = (s32[32,32]{1,0:T(8,128)S(1)}, s32[32,32]{1,0:T(8,128)}, u32[]{:S(2)}) copy-start(s32[32,32]{1,0:T(8,128)} %w_ref.3) | copy-start | bytes 12292
  0.6 40.5 %copy-start = (f32[1,8,2048]{2,1,0:T(8,128)S(1)}, f32[1,8,2048]{2,1,0:T(8,128)}, u32[]{:S(2)}) copy-start(f32[1,8,2048]{2,1,0:T(8,128)} %param.5) | copy-start | bytes 196612
  0.6 58.0 %copy-start.1 = (f32[1,8,2048]{2,1,0:T(8,128)S(1)}, f32[1,8,2048]{2,1,0:T(8,128)}, u32[]{:S(2)}) copy-start(f32[1,8,2048]{2,1,0:T(8,128)} %param.7) | copy-start | bytes 196612
  0.7 23.3 %all-to-all-start = ((bf16[32,8,512]{2,1,0:T(8,128)(2,1)}), bf16[32,8,512]{2,1,0:T(8,128)(2,1)S(1)}, u32[]{:S(2)}, u32[]{:S(2)}) async-start(bf16[32,8,512]{2,1,0:T(8,128)(2,1)} %bitcast.20), calls=%async_computation | async-start | bytes 524288 | tf_op jit(solution)/shard_map/all_to_all | solution.py:292
  11.0 0.7 copy-start.2
  41.2 14.3 %collective-permute-start = (s16[72,1024]{1,0:T(8,128)(2,1)S(1)}, s16[72,1024]{1,0:T(8,128)(2,1)S(1)}, u32[]{:S(2)}, u32[]{:S(2)}) collective-permute-start(s16[72,1024]{1,0:T(8,128)(2,1)S(1)} %get-tuple-element.14), channel_id=1, source_target_pairs={{0,1},{1,0},{2,3},{3,2},{4,5},{5,4},{6,7},{7,6},{8,9},{9,8},{10,11... | collective-permute-start | bytes 442376 | tf_op jit(solution)/shard_map/ppermute | solution.py:274
  43.7 14.9 %collective-permute-start.1 = (s16[72,1024]{1,0:T(8,128)(2,1)S(1)}, s16[72,1024]{1,0:T(8,128)(2,1)S(1)}, u32[]{:S(2)}, u32[]{:S(2)}) collective-permute-start(s16[72,1024]{1,0:T(8,128)(2,1)S(1)} %get-tuple-element.15), channel_id=1, source_target_pairs={{0,15},{1,2},{2,1},{3,4},{4,3},{5,6},{6,5},{7,8},{8,7},{9,10},{10,... | collective-permute-start | bytes 442376 | tf_op jit(solution)/shard_map/ppermute | solution.py:279
  61.0 17.2 %collective-permute-start.3 = (f32[32,2048]{1,0:T(8,128)S(1)}, f32[32,2048]{1,0:T(8,128)S(1)}, u32[]{:S(2)}, u32[]{:S(2)}) collective-permute-start(f32[32,2048]{1,0:T(8,128)S(1)} %get-tuple-element.18), channel_id=1, source_target_pairs={{0,1},{1,0},{2,3},{3,2},{4,5},{5,4},{6,7},{7,6},{8,9},{9,8},{10,11... | collective-permute-start | bytes 786440 | tf_op jit(solution)/shard_map/ppermute | solution.py:274
  62.9 15.2 %all-to-all-start.2 = ((f32[16,1,1152]{2,1,0:T(1,128)}), f32[16,1,1152]{2,1,0:T(1,128)S(1)}, u32[]{:S(2)}, u32[]{:S(2)}) async-start(f32[16,1,1152]{2,1,0:T(1,128)} %get-tuple-element.19), calls=%async_computation.2 | async-start | bytes 147456 | tf_op jit(solution)/shard_map/all_to_all | solution.py:332
  69.0 9.2 %collective-permute-start.2 = (s16[32,2048]{1,0:T(8,128)(2,1)S(1)}, s16[32,2048]{1,0:T(8,128)(2,1)S(1)}, u32[]{:S(2)}, u32[]{:S(2)}) collective-permute-start(s16[32,2048]{1,0:T(8,128)(2,1)S(1)} %get-tuple-element.17), channel_id=1, source_target_pairs={{0,15},{1,2},{2,1},{3,4},{4,3},{5,6},{6,5},{7,8},{8,7},{9,10},{10,... | collective-permute-start | bytes 393224 | tf_op jit(solution)/shard_map/ppermute | solution.py:279

commit v9 on v8

--- a/solution.py
+++ b/solution.py
@@ -31,7 +31,8 @@
     return jnp.round(x).astype(jnp.int32).astype(I16)
 
 
-def spread_kernel(w_ref, kron_ref, scale_ref):
+def spread_kernel(w_ref, terminal_ref, kron_ref, scale_ref, rim_ref):
+    rim_ref[...] = to_i16(terminal_ref[...] * TERMINAL_SCALE)
     pops = w_ref.shape[0]
     rows = kron_ref.shape[0]
     per = rows // pops
@@ -71,7 +72,7 @@
     return (lax.axis_index("tile") & 1) == 0
 
 
-def pack_kernel(blocks, steps, c_ref, terminal_ref, first_ref, second_ref):
+def pack_kernel(blocks, steps, c_ref, first_ref, second_ref):
     wide = c_ref[...].astype(F32)
     c = [rows_of_step(wide, t, blocks) for t in range(steps)]
     row = lax.broadcasted_iota(jnp.int32, c[0].shape, 0)
@@ -81,15 +82,14 @@
         down.append(jnp.where(row >= t, c[HALO - t], pltpu.roll(c[t], t, 0)))
         up.append(jnp.where(row < HALO - t, c[HALO - t], pltpu.roll(c[t], HALO - t, 0)))
     even = is_even()
-    edge = terminal_ref[...] * TERMINAL_SCALE
-    half = edge.shape[1] // 2
+    half = row.shape[1] // 2
     left, right = c[HALO // 2][:, :half], pltpu.roll(c[HALO // 2][:, half:], HALO // 2, 0)
     upper = row[:, :half] < HALO // 2
     down_mid = jnp.where(upper, right, left)
     up_mid = jnp.where(upper, left, right)
 
     def stacked(tiles, mid):
-        parts = [x[:, at : at + half] for x in tiles + [edge] for at in (0, half)]
+        parts = [x[:, at : at + half] for x in tiles for at in (0, half)]
         return to_i16(jnp.concatenate(parts + [mid], axis=0))
 
     first = [jnp.where(even, d, u) for d, u in zip(down, up)]
@@ -109,7 +109,7 @@
 
 
 def backward_kernel(
-    blocks, steps, w_ref, c_ref, terminal_ref, init_ref, first_ref, second_ref, u_ref, first_edge_ref, second_edge_ref, sums_ref
+    blocks, steps, w_ref, c_ref, terminal_ref, init_ref, first_rim_ref, second_rim_ref, first_ref, second_ref, u_ref, first_edge_ref, second_edge_ref, sums_ref
 ):
     pops = w_ref.shape[0]
     cols = terminal_ref.shape[1]
@@ -131,7 +131,7 @@
         return jnp.concatenate([x[at : at + HALO], x[at + HALO : at + 2 * HALO]], axis=1)
 
     def middle(x):
-        shared = x[HALO * HALO :]
+        shared = x[HALO * (HALO - 2) :]
         return jnp.concatenate([shared, pltpu.roll(shared, HALO // 2, 0)], axis=1)
 
     def levels(t):
@@ -148,12 +148,13 @@
             bottom = tile(below, HALO - t - 1)
         return jnp.concatenate([top, rows_of_step(wide, t, blocks), bottom], axis=0)
 
-    last = HALO // 2 - 1
+    first_rim = first_rim_ref[...].astype(F32) * (KAPPA / TERMINAL_SCALE)
+    second_rim = second_rim_ref[...].astype(F32) * (KAPPA / TERMINAL_SCALE)
     u = jnp.concatenate(
         [
-            tile(above, last) * (KAPPA / TERMINAL_SCALE),
+            jnp.where(even, second_rim, first_rim),
             terminal_ref[...] * KAPPA,
-            tile(below, last) * (KAPPA / TERMINAL_SCALE),
+            jnp.where(even, first_rim, second_rim),
         ],
         axis=0,
     )
@@ -290,11 +291,19 @@
     init = density_init[0]
     chunks = density_history[0].reshape(steps, rows, blocks, part).transpose(0, 2, 1, 3)
     chunks = lax.all_to_all(chunks.reshape(pops, rows, part), POP, 0, 0, tiled=True)
-    kron, scale = call(
+    kron, scale, rim = call(
         spread_kernel,
-        (struct((pops * rows, pops * rows), jnp.bfloat16), struct((pops * rows, 128), F32)),
+        (
+            struct((pops * rows, pops * rows), jnp.bfloat16),
+            struct((pops * rows, 128), F32),
+            struct((rows, cols), I16),
+        ),
         weights,
-    )
+        terminal,
+    )
+    first_rim = first_swap(rim)
+    second_rim = second_swap(rim)
+    chunks, first_rim, second_rim = lax.optimization_barrier((chunks, first_rim, second_rim))
     levels = call(
         coupling_kernel,
         struct((pops * rows, part), I16),
@@ -306,9 +315,8 @@
     levels = levels.reshape(pops * rows, part)
     first, second = call(
         functools.partial(pack_kernel, blocks, steps),
-        (struct((72, cols // 2), I16), struct((72, cols // 2), I16)),
+        (struct((56, cols // 2), I16), struct((56, cols // 2), I16)),
         levels,
-        terminal,
     )
     second = second_swap(second)
     first = first_swap(first)
@@ -324,6 +332,8 @@
         levels,
         terminal,
         init,
+        first_rim,
+        second_rim,
         first,
         second,
     )

time: 81.5 us -> 85.2 us (1.045)
  blocking collectives: 16.9 us -> 23.2 us
  waiting for transfers between devices: 18.3 us -> 12 us
  starting transfers between devices: 38.5 us -> 41.4 us
    all_to_all x1, waiting for transfers between devices: 12 us -> 0.01 us  [per_device(): lax.all_to_all(chunks.reshape(pops, rows, part), POP, 0, 0, tiled=True)]
    all_to_all x1, blocking collectives: 16.9 us -> 23.2 us  [per_device(): lax.all_to_all(levels.reshape(pops, rows, part), POP, 0, 0, tiled=True)]
    ppermute x2 -> x3, waiting for transfers between devices: 0.01 us -> 4.7 us  [first_swap(): return lax.ppermute(x, 'tile', [(i, i ^ 1) for i in range(peers)])]
    ppermute x2 -> x3, starting transfers between devices: 17.8 us -> 20.8 us  [second_swap(): lax.ppermute(x, 'tile', [(i, ((i + 1 ^ 1) - 1) % peers) for i in range(pe...]
    all_to_all x1, starting transfers between devices: 6.07 us -> 3.71 us  [per_device(): sums = lax.all_to_all(sums, 'tile', 0, 0, tiled=True)]
    ppermute x2 -> x3, starting transfers between devices: 4.41 us -> 6.54 us  [first_swap(): return lax.ppermute(x, 'tile', [(i, i ^ 1) for i in range(peers)])]
    ppermute x2 -> x3, waiting for transfers between devices: 6.32 us -> 7.26 us  [second_swap(): lax.ppermute(x, 'tile', [(i, ((i + 1 ^ 1) - 1) % peers) for i in range(pe...]
  transfers between devices with their start and end apart: 6 -> 8, of which waited for: 3 -> 4; matrix products, arithmetic and copies ran while one was open for 0% -> 0% of each run, Pallas kernels for 0% -> 0%
where the time goes in v9:
time: 85.2 us; the launch traced here: 84.6 us
  starting transfers between devices  41.4 us (49%)
  blocking collectives  23.2 us (27%)
  waiting for transfers between devices  12 us (14%)
  Pallas kernels  5.78 us (7%)
  local copies, waits for them, and re-layouts  1.56 us (2%)
    all_to_all x1, blocking collectives, per_device(): lax.all_to_all(levels.reshape(pops, rows, part), POP, 0, 0, tiled=True)  23.2 us
    ppermute x3, starting transfers between devices, second_swap(): lax.ppermute(x, 'tile', [(i, ((i + 1 ^ 1) - 1) % peers) for i in range(pe...  20.8 us
    all_to_all x1, starting transfers between devices, per_device(): lax.all_to_all(chunks.reshape(pops, rows, part), POP, 0, 0, tiled=True)  10.3 us
    ppermute x3, waiting for transfers between devices, second_swap(): lax.ppermute(x, 'tile', [(i, ((i + 1 ^ 1) - 1) % peers) for i in range(pe...  7.26 us
    ppermute x3, starting transfers between devices, first_swap(): return lax.ppermute(x, 'tile', [(i, i ^ 1) for i in range(peers)])  6.54 us
    pallas_call x5, Pallas kernels, call(): pl.pallas_call(kernel, out_shape=outs, in_specs=[spec] * len(args), out_s...  5.78 us
    ppermute x3, waiting for transfers between devices, first_swap(): return lax.ppermute(x, 'tile', [(i, i ^ 1) for i in range(peers)])  4.7 us
    all_to_all x1, starting transfers between devices, per_device(): sums = lax.all_to_all(sums, 'tile', 0, 0, tiled=True)  3.71 us
  transfers between devices with their start and end apart: 8, of which 4 were waited for; matrix products, arithmetic and copies ran while one was open for 0% of the time, Pallas kernels for 0%

profile of v9, /device:TPU:8, one launch (start us, length us, event | category | flops | bytes accessed | tf_op | source)
XLA Modules:
  0.0 84.6 jit_solution(5884087269265134545)
XLA Ops:
  0.6 0.0 copy-start.4
  0.6 0.0 copy-start.2
  0.6 0.0 copy-start
  0.7 10.3 %all-to-all-start = ((bf16[32,8,512]{2,1,0:T(8,128)(2,1)}), bf16[32,8,512]{2,1,0:T(8,128)(2,1)S(1)}, u32[]{:S(2)}, u32[]{:S(2)}) async-start(bf16[32,8,512]{2,1,0:T(8,128)(2,1)} %bitcast.20), calls=%async_computation | async-start | bytes 524288 | tf_op jit(solution)/shard_map/all_to_all | solution.py:293
  11.0 0.0 copy-start.1
  11.0 0.8 copy-done.1
  11.8 0.0 copy-start.3
  11.8 0.7 copy-done.3
  12.5 0.3 shard_map.59
  12.8 11.0 %collective-permute-start.1 = (s16[8,2048]{1,0:T(8,128)(2,1)S(1)}, s16[8,2048]{1,0:T(8,128)(2,1)S(1)}, u32[]{:S(2)}, u32[]{:S(2)}) collective-permute-start(s16[8,2048]{1,0:T(8,128)(2,1)S(1)} %get-tuple-element.18), channel_id=1, source_target_pairs={{0,15},{1,2},{2,1},{3,4},{4,3},{5,6},{6,5},{7,8},{8,7},{9,10},{10,... | collective-permute-start | bytes 98312 | tf_op jit(solution)/shard_map/ppermute | solution.py:280
  23.8 1.9 %collective-permute-start = (s16[8,2048]{1,0:T(8,128)(2,1)S(1)}, s16[8,2048]{1,0:T(8,128)(2,1)S(1)}, u32[]{:S(2)}, u32[]{:S(2)}) collective-permute-start(s16[8,2048]{1,0:T(8,128)(2,1)S(1)} %get-tuple-element.18), channel_id=1, source_target_pairs={{0,1},{1,0},{2,3},{3,2},{4,5},{5,4},{6,7},{7,6},{8,9},{9,8},{10,11... | collective-permute-start | bytes 98312 | tf_op jit(solution)/shard_map/ppermute | solution.py:275
  25.8 0.0 collective-permute-done.1.second_rim_ref
  25.8 3.9 %collective-permute-done.first_rim_ref = s16[8,2048]{1,0:T(8,128)(2,1)S(1)} collective-permute-done((s16[8,2048]{1,0:T(8,128)(2,1)S(1)}, s16[8,2048]{1,0:T(8,128)(2,1)S(1)}, u32[]{:S(2)}, u32[]{:S(2)}) %collective-permute-start) | collective-permute-done | bytes 32800 | tf_op jit(solution)/shard_map/ppermute | solution.py:275
  29.6 0.0 all-to-all-done
  29.6 0.2 shard_map.60
  29.9 23.2 %all_to_all.15 = s16[32,8,512]{2,1,0:T(8,128)(2,1)S(1)} all-to-all(s16[32,8,512]{2,1,0:T(8,128)(2,1)S(1)} %bitcast.15), channel_id=1, replica_groups=mesh['pop_0'=8,'pop_1'=2,'pop_2'=2,'tile'=16] {'pop_0','pop_1','pop_2'}, dimensions={0} | all-to-all | bytes 524288 | tf_op jit(solution)/shard_map/all_to_all | solution.py:314
  53.1 0.1 shard_map.61
  53.2 1.9 %collective-permute-start.2 = (s16[56,1024]{1,0:T(8,128)(2,1)S(1)}, s16[56,1024]{1,0:T(8,128)(2,1)S(1)}, u32[]{:S(2)}, u32[]{:S(2)}) collective-permute-start(s16[56,1024]{1,0:T(8,128)(2,1)S(1)} %get-tuple-element.22), channel_id=1, source_target_pairs={{0,1},{1,0},{2,3},{3,2},{4,5},{5,4},{6,7},{7,6},{8,9},{9,8},{10,11... | collective-permute-start | bytes 344072 | tf_op jit(solution)/shard_map/ppermute | solution.py:275
  55.1 3.9 %collective-permute-start.3 = (s16[56,1024]{1,0:T(8,128)(2,1)S(1)}, s16[56,1024]{1,0:T(8,128)(2,1)S(1)}, u32[]{:S(2)}, u32[]{:S(2)}) collective-permute-start(s16[56,1024]{1,0:T(8,128)(2,1)S(1)} %get-tuple-element.23), channel_id=1, source_target_pairs={{0,15},{1,2},{2,1},{3,4},{4,3},{5,6},{6,5},{7,8},{8,7},{9,10},{10,... | collective-permute-start | bytes 344072 | tf_op jit(solution)/shard_map/ppermute | solution.py:280
  59.0 0.8 collective-permute-done.2.first_ref
  59.9 4.0 %collective-permute-done.3.second_ref = s16[56,1024]{1,0:T(8,128)(2,1)S(1)} collective-permute-done((s16[56,1024]{1,0:T(8,128)(2,1)S(1)}, s16[56,1024]{1,0:T(8,128)(2,1)S(1)}, u32[]{:S(2)}, u32[]{:S(2)}) %collective-permute-start.3) | collective-permute-done | bytes 114720 | tf_op jit(solution)/shard_map/ppermute | solution.py:280
  63.9 0.0 copy-done.4
  63.9 0.0 copy-done.2
  63.9 0.0 copy-done
  63.9 2.4 %shard_map.62 = (f32[8,24,2048]{2,1,0:T(8,128)S(1)}, f32[32,2048]{1,0:T(8,128)S(1)}, s16[32,2048]{1,0:T(8,128)(2,1)S(1)}, f32[16,1,1152]{2,1,0:T(1,128)}) custom-call(s32[32,32]{1,0:T(8,128)S(1)} %copy-done.4, s16[256,512]{1,0:T(8,128)(2,1)S(1)} %bitcast.13, f32[8,2048]{1,0:T(8,128)S(1)} %bitcast.19, f32[8,2048]{1,0:T(8,128)S(1)} %bitcast.16, ...), custom_call_target="tpu_custom_call" | custom-call | tf_op jit(solution)/shard_map/pallas_call | solution.py:264
  66.3 2.7 %collective-permute-start.5 = (f32[32,2048]{1,0:T(8,128)S(1)}, f32[32,2048]{1,0:T(8,128)S(1)}, u32[]{:S(2)}, u32[]{:S(2)}) collective-permute-start(f32[32,2048]{1,0:T(8,128)S(1)} %get-tuple-element.26), channel_id=1, source_target_pairs={{0,1},{1,0},{2,3},{3,2},{4,5},{5,4},{6,7},{7,6},{8,9},{9,8},{10,11... | collective-permute-start | bytes 786440 | tf_op jit(solution)/shard_map/ppermute | solution.py:275
  69.0 3.7 %all-to-all-start.2 = ((f32[16,1,1152]{2,1,0:T(1,128)}), f32[16,1,1152]{2,1,0:T(1,128)S(1)}, u32[]{:S(2)}, u32[]{:S(2)}) async-start(f32[16,1,1152]{2,1,0:T(1,128)} %get-tuple-element.27), calls=%async_computation.2 | async-start | bytes 147456 | tf_op jit(solution)/shard_map/all_to_all | solution.py:342
  72.7 5.9 %collective-permute-start.4 = (s16[32,2048]{1,0:T(8,128)(2,1)S(1)}, s16[32,2048]{1,0:T(8,128)(2,1)S(1)}, u32[]{:S(2)}, u32[]{:S(2)}) collective-permute-start(s16[32,2048]{1,0:T(8,128)(2,1)S(1)} %get-tuple-element.25), channel_id=1, source_target_pairs={{0,15},{1,2},{2,1},{3,4},{4,3},{5,6},{6,5},{7,8},{8,7},{9,10},{10,... | collective-permute-start | bytes 393224 | tf_op jit(solution)/shard_map/ppermute | solution.py:280
  78.6 3.2 %collective-permute-done.4.second_ref = s16[32,2048]{1,0:T(8,128)(2,1)S(1)} collective-permute-done((s16[32,2048]{1,0:T(8,128)(2,1)S(1)}, s16[32,2048]{1,0:T(8,128)(2,1)S(1)}, u32[]{:S(2)}, u32[]{:S(2)}) %collective-permute-start.4) | collective-permute-done | bytes 131104 | tf_op jit(solution)/shard_map/ppermute | solution.py:280
  81.9 0.0 all-to-all-done.2.sums_ref
  81.9 0.0 collective-permute-done.5.first_ref
  81.9 2.8 %shard_map.63 = (f32[8,8,2048]{2,1,0:T(8,128)}, f32[8,2048]{1,0:T(8,128)}) custom-call(f32[8,24,2048]{2,1,0:T(8,128)S(1)} %get-tuple-element.24.u_ref, f32[8,2048]{1,0:T(8,128)S(1)} %bitcast.17, s16[32,2048]{1,0:T(8,128)(2,1)S(1)} %collective-permute-done.4.second_ref, f32[32,2048]{1,0:T(8,128)S(1)} %collective-permute-done.5.first_ref, ...), custom_call_target="tpu_custom_call" | custom-call | tf_op jit(solution)/shard_map/pallas_call | solution.py:264
Async XLA Ops:
  0.6 63.3 %copy-start.4 = (s32[32,32]{1,0:T(8,128)S(1)}, s32[32,32]{1,0:T(8,128)}, u32[]{:S(2)}) copy-start(s32[32,32]{1,0:T(8,128)} %w_ref.3) | copy-start | bytes 12292
  0.6 63.3 %copy-start.2 = (f32[1,8,2048]{2,1,0:T(8,128)S(1)}, f32[1,8,2048]{2,1,0:T(8,128)}, u32[]{:S(2)}) copy-start(f32[1,8,2048]{2,1,0:T(8,128)} %param.5) | copy-start | bytes 196612
  0.6 63.3 %copy-start = (f32[1,8,2048]{2,1,0:T(8,128)S(1)}, f32[1,8,2048]{2,1,0:T(8,128)}, u32[]{:S(2)}) copy-start(f32[1,8,2048]{2,1,0:T(8,128)} %param.7) | copy-start | bytes 196612
  0.7 29.0 %all-to-all-start = ((bf16[32,8,512]{2,1,0:T(8,128)(2,1)}), bf16[32,8,512]{2,1,0:T(8,128)(2,1)S(1)}, u32[]{:S(2)}, u32[]{:S(2)}) async-start(bf16[32,8,512]{2,1,0:T(8,128)(2,1)} %bitcast.20), calls=%async_computation | async-start | bytes 524288 | tf_op jit(solution)/shard_map/all_to_all | solution.py:293
  11.0 0.8 copy-start.1
  11.8 0.7 copy-start.3
  12.8 12.9 %collective-permute-start.1 = (s16[8,2048]{1,0:T(8,128)(2,1)S(1)}, s16[8,2048]{1,0:T(8,128)(2,1)S(1)}, u32[]{:S(2)}, u32[]{:S(2)}) collective-permute-start(s16[8,2048]{1,0:T(8,128)(2,1)S(1)} %get-tuple-element.18), channel_id=1, source_target_pairs={{0,15},{1,2},{2,1},{3,4},{4,3},{5,6},{6,5},{7,8},{8,7},{9,10},{10,... | collective-permute-start | bytes 98312 | tf_op jit(solution)/shard_map/ppermute | solution.py:280
  23.8 5.8 %collective-permute-start = (s16[8,2048]{1,0:T(8,128)(2,1)S(1)}, s16[8,2048]{1,0:T(8,128)(2,1)S(1)}, u32[]{:S(2)}, u32[]{:S(2)}) collective-permute-start(s16[8,2048]{1,0:T(8,128)(2,1)S(1)} %get-tuple-element.18), channel_id=1, source_target_pairs={{0,1},{1,0},{2,3},{3,2},{4,5},{5,4},{6,7},{7,6},{8,9},{9,8},{10,11... | collective-permute-start | bytes 98312 | tf_op jit(solution)/shard_map/ppermute | solution.py:275
  53.2 6.7 %collective-permute-start.2 = (s16[56,1024]{1,0:T(8,128)(2,1)S(1)}, s16[56,1024]{1,0:T(8,128)(2,1)S(1)}, u32[]{:S(2)}, u32[]{:S(2)}) collective-permute-start(s16[56,1024]{1,0:T(8,128)(2,1)S(1)} %get-tuple-element.22), channel_id=1, source_target_pairs={{0,1},{1,0},{2,3},{3,2},{4,5},{5,4},{6,7},{7,6},{8,9},{9,8},{10,11... | collective-permute-start | bytes 344072 | tf_op jit(solution)/shard_map/ppermute | solution.py:275
  55.1 8.8 %collective-permute-start.3 = (s16[56,1024]{1,0:T(8,128)(2,1)S(1)}, s16[56,1024]{1,0:T(8,128)(2,1)S(1)}, u32[]{:S(2)}, u32[]{:S(2)}) collective-permute-start(s16[56,1024]{1,0:T(8,128)(2,1)S(1)} %get-tuple-element.23), channel_id=1, source_target_pairs={{0,15},{1,2},{2,1},{3,4},{4,3},{5,6},{6,5},{7,8},{8,7},{9,10},{10,... | collective-permute-start | bytes 344072 | tf_op jit(solution)/shard_map/ppermute | solution.py:280
  66.3 15.6 %collective-permute-start.5 = (f32[32,2048]{1,0:T(8,128)S(1)}, f32[32,2048]{1,0:T(8,128)S(1)}, u32[]{:S(2)}, u32[]{:S(2)}) collective-permute-start(f32[32,2048]{1,0:T(8,128)S(1)} %get-tuple-element.26), channel_id=1, source_target_pairs={{0,1},{1,0},{2,3},{3,2},{4,5},{5,4},{6,7},{7,6},{8,9},{9,8},{10,11... | collective-permute-start | bytes 786440 | tf_op jit(solution)/shard_map/ppermute | solution.py:275
  69.0 12.9 %all-to-all-start.2 = ((f32[16,1,1152]{2,1,0:T(1,128)}), f32[16,1,1152]{2,1,0:T(1,128)S(1)}, u32[]{:S(2)}, u32[]{:S(2)}) async-start(f32[16,1,1152]{2,1,0:T(1,128)} %get-tuple-element.27), calls=%async_computation.2 | async-start | bytes 147456 | tf_op jit(solution)/shard_map/all_to_all | solution.py:342
  72.7 9.2 %collective-permute-start.4 = (s16[32,2048]{1,0:T(8,128)(2,1)S(1)}, s16[32,2048]{1,0:T(8,128)(2,1)S(1)}, u32[]{:S(2)}, u32[]{:S(2)}) collective-permute-start(s16[32,2048]{1,0:T(8,128)(2,1)S(1)} %get-tuple-element.25), channel_id=1, source_target_pairs={{0,15},{1,2},{2,1},{3,4},{4,3},{5,6},{6,5},{7,8},{8,7},{9,10},{10,... | collective-permute-start | bytes 393224 | tf_op jit(solution)/shard_map/ppermute | solution.py:280

commit v10 on v8

--- a/solution.py
+++ b/solution.py
@@ -190,11 +190,7 @@
     exponent = jnp.ceil(jnp.log2(jnp.maximum(largest, 1e-30)))
     scale = LEVELS / jnp.exp2(exponent)
     inner = jnp.where((row >= 1) & (row <= 6), kept[1], pltpu.roll(kept[3], 4, 0))
-    first_edge_ref[0:8] = init_ref[...]
-    first_edge_ref[8:16] = kept[0]
-    first_edge_ref[16:24] = inner
-    first_edge_ref[24:32] = kept[2]
-    second_edge_ref[...] = to_i16(
+    edges = to_i16(
         jnp.concatenate(
             [
                 (init_ref[...] - INIT_MID) * INIT_SCALE,
@@ -205,6 +201,9 @@
             axis=0,
         )
     )
+    second_edge_ref[...] = edges
+    spare = first_edge_ref.shape[0] - edges.shape[0]
+    first_edge_ref[...] = jnp.concatenate([edges, edges[:spare]], axis=0)
 
 
 def decoded(edge):
@@ -219,7 +218,7 @@
     cols = init_ref.shape[1]
     row = lax.broadcasted_iota(jnp.int32, (HALO, cols), 0)
     even = is_even()
-    first = first_ref[...]
+    first = decoded(first_ref[...])
     second = decoded(second_ref[...])
     above = jnp.where(even, second, first)
     below = jnp.where(even, first, second)
@@ -316,7 +315,7 @@
         functools.partial(backward_kernel, blocks, steps),
         (
             struct((steps, 3 * HALO, cols), F32),
-            struct((32, cols), F32),
+            struct((40, cols), I16),
             struct((32, cols), I16),
             struct((tiles, 1, 1152), F32),
         ),

time: 81.5 us -> 81.5 us (level)
  no operation moved by 1% of the time
where the time goes in v10:
time: 81.5 us; the launch traced here: 81 us
  starting transfers between devices  38.5 us (47%)
  waiting for transfers between devices  18.3 us (22%)
  blocking collectives  16.9 us (21%)
  Pallas kernels  5.8 us (7%)
    ppermute x2, starting transfers between devices, second_swap(): lax.ppermute(x, 'tile', [(i, ((i + 1 ^ 1) - 1) % peers) for i in range(pe...  17.8 us
    all_to_all x1, blocking collectives, per_device(): lax.all_to_all(levels.reshape(pops, rows, part), POP, 0, 0, tiled=True)  16.9 us
    all_to_all x1, waiting for transfers between devices, per_device(): lax.all_to_all(chunks.reshape(pops, rows, part), POP, 0, 0, tiled=True)  12 us
    all_to_all x1, starting transfers between devices, per_device(): lax.all_to_all(chunks.reshape(pops, rows, part), POP, 0, 0, tiled=True)  10.3 us
    ppermute x2, waiting for transfers between devices, second_swap(): lax.ppermute(x, 'tile', [(i, ((i + 1 ^ 1) - 1) % peers) for i in range(pe...  6.32 us
    all_to_all x1, starting transfers between devices, per_device(): sums = lax.all_to_all(sums, 'tile', 0, 0, tiled=True)  6.07 us
    pallas_call x5, Pallas kernels, call(): pl.pallas_call(kernel, out_shape=outs, in_specs=[spec] * len(args), out_s...  5.8 us
    ppermute x2, starting transfers between devices, first_swap(): return lax.ppermute(x, 'tile', [(i, i ^ 1) for i in range(peers)])  4.41 us
  transfers between devices with their start and end apart: 6, of which 3 were waited for; matrix products, arithmetic and copies ran while one was open for 0% of the time, Pallas kernels for 0%

profile of v10, /device:TPU:8, one launch (start us, length us, event | category | flops | bytes accessed | tf_op | source)
XLA Modules:
  0.0 81.0 jit_solution(12847908930477710317)
XLA Ops:
  0.6 0.0 copy-start.3
  0.6 0.0 copy-start
  0.6 0.0 copy-start.1
  0.7 10.3 %all-to-all-start = ((bf16[32,8,512]{2,1,0:T(8,128)(2,1)}), bf16[32,8,512]{2,1,0:T(8,128)(2,1)S(1)}, u32[]{:S(2)}, u32[]{:S(2)}) async-start(bf16[32,8,512]{2,1,0:T(8,128)(2,1)} %bitcast.20), calls=%async_computation | async-start | bytes 524288 | tf_op jit(solution)/shard_map/all_to_all | solution.py:291
  11.0 0.0 copy-start.2
  11.0 0.7 copy-done.2
  11.7 0.3 shard_map.59
  12.0 12.0 %all-to-all-done = bf16[32,8,512]{2,1,0:T(8,128)(2,1)S(1)} async-done(((bf16[32,8,512]{2,1,0:T(8,128)(2,1)}), bf16[32,8,512]{2,1,0:T(8,128)(2,1)S(1)}, u32[]{:S(2)}, u32[]{:S(2)}) %all-to-all-start) | async-done | bytes 262176 | tf_op jit(solution)/shard_map/all_to_all | solution.py:291
  24.0 0.2 shard_map.60
  24.2 16.9 %all_to_all.15 = s16[32,8,512]{2,1,0:T(8,128)(2,1)S(1)} all-to-all(s16[32,8,512]{2,1,0:T(8,128)(2,1)S(1)} %bitcast.15), channel_id=1, replica_groups=mesh['pop_0'=8,'pop_1'=2,'pop_2'=2,'tile'=16] {'pop_0','pop_1','pop_2'}, dimensions={0} | all-to-all | bytes 524288 | tf_op jit(solution)/shard_map/all_to_all | solution.py:304
  41.1 0.0 copy-done
  41.1 0.1 shard_map.61
  41.2 2.5 %collective-permute-start = (s16[72,1024]{1,0:T(8,128)(2,1)S(1)}, s16[72,1024]{1,0:T(8,128)(2,1)S(1)}, u32[]{:S(2)}, u32[]{:S(2)}) collective-permute-start(s16[72,1024]{1,0:T(8,128)(2,1)S(1)} %get-tuple-element.14), channel_id=1, source_target_pairs={{0,1},{1,0},{2,3},{3,2},{4,5},{5,4},{6,7},{7,6},{8,9},{9,8},{10,11... | collective-permute-start | bytes 442376 | tf_op jit(solution)/shard_map/ppermute | solution.py:273
  43.7 11.8 %collective-permute-start.1 = (s16[72,1024]{1,0:T(8,128)(2,1)S(1)}, s16[72,1024]{1,0:T(8,128)(2,1)S(1)}, u32[]{:S(2)}, u32[]{:S(2)}) collective-permute-start(s16[72,1024]{1,0:T(8,128)(2,1)S(1)} %get-tuple-element.15), channel_id=1, source_target_pairs={{0,15},{1,2},{2,1},{3,4},{4,3},{5,6},{6,5},{7,8},{8,7},{9,10},{10,... | collective-permute-start | bytes 442376 | tf_op jit(solution)/shard_map/ppermute | solution.py:278
  55.5 0.0 collective-permute-done.first_ref
  55.6 3.1 %collective-permute-done.1.second_ref = s16[72,1024]{1,0:T(8,128)(2,1)S(1)} collective-permute-done((s16[72,1024]{1,0:T(8,128)(2,1)S(1)}, s16[72,1024]{1,0:T(8,128)(2,1)S(1)}, u32[]{:S(2)}, u32[]{:S(2)}) %collective-permute-start.1) | collective-permute-done | bytes 147488 | tf_op jit(solution)/shard_map/ppermute | solution.py:278
  58.6 0.0 copy-done.3
  58.7 0.0 copy-done.1
  58.7 2.4 %shard_map.62 = (f32[8,24,2048]{2,1,0:T(8,128)S(1)}, s16[40,2048]{1,0:T(8,128)(2,1)S(1)}, s16[32,2048]{1,0:T(8,128)(2,1)S(1)}, f32[16,1,1152]{2,1,0:T(1,128)}) custom-call(s32[32,32]{1,0:T(8,128)S(1)} %copy-done.3, s16[256,512]{1,0:T(8,128)(2,1)S(1)} %bitcast.13, f32[8,2048]{1,0:T(8,128)S(1)} %bitcast.17, f32[8,2048]{1,0:T(8,128)S(1)} %bitcast.18, ...), custom_call_target="tpu_custom_call" | custom-call | tf_op jit(solution)/shard_map/pallas_call | solution.py:262
  61.0 1.9 %collective-permute-start.3 = (s16[40,2048]{1,0:T(8,128)(2,1)S(1)}, s16[40,2048]{1,0:T(8,128)(2,1)S(1)}, u32[]{:S(2)}, u32[]{:S(2)}) collective-permute-start(s16[40,2048]{1,0:T(8,128)(2,1)S(1)} %get-tuple-element.18), channel_id=1, source_target_pairs={{0,1},{1,0},{2,3},{3,2},{4,5},{5,4},{6,7},{7,6},{8,9},{9,8},{10,11... | collective-permute-start | bytes 491528 | tf_op jit(solution)/shard_map/ppermute | solution.py:273
  62.9 6.1 %all-to-all-start.2 = ((f32[16,1,1152]{2,1,0:T(1,128)}), f32[16,1,1152]{2,1,0:T(1,128)S(1)}, u32[]{:S(2)}, u32[]{:S(2)}) async-start(f32[16,1,1152]{2,1,0:T(1,128)} %get-tuple-element.19), calls=%async_computation.2 | async-start | bytes 147456 | tf_op jit(solution)/shard_map/all_to_all | solution.py:331
  69.0 5.9 %collective-permute-start.2 = (s16[32,2048]{1,0:T(8,128)(2,1)S(1)}, s16[32,2048]{1,0:T(8,128)(2,1)S(1)}, u32[]{:S(2)}, u32[]{:S(2)}) collective-permute-start(s16[32,2048]{1,0:T(8,128)(2,1)S(1)} %get-tuple-element.17), channel_id=1, source_target_pairs={{0,15},{1,2},{2,1},{3,4},{4,3},{5,6},{6,5},{7,8},{8,7},{9,10},{10,... | collective-permute-start | bytes 393224 | tf_op jit(solution)/shard_map/ppermute | solution.py:278
  75.0 3.2 %collective-permute-done.2.second_ref = s16[32,2048]{1,0:T(8,128)(2,1)S(1)} collective-permute-done((s16[32,2048]{1,0:T(8,128)(2,1)S(1)}, s16[32,2048]{1,0:T(8,128)(2,1)S(1)}, u32[]{:S(2)}, u32[]{:S(2)}) %collective-permute-start.2) | collective-permute-done | bytes 131104 | tf_op jit(solution)/shard_map/ppermute | solution.py:278
  78.2 0.0 all-to-all-done.2.sums_ref
  78.2 0.0 collective-permute-done.3.first_ref
  78.2 2.8 %shard_map.63 = (f32[8,8,2048]{2,1,0:T(8,128)}, f32[8,2048]{1,0:T(8,128)}) custom-call(f32[8,24,2048]{2,1,0:T(8,128)S(1)} %get-tuple-element.16.u_ref, f32[8,2048]{1,0:T(8,128)S(1)} %bitcast.19, s16[32,2048]{1,0:T(8,128)(2,1)S(1)} %collective-permute-done.2.second_ref, s16[40,2048]{1,0:T(8,128)(2,1)S(1)} %collective-permute-done.3.first_ref, ...), custom_call_target="tpu_custom_call" | custom-call | tf_op jit(solution)/shard_map/pallas_call | solution.py:262
Async XLA Ops:
  0.6 58.0 %copy-start.3 = (s32[32,32]{1,0:T(8,128)S(1)}, s32[32,32]{1,0:T(8,128)}, u32[]{:S(2)}) copy-start(s32[32,32]{1,0:T(8,128)} %w_ref.3) | copy-start | bytes 12292
  0.6 40.5 %copy-start = (f32[1,8,2048]{2,1,0:T(8,128)S(1)}, f32[1,8,2048]{2,1,0:T(8,128)}, u32[]{:S(2)}) copy-start(f32[1,8,2048]{2,1,0:T(8,128)} %param.5) | copy-start | bytes 196612
  0.6 58.0 %copy-start.1 = (f32[1,8,2048]{2,1,0:T(8,128)S(1)}, f32[1,8,2048]{2,1,0:T(8,128)}, u32[]{:S(2)}) copy-start(f32[1,8,2048]{2,1,0:T(8,128)} %param.7) | copy-start | bytes 196612
  0.7 23.3 %all-to-all-start = ((bf16[32,8,512]{2,1,0:T(8,128)(2,1)}), bf16[32,8,512]{2,1,0:T(8,128)(2,1)S(1)}, u32[]{:S(2)}, u32[]{:S(2)}) async-start(bf16[32,8,512]{2,1,0:T(8,128)(2,1)} %bitcast.20), calls=%async_computation | async-start | bytes 524288 | tf_op jit(solution)/shard_map/all_to_all | solution.py:291
  11.0 0.7 copy-start.2
  41.2 14.3 %collective-permute-start = (s16[72,1024]{1,0:T(8,128)(2,1)S(1)}, s16[72,1024]{1,0:T(8,128)(2,1)S(1)}, u32[]{:S(2)}, u32[]{:S(2)}) collective-permute-start(s16[72,1024]{1,0:T(8,128)(2,1)S(1)} %get-tuple-element.14), channel_id=1, source_target_pairs={{0,1},{1,0},{2,3},{3,2},{4,5},{5,4},{6,7},{7,6},{8,9},{9,8},{10,11... | collective-permute-start | bytes 442376 | tf_op jit(solution)/shard_map/ppermute | solution.py:273
  43.7 14.9 %collective-permute-start.1 = (s16[72,1024]{1,0:T(8,128)(2,1)S(1)}, s16[72,1024]{1,0:T(8,128)(2,1)S(1)}, u32[]{:S(2)}, u32[]{:S(2)}) collective-permute-start(s16[72,1024]{1,0:T(8,128)(2,1)S(1)} %get-tuple-element.15), channel_id=1, source_target_pairs={{0,15},{1,2},{2,1},{3,4},{4,3},{5,6},{6,5},{7,8},{8,7},{9,10},{10,... | collective-permute-start | bytes 442376 | tf_op jit(solution)/shard_map/ppermute | solution.py:278
  61.0 17.2 %collective-permute-start.3 = (s16[40,2048]{1,0:T(8,128)(2,1)S(1)}, s16[40,2048]{1,0:T(8,128)(2,1)S(1)}, u32[]{:S(2)}, u32[]{:S(2)}) collective-permute-start(s16[40,2048]{1,0:T(8,128)(2,1)S(1)} %get-tuple-element.18), channel_id=1, source_target_pairs={{0,1},{1,0},{2,3},{3,2},{4,5},{5,4},{6,7},{7,6},{8,9},{9,8},{10,11... | collective-permute-start | bytes 491528 | tf_op jit(solution)/shard_map/ppermute | solution.py:273
  62.9 15.2 %all-to-all-start.2 = ((f32[16,1,1152]{2,1,0:T(1,128)}), f32[16,1,1152]{2,1,0:T(1,128)S(1)}, u32[]{:S(2)}, u32[]{:S(2)}) async-start(f32[16,1,1152]{2,1,0:T(1,128)} %get-tuple-element.19), calls=%async_computation.2 | async-start | bytes 147456 | tf_op jit(solution)/shard_map/all_to_all | solution.py:331
  69.0 9.2 %collective-permute-start.2 = (s16[32,2048]{1,0:T(8,128)(2,1)S(1)}, s16[32,2048]{1,0:T(8,128)(2,1)S(1)}, u32[]{:S(2)}, u32[]{:S(2)}) collective-permute-start(s16[32,2048]{1,0:T(8,128)(2,1)S(1)} %get-tuple-element.17), channel_id=1, source_target_pairs={{0,15},{1,2},{2,1},{3,4},{4,3},{5,6},{6,5},{7,8},{8,7},{9,10},{10,... | collective-permute-start | bytes 393224 | tf_op jit(solution)/shard_map/ppermute | solution.py:278

commit v11 on v10

--- a/solution.py
+++ b/solution.py
@@ -167,8 +167,11 @@
         low_c, up_c = shares(ahead_c)
         source = levels(t) * slope + offset
         u = (u + source) + (low_r - pltpu.roll(up_r, 1, 0)) + (low_c - pltpu.roll(up_c, 1, 1))
-        u_ref[t] = u
         mine = u[HALO : 2 * HALO]
+        if t == 0:
+            u_ref[t, HALO : 2 * HALO, :] = mine
+        else:
+            u_ref[t] = u
         kept[t] = mine
         lanes = mine[:, :128]
         for k in range(1, cols // 128):
@@ -226,13 +229,14 @@
     high = m.shape[0]
 
     def field(t):
+        if t == 0:
+            own = u_ref[0, HALO : 2 * HALO, :]
+            return jnp.concatenate([above[8:16], own, below[8:16]], axis=0)
         u = u_ref[t]
         if t > 3:
             return u
 
         def side(far, near):
-            if t == 0:
-                return far[8:16]
             if t == 1:
                 return jnp.where((row >= 1) & (row <= 6), far[16:24], near)
             if t == 2:

time: 81.5 us -> 81.4 us (level)
  no operation moved by 1% of the time
where the time goes in v11:
time: 81.4 us; the launch traced here: 80.9 us
  starting transfers between devices  38.5 us (47%)
  waiting for transfers between devices  18.3 us (22%)
  blocking collectives  16.9 us (21%)
  Pallas kernels  5.75 us (7%)
    ppermute x2, starting transfers between devices, second_swap(): lax.ppermute(x, 'tile', [(i, ((i + 1 ^ 1) - 1) % peers) for i in range(pe...  17.8 us
    all_to_all x1, blocking collectives, per_device(): lax.all_to_all(levels.reshape(pops, rows, part), POP, 0, 0, tiled=True)  16.9 us
    all_to_all x1, waiting for transfers between devices, per_device(): lax.all_to_all(chunks.reshape(pops, rows, part), POP, 0, 0, tiled=True)  12 us
    all_to_all x1, starting transfers between devices, per_device(): lax.all_to_all(chunks.reshape(pops, rows, part), POP, 0, 0, tiled=True)  10.3 us
    ppermute x2, waiting for transfers between devices, second_swap(): lax.ppermute(x, 'tile', [(i, ((i + 1 ^ 1) - 1) % peers) for i in range(pe...  6.32 us
    all_to_all x1, starting transfers between devices, per_device(): sums = lax.all_to_all(sums, 'tile', 0, 0, tiled=True)  6.07 us
    pallas_call x5, Pallas kernels, call(): pl.pallas_call(kernel, out_shape=outs, in_specs=[spec] * len(args), out_s...  5.75 us
    ppermute x2, starting transfers between devices, first_swap(): return lax.ppermute(x, 'tile', [(i, i ^ 1) for i in range(peers)])  4.41 us
  transfers between devices with their start and end apart: 6, of which 3 were waited for; matrix products, arithmetic and copies ran while one was open for 0% of the time, Pallas kernels for 0%

profile of v11, /device:TPU:8, one launch (start us, length us, event | category | flops | bytes accessed | tf_op | source)
XLA Modules:
  0.0 80.9 jit_solution(14104474095018314102)
XLA Ops:
  0.6 0.0 copy-start.3
  0.6 0.0 copy-start
  0.6 0.0 copy-start.1
  0.7 10.3 %all-to-all-start = ((bf16[32,8,512]{2,1,0:T(8,128)(2,1)}), bf16[32,8,512]{2,1,0:T(8,128)(2,1)S(1)}, u32[]{:S(2)}, u32[]{:S(2)}) async-start(bf16[32,8,512]{2,1,0:T(8,128)(2,1)} %bitcast.20), calls=%async_computation | async-start | bytes 524288 | tf_op jit(solution)/shard_map/all_to_all | solution.py:295
  11.0 0.0 copy-start.2
  11.0 0.7 copy-done.2
  11.7 0.3 shard_map.59
  12.0 12.0 %all-to-all-done = bf16[32,8,512]{2,1,0:T(8,128)(2,1)S(1)} async-done(((bf16[32,8,512]{2,1,0:T(8,128)(2,1)}), bf16[32,8,512]{2,1,0:T(8,128)(2,1)S(1)}, u32[]{:S(2)}, u32[]{:S(2)}) %all-to-all-start) | async-done | bytes 262176 | tf_op jit(solution)/shard_map/all_to_all | solution.py:295
  24.0 0.2 shard_map.60
  24.2 16.9 %all_to_all.15 = s16[32,8,512]{2,1,0:T(8,128)(2,1)S(1)} all-to-all(s16[32,8,512]{2,1,0:T(8,128)(2,1)S(1)} %bitcast.15), channel_id=1, replica_groups=mesh['pop_0'=8,'pop_1'=2,'pop_2'=2,'tile'=16] {'pop_0','pop_1','pop_2'}, dimensions={0} | all-to-all | bytes 524288 | tf_op jit(solution)/shard_map/all_to_all | solution.py:308
  41.1 0.0 copy-done
  41.1 0.1 shard_map.61
  41.2 2.5 %collective-permute-start = (s16[72,1024]{1,0:T(8,128)(2,1)S(1)}, s16[72,1024]{1,0:T(8,128)(2,1)S(1)}, u32[]{:S(2)}, u32[]{:S(2)}) collective-permute-start(s16[72,1024]{1,0:T(8,128)(2,1)S(1)} %get-tuple-element.14), channel_id=1, source_target_pairs={{0,1},{1,0},{2,3},{3,2},{4,5},{5,4},{6,7},{7,6},{8,9},{9,8},{10,11... | collective-permute-start | bytes 442376 | tf_op jit(solution)/shard_map/ppermute | solution.py:277
  43.7 11.8 %collective-permute-start.1 = (s16[72,1024]{1,0:T(8,128)(2,1)S(1)}, s16[72,1024]{1,0:T(8,128)(2,1)S(1)}, u32[]{:S(2)}, u32[]{:S(2)}) collective-permute-start(s16[72,1024]{1,0:T(8,128)(2,1)S(1)} %get-tuple-element.15), channel_id=1, source_target_pairs={{0,15},{1,2},{2,1},{3,4},{4,3},{5,6},{6,5},{7,8},{8,7},{9,10},{10,... | collective-permute-start | bytes 442376 | tf_op jit(solution)/shard_map/ppermute | solution.py:282
  55.5 0.0 collective-permute-done.first_ref
  55.6 3.1 %collective-permute-done.1.second_ref = s16[72,1024]{1,0:T(8,128)(2,1)S(1)} collective-permute-done((s16[72,1024]{1,0:T(8,128)(2,1)S(1)}, s16[72,1024]{1,0:T(8,128)(2,1)S(1)}, u32[]{:S(2)}, u32[]{:S(2)}) %collective-permute-start.1) | collective-permute-done | bytes 147488 | tf_op jit(solution)/shard_map/ppermute | solution.py:282
  58.6 0.0 copy-done.3
  58.7 0.0 copy-done.1
  58.7 2.3 %shard_map.62 = (f32[8,24,2048]{2,1,0:T(8,128)S(1)}, s16[40,2048]{1,0:T(8,128)(2,1)S(1)}, s16[32,2048]{1,0:T(8,128)(2,1)S(1)}, f32[16,1,1152]{2,1,0:T(1,128)}) custom-call(s32[32,32]{1,0:T(8,128)S(1)} %copy-done.3, s16[256,512]{1,0:T(8,128)(2,1)S(1)} %bitcast.13, f32[8,2048]{1,0:T(8,128)S(1)} %bitcast.17, f32[8,2048]{1,0:T(8,128)S(1)} %bitcast.18, ...), custom_call_target="tpu_custom_call" | custom-call | tf_op jit(solution)/shard_map/pallas_call | solution.py:266
  61.0 1.9 %collective-permute-start.3 = (s16[40,2048]{1,0:T(8,128)(2,1)S(1)}, s16[40,2048]{1,0:T(8,128)(2,1)S(1)}, u32[]{:S(2)}, u32[]{:S(2)}) collective-permute-start(s16[40,2048]{1,0:T(8,128)(2,1)S(1)} %get-tuple-element.18), channel_id=1, source_target_pairs={{0,1},{1,0},{2,3},{3,2},{4,5},{5,4},{6,7},{7,6},{8,9},{9,8},{10,11... | collective-permute-start | bytes 491528 | tf_op jit(solution)/shard_map/ppermute | solution.py:277
  62.9 6.1 %all-to-all-start.2 = ((f32[16,1,1152]{2,1,0:T(1,128)}), f32[16,1,1152]{2,1,0:T(1,128)S(1)}, u32[]{:S(2)}, u32[]{:S(2)}) async-start(f32[16,1,1152]{2,1,0:T(1,128)} %get-tuple-element.19), calls=%async_computation.2 | async-start | bytes 147456 | tf_op jit(solution)/shard_map/all_to_all | solution.py:335
  69.0 5.9 %collective-permute-start.2 = (s16[32,2048]{1,0:T(8,128)(2,1)S(1)}, s16[32,2048]{1,0:T(8,128)(2,1)S(1)}, u32[]{:S(2)}, u32[]{:S(2)}) collective-permute-start(s16[32,2048]{1,0:T(8,128)(2,1)S(1)} %get-tuple-element.17), channel_id=1, source_target_pairs={{0,15},{1,2},{2,1},{3,4},{4,3},{5,6},{6,5},{7,8},{8,7},{9,10},{10,... | collective-permute-start | bytes 393224 | tf_op jit(solution)/shard_map/ppermute | solution.py:282
  74.9 3.2 %collective-permute-done.2.second_ref = s16[32,2048]{1,0:T(8,128)(2,1)S(1)} collective-permute-done((s16[32,2048]{1,0:T(8,128)(2,1)S(1)}, s16[32,2048]{1,0:T(8,128)(2,1)S(1)}, u32[]{:S(2)}, u32[]{:S(2)}) %collective-permute-start.2) | collective-permute-done | bytes 131104 | tf_op jit(solution)/shard_map/ppermute | solution.py:282
  78.1 0.0 all-to-all-done.2.sums_ref
  78.1 0.0 collective-permute-done.3.first_ref
  78.1 2.8 %shard_map.63 = (f32[8,8,2048]{2,1,0:T(8,128)}, f32[8,2048]{1,0:T(8,128)}) custom-call(f32[8,24,2048]{2,1,0:T(8,128)S(1)} %get-tuple-element.16.u_ref, f32[8,2048]{1,0:T(8,128)S(1)} %bitcast.19, s16[32,2048]{1,0:T(8,128)(2,1)S(1)} %collective-permute-done.2.second_ref, s16[40,2048]{1,0:T(8,128)(2,1)S(1)} %collective-permute-done.3.first_ref, ...), custom_call_target="tpu_custom_call" | custom-call | tf_op jit(solution)/shard_map/pallas_call | solution.py:266
Async XLA Ops:
  0.6 58.0 %copy-start.3 = (s32[32,32]{1,0:T(8,128)S(1)}, s32[32,32]{1,0:T(8,128)}, u32[]{:S(2)}) copy-start(s32[32,32]{1,0:T(8,128)} %w_ref.3) | copy-start | bytes 12292
  0.6 40.5 %copy-start = (f32[1,8,2048]{2,1,0:T(8,128)S(1)}, f32[1,8,2048]{2,1,0:T(8,128)}, u32[]{:S(2)}) copy-start(f32[1,8,2048]{2,1,0:T(8,128)} %param.5) | copy-start | bytes 196612
  0.6 58.0 %copy-start.1 = (f32[1,8,2048]{2,1,0:T(8,128)S(1)}, f32[1,8,2048]{2,1,0:T(8,128)}, u32[]{:S(2)}) copy-start(f32[1,8,2048]{2,1,0:T(8,128)} %param.7) | copy-start | bytes 196612
  0.7 23.3 %all-to-all-start = ((bf16[32,8,512]{2,1,0:T(8,128)(2,1)}), bf16[32,8,512]{2,1,0:T(8,128)(2,1)S(1)}, u32[]{:S(2)}, u32[]{:S(2)}) async-start(bf16[32,8,512]{2,1,0:T(8,128)(2,1)} %bitcast.20), calls=%async_computation | async-start | bytes 524288 | tf_op jit(solution)/shard_map/all_to_all | solution.py:295
  11.0 0.7 copy-start.2
  41.2 14.3 %collective-permute-start = (s16[72,1024]{1,0:T(8,128)(2,1)S(1)}, s16[72,1024]{1,0:T(8,128)(2,1)S(1)}, u32[]{:S(2)}, u32[]{:S(2)}) collective-permute-start(s16[72,1024]{1,0:T(8,128)(2,1)S(1)} %get-tuple-element.14), channel_id=1, source_target_pairs={{0,1},{1,0},{2,3},{3,2},{4,5},{5,4},{6,7},{7,6},{8,9},{9,8},{10,11... | collective-permute-start | bytes 442376 | tf_op jit(solution)/shard_map/ppermute | solution.py:277
  43.7 14.9 %collective-permute-start.1 = (s16[72,1024]{1,0:T(8,128)(2,1)S(1)}, s16[72,1024]{1,0:T(8,128)(2,1)S(1)}, u32[]{:S(2)}, u32[]{:S(2)}) collective-permute-start(s16[72,1024]{1,0:T(8,128)(2,1)S(1)} %get-tuple-element.15), channel_id=1, source_target_pairs={{0,15},{1,2},{2,1},{3,4},{4,3},{5,6},{6,5},{7,8},{8,7},{9,10},{10,... | collective-permute-start | bytes 442376 | tf_op jit(solution)/shard_map/ppermute | solution.py:282
  61.0 17.2 %collective-permute-start.3 = (s16[40,2048]{1,0:T(8,128)(2,1)S(1)}, s16[40,2048]{1,0:T(8,128)(2,1)S(1)}, u32[]{:S(2)}, u32[]{:S(2)}) collective-permute-start(s16[40,2048]{1,0:T(8,128)(2,1)S(1)} %get-tuple-element.18), channel_id=1, source_target_pairs={{0,1},{1,0},{2,3},{3,2},{4,5},{5,4},{6,7},{7,6},{8,9},{9,8},{10,11... | collective-permute-start | bytes 491528 | tf_op jit(solution)/shard_map/ppermute | solution.py:277
  62.9 15.2 %all-to-all-start.2 = ((f32[16,1,1152]{2,1,0:T(1,128)}), f32[16,1,1152]{2,1,0:T(1,128)S(1)}, u32[]{:S(2)}, u32[]{:S(2)}) async-start(f32[16,1,1152]{2,1,0:T(1,128)} %get-tuple-element.19), calls=%async_computation.2 | async-start | bytes 147456 | tf_op jit(solution)/shard_map/all_to_all | solution.py:335
  69.0 9.2 %collective-permute-start.2 = (s16[32,2048]{1,0:T(8,128)(2,1)S(1)}, s16[32,2048]{1,0:T(8,128)(2,1)S(1)}, u32[]{:S(2)}, u32[]{:S(2)}) collective-permute-start(s16[32,2048]{1,0:T(8,128)(2,1)S(1)} %get-tuple-element.17), channel_id=1, source_target_pairs={{0,15},{1,2},{2,1},{3,4},{4,3},{5,6},{6,5},{7,8},{8,7},{9,10},{10,... | collective-permute-start | bytes 393224 | tf_op jit(solution)/shard_map/ppermute | solution.py:282

commit v12 on v11

--- a/solution.py
+++ b/solution.py
@@ -193,20 +193,14 @@
     exponent = jnp.ceil(jnp.log2(jnp.maximum(largest, 1e-30)))
     scale = LEVELS / jnp.exp2(exponent)
     inner = jnp.where((row >= 1) & (row <= 6), kept[1], pltpu.roll(kept[3], 4, 0))
-    edges = to_i16(
-        jnp.concatenate(
-            [
-                (init_ref[...] - INIT_MID) * INIT_SCALE,
-                kept[0] * scale,
-                inner * scale,
-                jnp.where(row == 0, exponent, kept[2] * scale),
-            ],
-            axis=0,
-        )
-    )
-    second_edge_ref[...] = edges
-    spare = first_edge_ref.shape[0] - edges.shape[0]
-    first_edge_ref[...] = jnp.concatenate([edges, edges[:spare]], axis=0)
+    edges = [
+        (init_ref[...] - INIT_MID) * INIT_SCALE,
+        kept[0] * scale,
+        inner * scale,
+        jnp.where(row == 0, exponent, kept[2] * scale),
+    ]
+    second_edge_ref[...] = to_i16(jnp.concatenate(edges, axis=0))
+    first_edge_ref[...] = to_i16(jnp.concatenate(edges + edges[:1], axis=0))
 
 
 def decoded(edge):

time: 81.4 us -> 81.4 us (level)
  no operation moved by 1% of the time
where the time goes in v12:
time: 81.4 us; the launch traced here: 80.9 us
  starting transfers between devices  38.5 us (47%)
  waiting for transfers between devices  18.3 us (22%)
  blocking collectives  16.9 us (21%)
  Pallas kernels  5.75 us (7%)
    ppermute x2, starting transfers between devices, second_swap(): lax.ppermute(x, 'tile', [(i, ((i + 1 ^ 1) - 1) % peers) for i in range(pe...  17.8 us
    all_to_all x1, blocking collectives, per_device(): lax.all_to_all(levels.reshape(pops, rows, part), POP, 0, 0, tiled=True)  16.9 us
    all_to_all x1, waiting for transfers between devices, per_device(): lax.all_to_all(chunks.reshape(pops, rows, part), POP, 0, 0, tiled=True)  12 us
    all_to_all x1, starting transfers between devices, per_device(): lax.all_to_all(chunks.reshape(pops, rows, part), POP, 0, 0, tiled=True)  10.3 us
    ppermute x2, waiting for transfers between devices, second_swap(): lax.ppermute(x, 'tile', [(i, ((i + 1 ^ 1) - 1) % peers) for i in range(pe...  6.32 us
    all_to_all x1, starting transfers between devices, per_device(): sums = lax.all_to_all(sums, 'tile', 0, 0, tiled=True)  6.07 us
    pallas_call x5, Pallas kernels, call(): pl.pallas_call(kernel, out_shape=outs, in_specs=[spec] * len(args), out_s...  5.75 us
    ppermute x2, starting transfers between devices, first_swap(): return lax.ppermute(x, 'tile', [(i, i ^ 1) for i in range(peers)])  4.41 us
  transfers between devices with their start and end apart: 6, of which 3 were waited for; matrix products, arithmetic and copies ran while one was open for 0% of the time, Pallas kernels for 0%

profile of v12, /device:TPU:8, one launch (start us, length us, event | category | flops | bytes accessed | tf_op | source)
XLA Modules:
  0.0 80.9 jit_solution(14104474095018314102)
XLA Ops:
  0.6 0.0 copy-start.3
  0.6 0.0 copy-start
  0.6 0.0 copy-start.1
  0.7 10.3 %all-to-all-start = ((bf16[32,8,512]{2,1,0:T(8,128)(2,1)}), bf16[32,8,512]{2,1,0:T(8,128)(2,1)S(1)}, u32[]{:S(2)}, u32[]{:S(2)}) async-start(bf16[32,8,512]{2,1,0:T(8,128)(2,1)} %bitcast.20), calls=%async_computation | async-start | bytes 524288 | tf_op jit(solution)/shard_map/all_to_all | solution.py:289
  11.0 0.0 copy-start.2
  11.0 0.7 copy-done.2
  11.7 0.3 shard_map.59
  12.0 12.0 %all-to-all-done = bf16[32,8,512]{2,1,0:T(8,128)(2,1)S(1)} async-done(((bf16[32,8,512]{2,1,0:T(8,128)(2,1)}), bf16[32,8,512]{2,1,0:T(8,128)(2,1)S(1)}, u32[]{:S(2)}, u32[]{:S(2)}) %all-to-all-start) | async-done | bytes 262176 | tf_op jit(solution)/shard_map/all_to_all | solution.py:289
  24.0 0.2 shard_map.60
  24.2 16.9 %all_to_all.15 = s16[32,8,512]{2,1,0:T(8,128)(2,1)S(1)} all-to-all(s16[32,8,512]{2,1,0:T(8,128)(2,1)S(1)} %bitcast.15), channel_id=1, replica_groups=mesh['pop_0'=8,'pop_1'=2,'pop_2'=2,'tile'=16] {'pop_0','pop_1','pop_2'}, dimensions={0} | all-to-all | bytes 524288 | tf_op jit(solution)/shard_map/all_to_all | solution.py:302
  41.1 0.0 copy-done
  41.1 0.1 shard_map.61
  41.2 2.5 %collective-permute-start = (s16[72,1024]{1,0:T(8,128)(2,1)S(1)}, s16[72,1024]{1,0:T(8,128)(2,1)S(1)}, u32[]{:S(2)}, u32[]{:S(2)}) collective-permute-start(s16[72,1024]{1,0:T(8,128)(2,1)S(1)} %get-tuple-element.14), channel_id=1, source_target_pairs={{0,1},{1,0},{2,3},{3,2},{4,5},{5,4},{6,7},{7,6},{8,9},{9,8},{10,11... | collective-permute-start | bytes 442376 | tf_op jit(solution)/shard_map/ppermute | solution.py:271
  43.7 11.8 %collective-permute-start.1 = (s16[72,1024]{1,0:T(8,128)(2,1)S(1)}, s16[72,1024]{1,0:T(8,128)(2,1)S(1)}, u32[]{:S(2)}, u32[]{:S(2)}) collective-permute-start(s16[72,1024]{1,0:T(8,128)(2,1)S(1)} %get-tuple-element.15), channel_id=1, source_target_pairs={{0,15},{1,2},{2,1},{3,4},{4,3},{5,6},{6,5},{7,8},{8,7},{9,10},{10,... | collective-permute-start | bytes 442376 | tf_op jit(solution)/shard_map/ppermute | solution.py:276
  55.5 0.0 collective-permute-done.first_ref
  55.6 3.1 %collective-permute-done.1.second_ref = s16[72,1024]{1,0:T(8,128)(2,1)S(1)} collective-permute-done((s16[72,1024]{1,0:T(8,128)(2,1)S(1)}, s16[72,1024]{1,0:T(8,128)(2,1)S(1)}, u32[]{:S(2)}, u32[]{:S(2)}) %collective-permute-start.1) | collective-permute-done | bytes 147488 | tf_op jit(solution)/shard_map/ppermute | solution.py:276
  58.6 0.0 copy-done.3
  58.7 0.0 copy-done.1
  58.7 2.3 %shard_map.62 = (f32[8,24,2048]{2,1,0:T(8,128)S(1)}, s16[40,2048]{1,0:T(8,128)(2,1)S(1)}, s16[32,2048]{1,0:T(8,128)(2,1)S(1)}, f32[16,1,1152]{2,1,0:T(1,128)}) custom-call(s32[32,32]{1,0:T(8,128)S(1)} %copy-done.3, s16[256,512]{1,0:T(8,128)(2,1)S(1)} %bitcast.13, f32[8,2048]{1,0:T(8,128)S(1)} %bitcast.17, f32[8,2048]{1,0:T(8,128)S(1)} %bitcast.18, ...), custom_call_target="tpu_custom_call" | custom-call | tf_op jit(solution)/shard_map/pallas_call | solution.py:260
  61.0 1.9 %collective-permute-start.3 = (s16[40,2048]{1,0:T(8,128)(2,1)S(1)}, s16[40,2048]{1,0:T(8,128)(2,1)S(1)}, u32[]{:S(2)}, u32[]{:S(2)}) collective-permute-start(s16[40,2048]{1,0:T(8,128)(2,1)S(1)} %get-tuple-element.18), channel_id=1, source_target_pairs={{0,1},{1,0},{2,3},{3,2},{4,5},{5,4},{6,7},{7,6},{8,9},{9,8},{10,11... | collective-permute-start | bytes 491528 | tf_op jit(solution)/shard_map/ppermute | solution.py:271
  62.9 6.1 %all-to-all-start.2 = ((f32[16,1,1152]{2,1,0:T(1,128)}), f32[16,1,1152]{2,1,0:T(1,128)S(1)}, u32[]{:S(2)}, u32[]{:S(2)}) async-start(f32[16,1,1152]{2,1,0:T(1,128)} %get-tuple-element.19), calls=%async_computation.2 | async-start | bytes 147456 | tf_op jit(solution)/shard_map/all_to_all | solution.py:329
  69.0 5.9 %collective-permute-start.2 = (s16[32,2048]{1,0:T(8,128)(2,1)S(1)}, s16[32,2048]{1,0:T(8,128)(2,1)S(1)}, u32[]{:S(2)}, u32[]{:S(2)}) collective-permute-start(s16[32,2048]{1,0:T(8,128)(2,1)S(1)} %get-tuple-element.17), channel_id=1, source_target_pairs={{0,15},{1,2},{2,1},{3,4},{4,3},{5,6},{6,5},{7,8},{8,7},{9,10},{10,... | collective-permute-start | bytes 393224 | tf_op jit(solution)/shard_map/ppermute | solution.py:276
  74.9 3.2 %collective-permute-done.2.second_ref = s16[32,2048]{1,0:T(8,128)(2,1)S(1)} collective-permute-done((s16[32,2048]{1,0:T(8,128)(2,1)S(1)}, s16[32,2048]{1,0:T(8,128)(2,1)S(1)}, u32[]{:S(2)}, u32[]{:S(2)}) %collective-permute-start.2) | collective-permute-done | bytes 131104 | tf_op jit(solution)/shard_map/ppermute | solution.py:276
  78.1 0.0 all-to-all-done.2.sums_ref
  78.1 0.0 collective-permute-done.3.first_ref
  78.1 2.8 %shard_map.63 = (f32[8,8,2048]{2,1,0:T(8,128)}, f32[8,2048]{1,0:T(8,128)}) custom-call(f32[8,24,2048]{2,1,0:T(8,128)S(1)} %get-tuple-element.16.u_ref, f32[8,2048]{1,0:T(8,128)S(1)} %bitcast.19, s16[32,2048]{1,0:T(8,128)(2,1)S(1)} %collective-permute-done.2.second_ref, s16[40,2048]{1,0:T(8,128)(2,1)S(1)} %collective-permute-done.3.first_ref, ...), custom_call_target="tpu_custom_call" | custom-call | tf_op jit(solution)/shard_map/pallas_call | solution.py:260
Async XLA Ops:
  0.6 58.0 %copy-start.3 = (s32[32,32]{1,0:T(8,128)S(1)}, s32[32,32]{1,0:T(8,128)}, u32[]{:S(2)}) copy-start(s32[32,32]{1,0:T(8,128)} %w_ref.3) | copy-start | bytes 12292
  0.6 40.5 %copy-start = (f32[1,8,2048]{2,1,0:T(8,128)S(1)}, f32[1,8,2048]{2,1,0:T(8,128)}, u32[]{:S(2)}) copy-start(f32[1,8,2048]{2,1,0:T(8,128)} %param.5) | copy-start | bytes 196612
  0.6 58.0 %copy-start.1 = (f32[1,8,2048]{2,1,0:T(8,128)S(1)}, f32[1,8,2048]{2,1,0:T(8,128)}, u32[]{:S(2)}) copy-start(f32[1,8,2048]{2,1,0:T(8,128)} %param.7) | copy-start | bytes 196612
  0.7 23.3 %all-to-all-start = ((bf16[32,8,512]{2,1,0:T(8,128)(2,1)}), bf16[32,8,512]{2,1,0:T(8,128)(2,1)S(1)}, u32[]{:S(2)}, u32[]{:S(2)}) async-start(bf16[32,8,512]{2,1,0:T(8,128)(2,1)} %bitcast.20), calls=%async_computation | async-start | bytes 524288 | tf_op jit(solution)/shard_map/all_to_all | solution.py:289
  11.0 0.7 copy-start.2
  41.2 14.3 %collective-permute-start = (s16[72,1024]{1,0:T(8,128)(2,1)S(1)}, s16[72,1024]{1,0:T(8,128)(2,1)S(1)}, u32[]{:S(2)}, u32[]{:S(2)}) collective-permute-start(s16[72,1024]{1,0:T(8,128)(2,1)S(1)} %get-tuple-element.14), channel_id=1, source_target_pairs={{0,1},{1,0},{2,3},{3,2},{4,5},{5,4},{6,7},{7,6},{8,9},{9,8},{10,11... | collective-permute-start | bytes 442376 | tf_op jit(solution)/shard_map/ppermute | solution.py:271
  43.7 14.9 %collective-permute-start.1 = (s16[72,1024]{1,0:T(8,128)(2,1)S(1)}, s16[72,1024]{1,0:T(8,128)(2,1)S(1)}, u32[]{:S(2)}, u32[]{:S(2)}) collective-permute-start(s16[72,1024]{1,0:T(8,128)(2,1)S(1)} %get-tuple-element.15), channel_id=1, source_target_pairs={{0,15},{1,2},{2,1},{3,4},{4,3},{5,6},{6,5},{7,8},{8,7},{9,10},{10,... | collective-permute-start | bytes 442376 | tf_op jit(solution)/shard_map/ppermute | solution.py:276
  61.0 17.2 %collective-permute-start.3 = (s16[40,2048]{1,0:T(8,128)(2,1)S(1)}, s16[40,2048]{1,0:T(8,128)(2,1)S(1)}, u32[]{:S(2)}, u32[]{:S(2)}) collective-permute-start(s16[40,2048]{1,0:T(8,128)(2,1)S(1)} %get-tuple-element.18), channel_id=1, source_target_pairs={{0,1},{1,0},{2,3},{3,2},{4,5},{5,4},{6,7},{7,6},{8,9},{9,8},{10,11... | collective-permute-start | bytes 491528 | tf_op jit(solution)/shard_map/ppermute | solution.py:271
  62.9 15.2 %all-to-all-start.2 = ((f32[16,1,1152]{2,1,0:T(1,128)}), f32[16,1,1152]{2,1,0:T(1,128)S(1)}, u32[]{:S(2)}, u32[]{:S(2)}) async-start(f32[16,1,1152]{2,1,0:T(1,128)} %get-tuple-element.19), calls=%async_computation.2 | async-start | bytes 147456 | tf_op jit(solution)/shard_map/all_to_all | solution.py:329
  69.0 9.2 %collective-permute-start.2 = (s16[32,2048]{1,0:T(8,128)(2,1)S(1)}, s16[32,2048]{1,0:T(8,128)(2,1)S(1)}, u32[]{:S(2)}, u32[]{:S(2)}) collective-permute-start(s16[32,2048]{1,0:T(8,128)(2,1)S(1)} %get-tuple-element.17), channel_id=1, source_target_pairs={{0,15},{1,2},{2,1},{3,4},{4,3},{5,6},{6,5},{7,8},{8,7},{9,10},{10,... | collective-permute-start | bytes 393224 | tf_op jit(solution)/shard_map/ppermute | solution.py:276
